TPU v7x, 128 devices: a whole 4x4x4 slice. The times are simulated.
128 devices in a mesh: px: 16 (over x, y), py: 8 (over z, core).
Axes of the slice: x: 4, y: 4, z: 4, core: 2. Of those that a mesh axis runs over, the one named last changes fastest.
Arguments:
- plastic_distortion: float32 [9, 256, 256, 256], P(None, 'px', 'py'), may hold values from -4 to 4
- grain_ids: int32 [256, 256, 256], P('px', 'py'), may hold values from 0 to 63
- grain_moduli: float32 [2, 64], replicated, may hold values from 0.5 to 2
- seg_source: int32 [65536, 1], P(('px', 'py')), may hold values from 0 to 127; in each aligned block of 512 rows (0 to 511, 512 to 1023, ...) at most 8 rows name the same one
- seg_tile: int32 [65536], P(('px', 'py')), may hold values from 0 to 1023
- seg_center: int32 [65536], P(('px', 'py')), may hold values from 0 to 127
- burgers: float32 [3, 65536], P(None, ('px', 'py')), may hold values from -4 to 4
- line_vector: float32 [3, 65536], P(None, ('px', 'py')), may hold values from -4 to 4
Outputs:
- stress_field: float32 [6, 256, 256, 256], P(None, 'px', 'py')
- seg_force: float32 [3, 65536], P(None, ('px', 'py'))
Inputs may be any that keep to these rules, and one draw needn't show every extreme that they name: `seg_source`: among the segments of one device no source device is named more than 8 times; every device is named by some segment.
All inputs are finite; a program needn't handle non-finite values.
Results may differ from a plain program's by a relative error of at most 0.0003.
Values sent between devices are 32-bit elements; how exact they have to be, the bound alone decides.
A program may use at most 128 MiB of HBM per device.

v0:
```python
import math

import jax
import jax.numpy as jnp
from jax import lax
from jax.sharding import PartitionSpec as P

TILE = 128


ref_lambda = 1.25
ref_shear = 1.25
highest = lax.Precision.HIGHEST


def extended(cells, sides, width):
    for axis, dim in sides:
        count = lax.axis_size(axis)
        head = lax.slice_in_dim(cells, 0, width, axis=dim)
        tail = lax.slice_in_dim(cells, cells.shape[dim] - width, cells.shape[dim], axis=dim)
        cells = jnp.concatenate(
            [
                lax.ppermute(tail, axis, [(i, (i + 1) % count) for i in range(count)]),
                cells,
                lax.ppermute(head, axis, [((i + 1) % count, i) for i in range(count)]),
            ],
            axis=dim,
        )
    return cells


def symmetric_part(distortion):
    return jnp.stack(
        [
            distortion[0],
            distortion[4],
            distortion[8],
            (distortion[5] + distortion[7]) * 0.5,
            (distortion[2] + distortion[6]) * 0.5,
            (distortion[1] + distortion[3]) * 0.5,
        ]
    )


def stiffness(strain, lame_mod, shear_mod):
    trace_sum = strain[0] + strain[1] + strain[2]
    diagonal = [2.0 * shear_mod * strain[index] + lame_mod * trace_sum for index in range(3)]
    shears = [2.0 * shear_mod * strain[index] for index in range(3, 6)]
    return jnp.stack(diagonal + shears)


def polarization(strain, plastic, lame_mod, shear_mod):
    return stiffness(strain - plastic, lame_mod, shear_mod) - stiffness(
        strain, ref_lambda, ref_shear
    )


def divergence(grad_x, grad_y, grad_z):
    return jnp.stack(
        [
            grad_x[0] + grad_y[5] + grad_z[4],
            grad_x[5] + grad_y[1] + grad_z[3],
            grad_x[4] + grad_y[3] + grad_z[2],
        ]
    )


def sym_gradient(grad_x, grad_y, grad_z):
    return jnp.stack(
        [
            grad_x[0],
            grad_y[1],
            grad_z[2],
            (grad_z[1] + grad_y[2]) * 0.5,
            (grad_z[0] + grad_x[2]) * 0.5,
            (grad_y[0] + grad_x[1]) * 0.5,
        ]
    )


def wave_numbers(first, length, total):
    index = first + jnp.arange(length, dtype=jnp.int32)
    angle = index.astype(jnp.float32) * (2.0 * math.pi / total)
    return (jnp.sin(angle), index % (total // 2) == 0)


def solve_waves(parts, wave_x, wave_y, wave_z, null_mode):
    squared = wave_x * wave_x + wave_y * wave_y + wave_z * wave_z
    inverse_sq = jnp.where(null_mode, 0.0, 1.0 / jnp.where(null_mode, 1.0, squared))
    coupling = (ref_lambda + ref_shear) / (ref_lambda + 2.0 * ref_shear)
    along_wave = wave_x * parts[0] + wave_y * parts[1] + wave_z * parts[2]
    common = coupling * inverse_sq * inverse_sq * along_wave
    return [
        (inverse_sq * parts[0] - common * wave_x) / ref_shear,
        (inverse_sq * parts[1] - common * wave_y) / ref_shear,
        (inverse_sq * parts[2] - common * wave_z) / ref_shear,
    ]


def core_weights(center, tile_len):
    offsets = jnp.arange(tile_len, dtype=jnp.float32)
    spread = tile_len / 8.0
    distance = offsets - center[..., None].astype(jnp.float32)
    weights = jnp.exp(-distance * distance / (2.0 * spread * spread))
    return weights / jnp.sum(weights, axis=-1, keepdims=True)


def peach_koehler(tensor, burgers, line_vector):
    push_x = tensor[0] * burgers[0] + tensor[5] * burgers[1] + tensor[4] * burgers[2]
    push_y = tensor[5] * burgers[0] + tensor[1] * burgers[1] + tensor[3] * burgers[2]
    push_z = tensor[4] * burgers[0] + tensor[3] * burgers[1] + tensor[2] * burgers[2]
    return jnp.stack(
        [
            push_y * line_vector[2] - push_z * line_vector[1],
            push_z * line_vector[0] - push_x * line_vector[2],
            push_x * line_vector[1] - push_y * line_vector[0],
        ]
    )


def dft_tables(length):
    index = jnp.arange(length, dtype=jnp.int32)
    phase = index[:, None] * index[None, :] % length
    angle = phase.astype(jnp.float32) * (2.0 * math.pi / length)
    cos_table = jnp.cos(angle)
    sin_table = jnp.sin(angle)
    forward_mix = jnp.stack([jnp.stack([cos_table, -sin_table]), jnp.stack([sin_table, cos_table])])
    inverse_mix = jnp.stack([jnp.stack([cos_table, sin_table]), jnp.stack([-sin_table, cos_table])])
    split_table = jnp.stack([cos_table, -sin_table])
    return (forward_mix, inverse_mix, split_table)


def contract(form, values, tables):
    return jnp.einsum(form, values, tables, precision=highest, preferred_element_type=jnp.float32)


def across_columns(values, step_fn):
    return step_fn(lax.all_to_all(values, "py", split_axis=4, concat_axis=3, tiled=True))


def across_rows(values, step_fn):
    return step_fn(lax.all_to_all(values, "px", split_axis=4, concat_axis=2, tiled=True))


def derivatives(values):
    padded = extended(values, (("px", 1), ("py", 2)), 1)
    grad_x = (padded[:, 2:, 1:-1] - padded[:, :-2, 1:-1]) * 0.5
    grad_y = (padded[:, 1:-1, 2:] - padded[:, 1:-1, :-2]) * 0.5
    grad_z = (jnp.roll(values, -1, 3) - jnp.roll(values, 1, 3)) * 0.5
    return (grad_x, grad_y, grad_z)


def forward(density, tables):
    forward_mix, inverse_mix, split_table = tables
    complex_pair = contract("cxyz,bzq->bcxyq", density, split_table)

    def forward_along_y(pieces):
        return contract("acxyz,abyq->bcxzq", pieces, forward_mix)

    complex_pair = across_columns(complex_pair, forward_along_y)

    def along_x(pieces):
        return contract("acxzy,abxq->bcyzq", pieces, forward_mix)

    return across_rows(complex_pair, along_x)


def inverse(spectrum, tables, grid_len):
    forward_mix, inverse_mix, split_table = tables
    factor = 1.0 / grid_len
    complex_pair = contract("acyzx,abxq->bcyzq", spectrum, inverse_mix) * factor

    def inverse_along_y(pieces):
        return contract("acyzx,abyq->bcxzq", pieces, inverse_mix) * factor

    complex_pair = across_rows(complex_pair, inverse_along_y)

    def along_z(pieces):
        return (contract("acxzy,azq->cxyq", pieces, split_table) * factor)[None]

    return across_columns(complex_pair, along_z)[0]


def shards(
    plastic_distortion,
    grain_ids,
    grain_moduli,
    seg_source,
    seg_tile,
    seg_center,
    burgers,
    line_vector,
):
    grid_len = plastic_distortion.shape[3]
    tables = dft_tables(grid_len)
    plastic = symmetric_part(plastic_distortion)
    grains = grain_moduli.shape[1]
    matched = grain_ids[..., None] == jnp.arange(grains, dtype=jnp.int32)
    lame_mod = jnp.sum(jnp.where(matched, grain_moduli[0], 0.0), axis=-1)
    shear_mod = jnp.sum(jnp.where(matched, grain_moduli[1], 0.0), axis=-1)
    strain = jnp.zeros_like(plastic)
    polar = polarization(strain, plastic, lame_mod, shear_mod)
    force_density = divergence(*derivatives(polar))
    spectrum = forward(force_density, tables)
    ky_len = spectrum.shape[2]
    kz_len = spectrum.shape[3]
    wave_yl, null_yl = wave_numbers(lax.axis_index("px") * ky_len, ky_len, grid_len)
    wave_zl, null_zl = wave_numbers(lax.axis_index("py") * kz_len, kz_len, grid_len)
    wave_xl, null_xl = wave_numbers(0, grid_len, grid_len)
    null_mode = null_yl[:, None, None] & null_zl[None, :, None] & null_xl[None, None, :]
    solved = solve_waves(
        [spectrum[:, 0], spectrum[:, 1], spectrum[:, 2]],
        wave_xl[None, None, :],
        wave_yl[:, None, None],
        wave_zl[None, :, None],
        null_mode,
    )
    displace = inverse(jnp.stack(solved, axis=1), tables, grid_len)
    strain = sym_gradient(*derivatives(displace))
    stress_field = stiffness(strain - plastic, lame_mod, shear_mod)
    devices = lax.axis_size(("px", "py"))
    seg_count = seg_tile.shape[0]
    capacity = 2 * seg_count // devices
    source = seg_source[:, 0]
    matches = (source[:, None] == jnp.arange(devices, dtype=jnp.int32)[None, :]).astype(jnp.int32)
    before = jnp.cumsum(matches, axis=0) - matches
    slot_index = jnp.sum(before * matches, axis=1)
    flat_index = source * capacity + slot_index
    tiles = stress_field.reshape(6, -1, TILE)
    wanted = (
        jnp.zeros((devices * capacity,), jnp.int32)
        .at[flat_index]
        .set(seg_tile)
        .reshape(devices, capacity)
    )
    requests = lax.all_to_all(wanted, ("px", "py"), split_axis=0, concat_axis=0, tiled=True)
    picked = jnp.take(tiles, requests.reshape(-1), axis=1).reshape(
        6, devices, requests.shape[1], TILE
    )
    received = lax.all_to_all(picked, ("px", "py"), split_axis=1, concat_axis=1, tiled=True)
    own_tiles = received[:, source, slot_index, :]
    weights = core_weights(seg_center, TILE)
    seg_stress = jnp.sum(own_tiles * weights[None], axis=-1)
    seg_force = peach_koehler(seg_stress, burgers, line_vector)
    return (stress_field, seg_force)


def solution(mesh):
    return jax.shard_map(
        shards,
        mesh=mesh,
        in_specs=(
            P(None, "px", "py", None),
            P("px", "py", None),
            P(),
            P(("px", "py"), None),
            P(("px", "py")),
            P(("px", "py")),
            P(None, ("px", "py")),
            P(None, ("px", "py")),
        ),
        out_specs=(P(None, "px", "py", None), P(None, ("px", "py"))),
        check_vma=False,
    )
```

profile of v0, /device:TPU:1, one launch (start us, length us, event | category | flops | bytes accessed | tf_op | source)
XLA Modules:
  0.0 667.9 jit_solution(10492414765101156050)
XLA Ops:
  10.2 18.3 %select_reduce_fusion.1 = (f32[16,32,256]{2,1,0:T(8,128)S(1)}, f32[16,32,256]{2,1,0:T(8,128)S(1)}) fusion(f32[64]{0:T(128)S(1)} %get-tuple-element.64, s32[16,32,256]{2,1,0:T(8,128)S(1)} %copy-done.12, f32[64]{0:T(128)S(1)} %get-tuple-element.63), kind=kLoop, calls=%fused_computation.4 | loop fusion | flops 41680896 | bytes 1573376 | tf_op jit(solution)/shard_map/reduce_sum | solution.py:200
  67.1 10.6 %reshape.435 = f32[8,1,98304]{2,1,0:T(1,128)} reshape(f32[256,2,3,16,32]{4,3,2,1,0:T(8,128)} %bitcast.209) | data formatting | bytes 6291456
  88.6 34.0 %all-to-all-done = f32[8,1,98304]{2,1,0:T(1,128)S(1)} async-done(((f32[8,1,98304]{2,1,0:T(1,128)}), f32[8,1,98304]{2,1,0:T(1,128)S(1)}, u32[]{:S(2)}, u32[]{:S(2)}) %all-to-all-start) | async-done | bytes 3145760 | tf_op jit(solution)/shard_map/all_to_all | solution.py:138
  123.1 11.1 %reduce.6 = f32[8,98304]{1,0:T(8,128)} reduce(f32[8,1,98304]{2,1,0:T(1,128)S(1)} %all-to-all-done, f32[]{:T(128)} %broadcast.609), dimensions={1}, to_apply=%all_to_all.61.reduce_sub_computation | reduce | bytes 6291460 | tf_op jit(solution)/shard_map/all_to_all | solution.py:138
  134.2 10.9 %reshape.436 = f32[256,2,3,16,32]{4,3,2,1,0:T(8,128)} reshape(f32[8,98304]{1,0:T(8,128)} %reduce.6) | data formatting | bytes 6291456
  145.1 16.4 %copy.287 = f32[2,3,16,32,8,32]{3,4,5,0,2,1:T(8,128)} copy(f32[2,3,16,32,8,32]{3,2,1,0,5,4:T(8,128)} %bitcast.201) | data formatting | bytes 6291456 | tf_op jit(solution)/shard_map/all_to_all | solution.py:138
  177.2 11.5 %copy.222 = f32[2,3,16,32,256]{3,2,1,0,4:T(8,128)} copy(f32[2,3,16,32,256]{4,3,2,1,0:T(8,128)} %convolution_bitcast_fusion) | data formatting | bytes 6291456 | tf_op jit(solution)/shard_map/acxyz,abyq->bcxzq/transpose | solution.py:134
  188.6 14.1 %reshape.437 = f32[16,1,49152]{2,1,0:T(1,128)} reshape(f32[256,2,3,16,32]{4,3,2,1,0:T(8,128)} %bitcast.210) | data formatting | bytes 6291456
  208.3 38.7 %all-to-all-done.1 = f32[16,1,49152]{2,1,0:T(1,128)S(1)} async-done(((f32[16,1,49152]{2,1,0:T(1,128)}), f32[16,1,49152]{2,1,0:T(1,128)S(1)}, u32[]{:S(2)}, u32[]{:S(2)}) %all-to-all-start.1) | async-done | bytes 3145760 | tf_op jit(solution)/shard_map/all_to_all | solution.py:142
  247.0 10.8 %reduce.7 = f32[16,49152]{1,0:T(8,128)} reduce(f32[16,1,49152]{2,1,0:T(1,128)S(1)} %all-to-all-done.1, f32[]{:T(128)} %broadcast.609), dimensions={1}, to_apply=%all_to_all.65.reduce_sub_computation | reduce | bytes 6291460 | tf_op jit(solution)/shard_map/all_to_all | solution.py:142
  257.8 12.4 %reshape.438 = f32[256,2,3,16,32]{4,3,2,1,0:T(8,128)} reshape(f32[16,49152]{1,0:T(8,128)} %reduce.7) | data formatting | bytes 6291456
  270.2 16.4 %copy.224 = f32[2,3,16,16,32,16]{4,5,3,2,1,0:T(8,128)} copy(f32[2,3,16,16,32,16]{4,3,1,0,5,2:T(8,128)} %bitcast.203) | data formatting | bytes 6291456 | tf_op jit(solution)/shard_map/all_to_all | solution.py:142
  319.0 14.1 %reshape.439 = f32[16,1,49152]{2,1,0:T(1,128)} reshape(f32[256,2,3,16,32]{4,3,2,1,0:T(8,128)} %bitcast.211) | data formatting | bytes 6291456
  348.4 31.2 %all-to-all-done.2 = f32[16,1,49152]{2,1,0:T(1,128)S(1)} async-done(((f32[16,1,49152]{2,1,0:T(1,128)}), f32[16,1,49152]{2,1,0:T(1,128)S(1)}, u32[]{:S(2)}, u32[]{:S(2)}) %all-to-all-start.2) | async-done | bytes 3145760 | tf_op jit(solution)/shard_map/all_to_all | solution.py:142
  379.6 12.5 %all-to-all-start.4 = ((s32[128,1,8]{2,1,0:T(1,128)}), s32[128,1,8]{2,1,0:T(1,128)S(1)}, u32[]{:S(2)}, u32[]{:S(2)}) async-start(s32[128,1,8]{2,1,0:T(1,128)} %bitcast.54), calls=%async_computation.4 | async-start | bytes 131072 | tf_op jit(solution)/shard_map/all_to_all | solution.py:236
  392.0 11.0 %reduce.8 = f32[16,49152]{1,0:T(8,128)} reduce(f32[16,1,49152]{2,1,0:T(1,128)S(1)} %all-to-all-done.2, f32[]{:T(128)} %broadcast.609), dimensions={1}, to_apply=%all_to_all.69.reduce_sub_computation | reduce | bytes 6291460 | tf_op jit(solution)/shard_map/all_to_all | solution.py:142
  403.0 12.6 %reshape.440 = f32[256,2,3,16,32]{4,3,2,1,0:T(8,128)} reshape(f32[16,49152]{1,0:T(8,128)} %reduce.8) | data formatting | bytes 6291456
  415.6 16.4 %copy.231 = f32[2,3,16,16,32,16]{4,5,3,2,1,0:T(8,128)} copy(f32[2,3,16,16,32,16]{4,3,1,0,5,2:T(8,128)} %bitcast.205) | data formatting | bytes 6291456 | tf_op jit(solution)/shard_map/all_to_all | solution.py:142
  447.1 11.5 %copy.234 = f32[2,3,16,32,256]{3,2,1,0,4:T(8,128)} copy(f32[2,3,16,32,256]{4,3,2,1,0:T(8,128)} %fusion.5) | data formatting | bytes 6291456 | tf_op jit(solution)/shard_map/mul | solution.py:174
  476.0 35.9 %all-to-all-done.3 = f32[8,1,98304]{2,1,0:T(1,128)S(1)} async-done(((f32[8,1,98304]{2,1,0:T(1,128)}), f32[8,1,98304]{2,1,0:T(1,128)S(1)}, u32[]{:S(2)}, u32[]{:S(2)}) %all-to-all-start.3) | async-done | bytes 3145760 | tf_op jit(solution)/shard_map/all_to_all | solution.py:138
  512.0 11.2 %reduce.9 = f32[8,98304]{1,0:T(8,128)} reduce(f32[8,1,98304]{2,1,0:T(1,128)S(1)} %all-to-all-done.3, f32[]{:T(128)} %broadcast.609), dimensions={1}, to_apply=%all_to_all.73.reduce_sub_computation | reduce | bytes 6291460 | tf_op jit(solution)/shard_map/all_to_all | solution.py:138
  523.2 10.7 %reshape.442 = f32[256,2,3,16,32]{4,3,2,1,0:T(8,128)} reshape(f32[8,98304]{1,0:T(8,128)} %reduce.9) | data formatting | bytes 6291456
  533.9 16.4 %copy.286 = f32[2,3,16,32,8,32]{3,4,5,0,2,1:T(8,128)} copy(f32[2,3,16,32,8,32]{3,2,1,0,5,4:T(8,128)} %bitcast.207) | data formatting | bytes 6291456 | tf_op jit(solution)/shard_map/all_to_all | solution.py:138
  617.2 41.5 %all-to-all-done.5 = f32[6,128,8,128]{3,2,0,1:T(8,128)S(1)} async-done(((f32[6,128,8,128]{3,2,0,1:T(8,128)}), f32[6,128,8,128]{3,2,0,1:T(8,128)S(1)}, u32[]{:S(2)}, u32[]{:S(2)}) %all-to-all-start.5) | async-done | bytes 3145760 | tf_op jit(solution)/shard_map/all_to_all | solution.py:240
  (168 shorter events, 236.0 us)
Async XLA Ops:
  8.5 1.7 copy-start.2
  30.1 9.4 %collective-permute-start = (f32[6,1,32,256]{3,2,1,0:T(8,128)S(1)}, f32[6,1,32,256]{3,2,1,0:T(8,128)S(1)}, u32[]{:S(2)}, u32[]{:S(2)}) collective-permute-start(f32[6,1,32,256]{3,2,1,0:T(8,128)S(1)} %get-tuple-element.38), channel_id=1, source_target_pairs={{8,0},{16,8},{24,16},{32,24},{40,32},{48,40},{56,48},{64,56},{72,6... | collective-permute-start | bytes 589832 | tf_op jit(solution)/shard_map/ppermute | solution.py:25
  35.9 9.2 %collective-permute-start.1 = (f32[6,1,32,256]{3,2,1,0:T(8,128)S(1)}, f32[6,1,32,256]{3,2,1,0:T(8,128)S(1)}, u32[]{:S(2)}, u32[]{:S(2)}) collective-permute-start(f32[6,1,32,256]{3,2,1,0:T(8,128)S(1)} %get-tuple-element.37), channel_id=1, source_target_pairs={{0,8},{8,16},{16,24},{24,32},{32,40},{40,48},{48,56},{56,64},{64,7... | collective-permute-start | bytes 589832 | tf_op jit(solution)/shard_map/ppermute | solution.py:23
  45.2 5.8 collective-permute-start.2
  47.1 4.0 collective-permute-start.3
  49.7 4.1 copy-start.7
  77.8 44.9 %all-to-all-start = ((f32[8,1,98304]{2,1,0:T(1,128)}), f32[8,1,98304]{2,1,0:T(1,128)S(1)}, u32[]{:S(2)}, u32[]{:S(2)}) async-start(f32[8,1,98304]{2,1,0:T(1,128)} %reshape.435), calls=%async_computation | async-start | bytes 6291456 | tf_op jit(solution)/shard_map/all_to_all | solution.py:138
  202.7 44.3 %all-to-all-start.1 = ((f32[16,1,49152]{2,1,0:T(1,128)}), f32[16,1,49152]{2,1,0:T(1,128)S(1)}, u32[]{:S(2)}, u32[]{:S(2)}) async-start(f32[16,1,49152]{2,1,0:T(1,128)} %reshape.437), calls=%async_computation.1 | async-start | bytes 6291456 | tf_op jit(solution)/shard_map/all_to_all | solution.py:142
  294.6 6.7 copy-start.4
  294.6 6.7 copy-start.8
  333.1 9.6 %copy-start.14 = (s32[512,1]{0,1:T(1,128)S(1)}, s32[512,1]{0,1:T(1,128)}, u32[]{:S(2)}) copy-start(s32[512,1]{0,1:T(1,128)} %param.11) | copy-start | bytes 6148
  333.1 46.5 %all-to-all-start.2 = ((f32[16,1,49152]{2,1,0:T(1,128)}), f32[16,1,49152]{2,1,0:T(1,128)S(1)}, u32[]{:S(2)}, u32[]{:S(2)}) async-start(f32[16,1,49152]{2,1,0:T(1,128)} %reshape.439), calls=%async_computation.2 | async-start | bytes 6291456 | tf_op jit(solution)/shard_map/all_to_all | solution.py:142
  379.6 89.6 %all-to-all-start.4 = ((s32[128,1,8]{2,1,0:T(1,128)}), s32[128,1,8]{2,1,0:T(1,128)S(1)}, u32[]{:S(2)}, u32[]{:S(2)}) async-start(s32[128,1,8]{2,1,0:T(1,128)} %bitcast.54), calls=%async_computation.4 | async-start | bytes 131072 | tf_op jit(solution)/shard_map/all_to_all | solution.py:236
  469.2 42.8 %all-to-all-start.3 = ((f32[8,1,98304]{2,1,0:T(1,128)}), f32[8,1,98304]{2,1,0:T(1,128)S(1)}, u32[]{:S(2)}, u32[]{:S(2)}) async-start(f32[8,1,98304]{2,1,0:T(1,128)} %reshape.441), calls=%async_computation.3 | async-start | bytes 6291456 | tf_op jit(solution)/shard_map/all_to_all | solution.py:138
  563.0 6.5 collective-permute-start.4
  567.8 6.8 %collective-permute-start.5 = (f32[3,1,32,256]{3,2,1,0:T(8,128)S(1)}, f32[3,1,32,256]{3,2,1,0:T(8,128)S(1)}, u32[]{:S(2)}, u32[]{:S(2)}) collective-permute-start(f32[3,1,32,256]{3,2,1,0:T(8,128)S(1)} %get-tuple-element.52), channel_id=1, source_target_pairs={{0,8},{8,16},{16,24},{24,32},{32,40},{40,48},{48,56},{56,64},{64,7... | collective-permute-start | bytes 294920 | tf_op jit(solution)/shard_map/ppermute | solution.py:23
  574.7 4.3 collective-permute-start.6
  577.0 2.0 collective-permute-start.7
  579.6 1.9 copy-start.3
  584.3 1.7 copy-start.13
  610.3 6.4 copy-start.17
  610.3 48.4 %all-to-all-start.5 = ((f32[6,128,8,128]{3,2,0,1:T(8,128)}), f32[6,128,8,128]{3,2,0,1:T(8,128)S(1)}, u32[]{:S(2)}, u32[]{:S(2)}) async-start(f32[6,128,8,128]{3,2,0,1:T(8,128)} %copy_select_fusion), calls=%async_computation.5 | async-start | bytes 6291456 | tf_op jit(solution)/shard_map/all_to_all | solution.py:240
  661.6 5.2 copy-start.15
  661.6 5.2 copy-start.16
  (8 other events, 8.6 us)
where the time goes:
time: 679 us; the launch traced here: 668 us
  local copies, waits for them, and re-layouts  283 us (42%)
  waiting for transfers between devices  196 us (29%)
  other arithmetic  92.4 us (14%)
  starting transfers between devices  62.1 us (9%)
  matrix products  33.3 us (5%)
    unnamed x51, local copies, waits for them, and re-layouts  105 us
    all_to_all x2, waiting for transfers between devices, across_columns(): lax.all_to_all(values, 'py', split_axis=4, concat_axis=3, tiled=True)  69.9 us
    all_to_all x2, waiting for transfers between devices, across_rows(): lax.all_to_all(values, 'px', split_axis=4, concat_axis=2, tiled=True)  69.8 us
    all_to_all x5, local copies, waits for them, and re-layouts, across_columns(): lax.all_to_all(values, 'py', split_axis=4, concat_axis=3, tiled=True)  49.8 us
    all_to_all x4, local copies, waits for them, and re-layouts, across_rows(): lax.all_to_all(values, 'px', split_axis=4, concat_axis=2, tiled=True)  48.3 us
    all_to_all x1, waiting for transfers between devices, shards(): lax.all_to_all(picked, ('px', 'py'), split_axis=1, concat_axis=1, tiled=T...  41.5 us
    dot_general x6, matrix products, contract(): jnp.einsum(form, values, tables, precision=highest, preferred_element_typ...  33.3 us
    all_to_all x2, other arithmetic, across_columns(): lax.all_to_all(values, 'py', split_axis=4, concat_axis=3, tiled=True)  22.3 us
  transfers between devices with their start and end apart: 14, of which 10 were waited for; matrix products, arithmetic and copies ran while one was open for 14% of the time, Pallas kernels for 0%

commit v1 on v0

v1 whole, which is shorter than its diff:
```python
import functools

import jax
import jax.numpy as jnp
import ml_dtypes
import numpy as np
from jax import lax
from jax.experimental import pallas as pl
from jax.experimental.pallas import tpu as pltpu
from jax.sharding import PartitionSpec as P

F32 = jnp.float32
BF16 = jnp.bfloat16
REF_LAMBDA = 1.25
REF_SHEAR = 1.25
GRID = 256
HALF = 128
NPX = 16
NPY = 8
NX = 16
NY = 32
VMEM_LIMIT = 56 * 1024 * 1024
VM = pl.BlockSpec(memory_space=pltpu.VMEM)


def two_parts(table):
    table = np.asarray(table, np.float32)
    high = table.astype(ml_dtypes.bfloat16)
    low = (table - high.astype(np.float32)).astype(ml_dtypes.bfloat16)
    return np.stack([high, low])


def z_tables():
    z = np.arange(GRID)
    fwd = np.zeros((GRID, GRID))
    inv = np.zeros((GRID, GRID))
    for row in range(GRID):
        p, kzlo, ri, kzhi = row // 32, (row // 8) % 4, (row // 4) % 2, row % 4
        wave = 16 * p + 4 * kzhi + kzlo
        angle = 2 * np.pi * ((wave * z) % GRID) / GRID
        if wave == 0:
            line = np.ones(GRID) if ri == 0 else 1.0 - 2.0 * (z % 2)
            fwd[row], inv[row] = line, line / GRID
        else:
            line = np.cos(angle) if ri == 0 else -np.sin(angle)
            fwd[row], inv[row] = line, 2 * line / GRID
    return fwd, inv


def half_tables():
    k = np.arange(HALF)
    fwd, inv = [], []
    for e in range(2):
        angle = 2 * np.pi * (((2 * k[:, None] + e) * k[None, :]) % GRID) / GRID
        cos, sin = np.cos(angle), np.sin(angle)
        fwd.append(np.block([[cos, sin], [-sin, cos]]))
        inv.append(np.block([[cos.T, -sin.T], [sin.T, cos.T]]) / GRID)
    return np.stack(fwd), np.stack(inv)


def sines():
    wave = np.arange(GRID)
    line = np.sin(2 * np.pi * wave / GRID)
    line[wave % HALF == 0] = 0.0
    return line


def wave_lines():
    line = sines()
    sx = np.stack([line[0::2], line[1::2]])[:, :, None] * np.ones((1, 1, 128))
    lane = np.arange(256)
    kz16 = (lane // 128) * 8 + (lane // 16) % 8
    ky16 = lane % 16
    sy = np.stack([line[2 * ((p % 8) * 16 + ky16) + p // 8] for p in range(NPX)])
    sz = np.stack([line[16 * p + kz16] for p in range(NPY)])
    return sx.astype(np.float32), sy.astype(np.float32), sz.astype(np.float32)


def tile_weights():
    v = np.arange(128, dtype=np.float64)
    weights = np.exp(-((v[None, :] - v[:, None]) ** 2) / (2.0 * 16.0**2))
    return weights / weights.sum(axis=1, keepdims=True)


def split(values):
    high = values.astype(BF16)
    low = (values - high.astype(F32)).astype(BF16)
    return high, low


def dot(a, b, dims=((1,), (0,))):
    return lax.dot_general(a, b, (dims, ((), ())), preferred_element_type=F32)


def dot3(a, b, dims=((1,), (0,))):
    (ah, al), (bh, bl) = a, b
    return dot(ah, bh, dims) + (dot(ah, bl, dims) + dot(al, bh, dims))


def swap_groups(values):
    count = len(values)
    width = 128 // count
    lane = lax.broadcasted_iota(jnp.int32, values[0].shape, values[0].ndim - 1)
    axis = values[0].ndim - 1
    values = list(values)
    step = 1
    while step < count:
        first = ((lane // (width * step)) % 2) == 0
        out = list(values)
        for i in range(count):
            if i & step == 0:
                low, high = values[i], values[i + step]
                out[i] = jnp.where(first, low, pltpu.roll(high, width * step, axis))
                out[i + step] = jnp.where(first, pltpu.roll(low, 128 - width * step, axis), high)
        values = out
        step *= 2
    return values


def call(body, out_shape, scratch=(), n_in=0):
    multi = isinstance(out_shape, (list, tuple))
    return pl.pallas_call(
        body,
        out_shape=out_shape,
        in_specs=[VM] * n_in,
        out_specs=[VM] * len(out_shape) if multi else VM,
        scratch_shapes=list(scratch),
        compiler_params=pltpu.CompilerParams(vmem_limit_bytes=VMEM_LIMIT),
    )


def sds(shape, dtype=F32):
    return jax.ShapeDtypeStruct(shape, dtype)


def moduli_of(table, ids):
    lame, shear = [], []
    for half in range(2):
        index = ids[:, half * 128 : (half + 1) * 128]
        lame.append(jnp.take_along_axis(table, index, axis=1))
        shear.append(jnp.take_along_axis(table, index + 64, axis=1))
    return jnp.concatenate(lame, axis=1), jnp.concatenate(shear, axis=1)


def table_of(moduli_ref):
    row = jnp.concatenate([moduli_ref[0:1, :], moduli_ref[1:2, :]], axis=1)
    return jnp.broadcast_to(row, (NY, 128))


def polar_body(dist, ids, moduli, polar, xlo, xhi, ylo, yhi):
    table = table_of(moduli)

    def at_x(x, carry):
        lame, shear = moduli_of(table, ids[x])
        exx, eyy, ezz = dist[0, x], dist[4, x], dist[8, x]
        trace = lame * (exx + eyy + ezz)
        twice = shear + shear
        polar[0, x] = -(twice * exx + trace)
        polar[1, x] = -(twice * eyy + trace)
        polar[2, x] = -(twice * ezz + trace)
        polar[3, x] = -(shear * (dist[5, x] + dist[7, x]))
        polar[4, x] = -(shear * (dist[2, x] + dist[6, x]))
        polar[5, x] = -(shear * (dist[1, x] + dist[3, x]))
        return carry

    lax.fori_loop(0, NX, at_x, 0)
    for slot, comp in enumerate((0, 5, 4)):
        xlo[slot] = polar[comp, 0]
        xhi[slot] = polar[comp, NX - 1]
    for slot, comp in enumerate((5, 1, 3)):
        ylo[slot] = polar[comp, :, 0, :]
        yhi[slot] = polar[comp, :, NY - 1, :]


def shift_y(values, before, after):
    row = lax.broadcasted_iota(jnp.int32, values.shape, 0)
    up = jnp.where(row == NY - 1, after, pltpu.roll(values, NY - 1, 0))
    down = jnp.where(row == 0, before, pltpu.roll(values, 1, 0))
    return up - down


def shift_z(values):
    return pltpu.roll(values, GRID - 1, 1) - pltpu.roll(values, 1, 1)


def forward_z_body(polar, xbefore, xafter, ybefore, yafter, tz, wire, force, swap):
    for c, (cx, cy, cz) in enumerate(((0, 5, 4), (5, 1, 3), (4, 3, 2))):
        for x in range(NX):
            after = xafter[c] if x == NX - 1 else polar[cx, x + 1]
            before = xbefore[c] if x == 0 else polar[cx, x - 1]
            grad_y = shift_y(polar[cy, x], ybefore[c, x : x + 1], yafter[c, x : x + 1])
            total = (after - before) + grad_y + shift_z(polar[cz, x])
            force[x * NY : (x + 1) * NY, :] = total * 0.5
        waves = dot3((tz[0], tz[1]), split(force[...]), ((1,), (1,)))
        for p in range(NPY):
            for xg in range(4):
                tiles = [
                    waves[p * 32 + kzlo * 8 : p * 32 + kzlo * 8 + 8, xg * 128 : xg * 128 + 128]
                    for kzlo in range(4)
                ]
                for x4, tile in enumerate(swap_groups(tiles)):
                    x = xg * 4 + x4
                    swap[p * 128 + x * 8 : p * 128 + x * 8 + 8, :] = tile
            for s in range(8):
                wire[p, c, s] = swap[pl.ds(p * 128 + s, NX, stride=8), :]


def forward_y_body(got, ty, wire, rows_h, rows_l):
    for c in range(3):
        for ri in range(2):
            for kzhi in range(4):
                s = ri * 4 + kzhi
                low = swap_groups([got[q, c, s] for q in range(4)])
                high = swap_groups([got[q + 4, c, s] for q in range(4)])
                for kzlo in range(4):
                    row = (kzhi * 4 + kzlo) * NX
                    for e in range(2):
                        mixed = low[kzlo] + high[kzlo] if e == 0 else low[kzlo] - high[kzlo]
                        hi, lo = split(mixed)
                        rows_h[e, row : row + NX, ri * 128 : ri * 128 + 128] = hi
                        rows_l[e, row : row + NX, ri * 128 : ri * 128 + 128] = lo
        for e in range(2):
            out = dot3((rows_h[e], rows_l[e]), (ty[0, e], ty[1, e]))
            for ri in range(2):
                for kzg in range(2):
                    tiles = [
                        out[(kzg * 8 + k) * NX : (kzg * 8 + k + 1) * NX, ri * 128 : ri * 128 + 128]
                        for k in range(8)
                    ]
                    lane = c * 256 + kzg * 128
                    for p8, tile in enumerate(swap_groups(tiles)):
                        wire[e * 8 + p8, ri, :, lane : lane + 128] = tile


def solve_x_body(got, tx, txi, sx, sy_all, sz_all, wire, rows_h, rows_l):
    sy = sy_all[pl.ds(lax.axis_index("px"), 1), :]
    sz = sz_all[pl.ds(lax.axis_index("py"), 1), :]
    for ri in range(2):
        for q in range(8):
            a, b = got[q, ri], got[q + 8, ri]
            row = ri * 128 + q * 16
            for e in range(2):
                hi, lo = split(a + b if e == 0 else a - b)
                rows_h[e, row : row + 16, :] = hi
                rows_l[e, row : row + 16, :] = lo
    coupling = (REF_LAMBDA + REF_SHEAR) / (REF_LAMBDA + 2.0 * REF_SHEAR)
    backs = []
    for e in range(2):
        waves = dot3((tx[0, e], tx[1, e]), (rows_h[e], rows_l[e]))
        wx = jnp.concatenate([sx[e], sx[e]], axis=1)
        squared = wx * wx + (sy * sy + sz * sz)
        null = squared == 0.0
        inverse = jnp.where(null, 0.0, 1.0 / jnp.where(null, 1.0, squared))
        scale = inverse * (1.0 / REF_SHEAR)
        for ri in range(2):
            parts = [waves[ri * 128 : ri * 128 + 128, c * 256 : c * 256 + 256] for c in range(3)]
            along = wx * parts[0] + sy * parts[1] + sz * parts[2]
            common = coupling * inverse * along
            for c, line in enumerate((wx, sy, sz)):
                hi, lo = split(scale * (parts[c] - common * line))
                rows_h[e, ri * 128 : ri * 128 + 128, c * 256 : c * 256 + 256] = hi
                rows_l[e, ri * 128 : ri * 128 + 128, c * 256 : c * 256 + 256] = lo
        backs.append(dot3((txi[0, e], txi[1, e]), (rows_h[e], rows_l[e])))
    first, second = backs[0] + backs[1], backs[0] - backs[1]
    for ri in range(2):
        for q in range(8):
            row = ri * 128 + q * 16
            wire[q, ri] = first[row : row + 16, :]
            wire[q + 8, ri] = second[row : row + 16, :]


def inverse_y_body(got, tyi, wire, rows_h, rows_l):
    for c in range(3):
        for e in range(2):
            for ri in range(2):
                for kzg in range(2):
                    lane = c * 256 + kzg * 128
                    tiles = swap_groups([got[e * 8 + p8, ri, :, lane : lane + 128] for p8 in range(8)])
                    for k, tile in enumerate(tiles):
                        row = (kzg * 8 + k) * NX
                        hi, lo = split(tile)
                        rows_h[e, row : row + NX, ri * 128 : ri * 128 + 128] = hi
                        rows_l[e, row : row + NX, ri * 128 : ri * 128 + 128] = lo
        even = dot3((rows_h[0], rows_l[0]), (tyi[0, 0], tyi[1, 0]))
        odd = dot3((rows_h[1], rows_l[1]), (tyi[0, 1], tyi[1, 1]))
        for half, out in enumerate((even + odd, even - odd)):
            for ri in range(2):
                for kzhi in range(4):
                    tiles = [
                        out[(kzhi * 4 + k) * NX : (kzhi * 4 + k + 1) * NX, ri * 128 : ri * 128 + 128]
                        for k in range(4)
                    ]
                    for q4, tile in enumerate(swap_groups(tiles)):
                        wire[half * 4 + q4, c, ri * 4 + kzhi] = tile


def inverse_z_body(got, tzi, disp, xlo, xhi, ylo, yhi, waves, swap):
    for c in range(3):
        for p in range(NPY):
            for s in range(8):
                swap[p * 128 + s * 16 : p * 128 + s * 16 + 16, :] = got[p, c, s]
            for xg in range(4):
                tiles = [swap[pl.ds(p * 128 + xg * 4 + x4, 8, stride=16), :] for x4 in range(4)]
                for kzlo, tile in enumerate(swap_groups(tiles)):
                    row = p * 32 + kzlo * 8
                    waves[row : row + 8, xg * 128 : xg * 128 + 128] = tile
        turned = jnp.transpose(waves[...])
        out = dot3(split(turned), (tzi[0], tzi[1]))
        for x in range(NX):
            disp[c, x] = out[x * NY : (x + 1) * NY, :]
        xlo[c] = disp[c, 0]
        xhi[c] = disp[c, NX - 1]
        ylo[c] = disp[c, :, 0, :]
        yhi[c] = disp[c, :, NY - 1, :]


def stress_body(
    disp, xbefore, xafter, ybefore, yafter, polar, ids, moduli, asked, weights, stress, reply, rows_h, rows_l
):
    table = table_of(moduli)
    for x in range(NX):
        lame, shear = moduli_of(table, ids[x])
        gx, gy, gz = [], [], []
        for c in range(3):
            after = xafter[c] if x == NX - 1 else disp[c, x + 1]
            before = xbefore[c] if x == 0 else disp[c, x - 1]
            gx.append(after - before)
            gy.append(shift_y(disp[c, x], ybefore[c, x : x + 1], yafter[c, x : x + 1]))
            gz.append(shift_z(disp[c, x]))
        trace = (0.5 * lame) * (gx[0] + gy[1] + gz[2])
        half = 0.5 * shear
        parts = (
            shear * gx[0] + trace,
            shear * gy[1] + trace,
            shear * gz[2] + trace,
            half * (gz[1] + gy[2]),
            half * (gz[0] + gx[2]),
            half * (gy[0] + gx[1]),
        )
        for c, part in enumerate(parts):
            total = part + polar[c, x]
            stress[c, x] = total
            hi, lo = split(total)
            rows_h[x * NY : (x + 1) * NY, c * 256 : c * 256 + 256] = hi
            rows_l[x * NY : (x + 1) * NY, c * 256 : c * 256 + 256] = lo
    column = lax.broadcasted_iota(jnp.int32, (128, 512), 1)
    lane = lax.broadcasted_iota(jnp.int32, (128, 128), 1)
    lane256 = lax.broadcasted_iota(jnp.int32, (128, 256), 1)
    out = jnp.zeros((128, 128), F32)
    wh, wl = weights[0], weights[1]
    for k in range(8):
        tile = asked[:, k : k + 1]
        centre = asked[:, 8 + k : 9 + k]
        pick = (column == tile // 2).astype(F32).astype(BF16)
        picked = dot(pick, rows_h[...]) + dot(pick, rows_l[...])
        at = (lane == centre).astype(F32).astype(BF16)
        row = dot(at, wh) + dot(at, wl)
        weight = jnp.where(lane256 // 128 == tile % 2, jnp.concatenate([row, row], axis=1), 0.0)
        for c in range(6):
            value = jnp.sum(picked[:, c * 256 : c * 256 + 256] * weight, axis=1, keepdims=True)
            out = jnp.where(lane == c * 8 + k, value, out)
    reply[...] = out


def request_body(source, tile, centre, asked, slot_out):
    src = jnp.broadcast_to(source[...], (512, 128)).astype(F32)
    src_lane = jnp.transpose(src)[0:1, :]
    same = src[:, 0:1] == src_lane
    first = lax.broadcasted_iota(jnp.int32, (512, 512), 0)
    second = lax.broadcasted_iota(jnp.int32, (512, 512), 1)
    slot_lane = jnp.sum(jnp.where(same & (first < second), 1.0, 0.0), axis=0, keepdims=True)
    slot_out[...] = jnp.sum(jnp.where(same & (second < first), 1.0, 0.0), axis=1, keepdims=True)
    match = (src == lax.broadcasted_iota(jnp.int32, (512, 128), 1).astype(F32)).astype(F32).astype(BF16)
    row = lax.broadcasted_iota(jnp.int32, (8, 512), 0).astype(F32)
    here = row == slot_lane
    tile_v = tile[...]
    values = [tile_v // 8, tile_v % 8, centre[...]]
    rows = [jnp.where(here, v.astype(F32), 0.0) for v in values]
    stacked = jnp.concatenate(rows + [jnp.zeros((8, 512), F32)], axis=0).astype(BF16)
    got = dot(stacked, match)
    both = jnp.concatenate([got[0:8] * 8.0 + got[8:16], got[16:24], jnp.zeros((112, 128), F32)], axis=0)
    asked[...] = jnp.transpose(both).astype(jnp.int32)


def force_body(reply, source, slot, burgers, line, out):
    src = jnp.broadcast_to(source[...], (512, 128))
    match = (src == lax.broadcasted_iota(jnp.int32, (512, 128), 1)).astype(F32).astype(BF16)
    value = reply[...]
    hi, lo = split(value)
    low = (value - hi.astype(F32) - lo.astype(F32)).astype(BF16)
    got = dot(match, hi) + (dot(match, lo) + dot(match, low))
    lane = lax.broadcasted_iota(jnp.int32, (512, 128), 1)
    slot_v = slot[...].astype(jnp.int32)
    mine = jnp.transpose(jnp.where(lane % 8 == slot_v, got, 0.0))
    t = [jnp.sum(mine[c * 8 : c * 8 + 8, :], axis=0, keepdims=True) for c in range(6)]
    b = [burgers[i : i + 1, :] for i in range(3)]
    v = [line[i : i + 1, :] for i in range(3)]
    push_x = t[0] * b[0] + t[5] * b[1] + t[4] * b[2]
    push_y = t[5] * b[0] + t[1] * b[1] + t[3] * b[2]
    push_z = t[4] * b[0] + t[3] * b[1] + t[2] * b[2]
    out[0:1, :] = push_y * v[2] - push_z * v[1]
    out[1:2, :] = push_z * v[0] - push_x * v[2]
    out[2:3, :] = push_x * v[1] - push_y * v[0]


def neighbours(low, high, axis, count):
    ahead = [(i, (i + 1) % count) for i in range(count)]
    back = [((i + 1) % count, i) for i in range(count)]
    return lax.ppermute(high, axis, ahead), lax.ppermute(low, axis, back)


def exchange(values, axis):
    return lax.all_to_all(values, axis, split_axis=0, concat_axis=0, tiled=True)


FACE_X = sds((3, NY, GRID))
FACE_Y = sds((3, NX, GRID))
FIELD_WIRE = (NPY, 3, 8, NX, 128)
WAVE_WIRE = (NPX, 2, NX, 768)


def shards(dist, ids, moduli, seg_source, seg_tile, seg_center, burgers, line_vector):
    fwd_z, inv_z = z_tables()
    fwd_h, inv_h = half_tables()
    tz, tzi = two_parts(fwd_z), two_parts(inv_z)
    tx, txi = two_parts(fwd_h), two_parts(inv_h)
    ty = two_parts(fwd_h.transpose(0, 2, 1))
    tyi = two_parts(inv_h.transpose(0, 2, 1))
    sx, sy, sz = wave_lines()
    weights = two_parts(tile_weights())

    asked, slot = call(request_body, (sds((128, 128), jnp.int32), sds((512, 1))), n_in=3)(
        seg_source, seg_tile.reshape(1, 512), seg_center.reshape(1, 512)
    )
    asked = exchange(asked, ("px", "py"))

    polar, xlo, xhi, ylo, yhi = call(
        polar_body, (sds((6, NX, NY, GRID)), FACE_X, FACE_X, FACE_Y, FACE_Y), n_in=3
    )(dist, ids, moduli)
    xbefore, xafter = neighbours(xlo, xhi, "px", NPX)
    ybefore, yafter = neighbours(ylo, yhi, "py", NPY)
    wire = call(
        forward_z_body,
        sds(FIELD_WIRE),
        [pltpu.VMEM((512, GRID), F32), pltpu.VMEM((1024, 128), F32)],
        n_in=6,
    )(polar, xbefore, xafter, ybefore, yafter, tz)
    got = exchange(wire.reshape(NPY, 384, 128), "py").reshape(FIELD_WIRE)
    pair = [pltpu.VMEM((2, 256, 256), BF16)] * 2
    wire = call(forward_y_body, sds(WAVE_WIRE), pair, n_in=2)(got, ty)
    got = exchange(wire.reshape(NPX, 32, 768), "px").reshape(WAVE_WIRE)
    wire = call(solve_x_body, sds(WAVE_WIRE), [pltpu.VMEM((2, 256, 768), BF16)] * 2, n_in=6)(
        got, tx, txi, sx, sy, sz
    )
    got = exchange(wire.reshape(NPX, 32, 768), "px").reshape(WAVE_WIRE)
    wire = call(inverse_y_body, sds(FIELD_WIRE), pair, n_in=2)(got, tyi)
    got = exchange(wire.reshape(NPY, 384, 128), "py").reshape(FIELD_WIRE)
    disp, xlo, xhi, ylo, yhi = call(
        inverse_z_body,
        (sds((3, NX, NY, GRID)), FACE_X, FACE_X, FACE_Y, FACE_Y),
        [pltpu.VMEM((256, 512), F32), pltpu.VMEM((1024, 128), F32)],
        n_in=2,
    )(got, tzi)
    xbefore, xafter = neighbours(xlo, xhi, "px", NPX)
    ybefore, yafter = neighbours(ylo, yhi, "py", NPY)
    stress, reply = call(
        stress_body,
        (sds((6, NX, NY, GRID)), sds((128, 128))),
        [pltpu.VMEM((512, 1536), BF16)] * 2,
        n_in=10,
    )(disp, xbefore, xafter, ybefore, yafter, polar, ids, moduli, asked, weights)
    reply = exchange(reply, ("px", "py"))
    seg_force = call(force_body, sds((3, 512)), n_in=5)(reply, seg_source, slot, burgers, line_vector)
    return stress, seg_force


def solution(mesh):
    return jax.shard_map(
        shards,
        mesh=mesh,
        in_specs=(
            P(None, "px", "py", None),
            P("px", "py", None),
            P(),
            P(("px", "py"), None),
            P(("px", "py")),
            P(("px", "py")),
            P(None, ("px", "py")),
            P(None, ("px", "py")),
        ),
        out_specs=(P(None, "px", "py", None), P(None, ("px", "py"))),
        check_vma=False,
    )
```

time: 679 us -> 217 us (0.32); the launches traced: 668 us -> 216 us
  local copies, waits for them, and re-layouts: 283 us -> 2.25 us
  waiting for transfers between devices: 196 us -> 11.3 us
  blocking collectives: 0 us -> 120 us
  other arithmetic: 92.4 us -> 0 us
  Pallas kernels: 0 us -> 62 us
  starting transfers between devices: 62.1 us -> 20.1 us
  matrix products: 33.3 us -> 0 us
    all_to_all x6 -> x1, waiting for transfers between devices: 181 us -> 7.59 us  [exchange(): return lax.all_to_all(values, axis, split_axis=0, concat_axis=0, tiled=True)]
    all_to_all x0 -> x5, blocking collectives: none -> 120 us  [exchange(): return lax.all_to_all(values, axis, split_axis=0, concat_axis=0, tiled=True)]
    unnamed x51 -> x21, local copies, waits for them, and re-layouts: 105 us -> 2.25 us
    all_to_all x12 -> x0, local copies, waits for them, and re-layouts: 102 us -> none  [the longest x5 49.8 us: across_columns(): lax.all_to_all(values, 'py', split_axis=4, concat_axis=3, tiled=True)]
    pallas_call x0 -> x9, Pallas kernels: none -> 62 us  [the longest x1 10.3 us: shards(): wire = call(forward_y_body, sds(WAVE_WIRE), pair, n_in=2)(got, ty)]
    all_to_all x5 -> x0, other arithmetic: 44.9 us -> none  [the longest x2 22.3 us: across_columns(): lax.all_to_all(values, 'py', split_axis=4, concat_axis=3, tiled=True)]
    all_to_all x6 -> x1, starting transfers between devices: 45.2 us -> 5 us  [exchange(): return lax.all_to_all(values, axis, split_axis=0, concat_axis=0, tiled=True)]
    dot_general x6 -> x0, matrix products: 33.3 us -> none  [contract(): jnp.einsum(form, values, tables, precision=highest, preferred_element_typ...]
  transfers between devices with their start and end apart: 14 -> 9, of which waited for: 10 -> 3; matrix products, arithmetic and copies ran while one was open for 14% -> 0% of each run, Pallas kernels for 0% -> 1%
where the time goes in v1:
time: 217 us; the launch traced here: 216 us
  blocking collectives  120 us (55%)
  Pallas kernels  62 us (29%)
  starting transfers between devices  20.1 us (9%)
  waiting for transfers between devices  11.3 us (5%)
  local copies, waits for them, and re-layouts  2.25 us (1%)
    all_to_all x5, blocking collectives, exchange(): return lax.all_to_all(values, axis, split_axis=0, concat_axis=0, tiled=True)  120 us
    ppermute x8, starting transfers between devices, neighbours(): return (lax.ppermute(high, axis, ahead), lax.ppermute(low, axis, back))  15.1 us
    pallas_call x1, Pallas kernels, shards(): wire = call(forward_y_body, sds(WAVE_WIRE), pair, n_in=2)(got, ty)  10.3 us
    pallas_call x1, Pallas kernels, shards(): wire = call(inverse_y_body, sds(FIELD_WIRE), pair, n_in=2)(got, tyi)  9.81 us
    pallas_call x1, Pallas kernels, shards(): call(forward_z_body, sds(FIELD_WIRE), [pltpu.VMEM((512, GRID), F32), pltp...  9.77 us
    pallas_call x1, Pallas kernels, shards(): call(stress_body, (sds((6, NX, NY, GRID)), sds((128, 128))), [pltpu.VMEM(...  8.99 us
    pallas_call x1, Pallas kernels, shards(): call(inverse_z_body, (sds((3, NX, NY, GRID)), FACE_X, FACE_X, FACE_Y, FAC...  7.71 us
    all_to_all x1, waiting for transfers between devices, exchange(): return lax.all_to_all(values, axis, split_axis=0, concat_axis=0, tiled=True)  7.59 us
  transfers between devices with their start and end apart: 9, of which 3 were waited for; matrix products, arithmetic and copies ran while one was open for 0% of the time, Pallas kernels for 1%

profile of v1, /device:TPU:1, one launch (start us, length us, event | category | flops | bytes accessed | tf_op | source)
XLA Modules:
  0.0 216.3 jit_solution(17950321868230110558)
XLA Ops:
  0.6 6.2 %shard_map.185 = (f32[6,16,32,256]{3,2,1,0:T(8,128)}, f32[3,32,256]{2,1,0:T(8,128)}, f32[3,32,256]{2,1,0:T(8,128)}, f32[3,16,256]{2,1,0:T(8,128)}, f32[3,16,256]{2,1,0:T(8,128)}) custom-call(f32[9,16,32,256]{3,2,1,0:T(8,128)} %dist.1, s32[16,32,256]{2,1,0:T(8,128)} %ids.3, f32[2,64]{1,0:T(2,128)} %moduli.3), custom_call_target="tpu_custom_call" | custom-call | tf_op jit(solution)/shard_map/pallas_call | solution.py:437
  6.8 2.1 collective-permute-start
  8.9 3.6 %collective-permute-start.1 = (f32[3,32,256]{2,1,0:T(8,128)}, f32[3,32,256]{2,1,0:T(8,128)S(1)}, u32[]{:S(2)}, u32[]{:S(2)}) collective-permute-start(f32[3,32,256]{2,1,0:T(8,128)} %get-tuple-element.18), channel_id=1, source_target_pairs={{8,0},{16,8},{24,16},{32,24},{40,32},{48,40},{56,48},{64,56},{72,6... | collective-permute-start | bytes 294920 | tf_op jit(solution)/shard_map/ppermute | solution.py:409
  12.5 2.6 %collective-permute-start.2 = (f32[3,16,256]{2,1,0:T(8,128)}, f32[3,16,256]{2,1,0:T(8,128)S(1)}, u32[]{:S(2)}, u32[]{:S(2)}) collective-permute-start(f32[3,16,256]{2,1,0:T(8,128)} %get-tuple-element.19), channel_id=1, source_target_pairs={{0,1},{1,2},{2,3},{3,4},{4,5},{5,6},{6,7},{7,0},{8,9},{9,10},{10,1... | collective-permute-start | bytes 147464 | tf_op jit(solution)/shard_map/ppermute | solution.py:409
  15.2 1.5 collective-permute-done.2.ybefore
  16.7 2.2 %collective-permute-done.3.yafter = f32[3,16,256]{2,1,0:T(8,128)S(1)} collective-permute-done((f32[3,16,256]{2,1,0:T(8,128)}, f32[3,16,256]{2,1,0:T(8,128)S(1)}, u32[]{:S(2)}, u32[]{:S(2)}) %collective-permute-start.3) | collective-permute-done | bytes 49184 | tf_op jit(solution)/shard_map/ppermute | solution.py:409
  19.6 9.8 %shard_map.186 = f32[8,3,8,16,128]{4,3,2,1,0:T(8,128)} custom-call(f32[6,16,32,256]{3,2,1,0:T(8,128)} %get-tuple-element.16.polar, f32[3,32,256]{2,1,0:T(8,128)} %copy-done.3, f32[3,32,256]{2,1,0:T(8,128)} %copy-done.4, f32[3,16,256]{2,1,0:T(8,128)} %copy-done.7, f32[3,16,256]{2,1,0:T(8,128)} %copy-done.8, bf16[2,256,256]{2,1,0:T(8,128)(2,1)} %constant.20.clone.tz), custom_call_target="tpu_custom_call" | custom-call | tf_op jit(solution)/shard_map/pallas_call | solution.py:442
  29.4 25.8 %all_to_all.42 = f32[8,384,128]{2,1,0:T(8,128)} all-to-all(f32[8,384,128]{2,1,0:T(8,128)} %bitcast.25), channel_id=1, replica_groups=mesh['px'=16,'py'=8] {'py'}, dimensions={0} | all-to-all | bytes 3145728 | tf_op jit(solution)/shard_map/all_to_all | solution.py:413
  55.2 10.3 %shard_map.187 = f32[16,2,16,768]{3,2,1,0:T(8,128)} custom-call(f32[8,3,8,16,128]{4,3,2,1,0:T(8,128)} %bitcast.21, bf16[2,2,256,256]{3,2,1,0:T(8,128)(2,1)} %constant.21.clone.ty), custom_call_target="tpu_custom_call" | custom-call | tf_op jit(solution)/shard_map/pallas_call | solution.py:450
  65.5 25.4 %all_to_all.43 = f32[16,32,768]{2,1,0:T(8,128)} all-to-all(f32[16,32,768]{2,1,0:T(8,128)} %bitcast.22), channel_id=1, replica_groups=mesh['px'=16,'py'=8] {'px'}, dimensions={0} | all-to-all | bytes 3145728 | tf_op jit(solution)/shard_map/all_to_all | solution.py:413
  91.0 5.1 %shard_map.188 = f32[16,2,16,768]{3,2,1,0:T(8,128)} custom-call(f32[16,2,16,768]{3,2,1,0:T(8,128)} %bitcast.19, bf16[2,2,256,256]{3,2,1,0:T(8,128)(2,1)} %constant.22.clone.tx, bf16[2,2,256,256]{3,2,1,0:T(8,128)(2,1)} %constant.23.clone.txi, f32[2,128,128]{2,1,0:T(8,128)} %constant.24.clone.sx, f32[16,256]{1,0:T(8,128)} %constant.25.clone.sy_all, ...), custom_call_target="tpu_custom_call" | custom-call | tf_op jit(solution)/shard_map/pallas_call | solution.py:452
  96.1 23.9 %all_to_all.44 = f32[16,32,768]{2,1,0:T(8,128)} all-to-all(f32[16,32,768]{2,1,0:T(8,128)} %bitcast.20), channel_id=1, replica_groups=mesh['px'=16,'py'=8] {'px'}, dimensions={0} | all-to-all | bytes 3145728 | tf_op jit(solution)/shard_map/all_to_all | solution.py:413
  120.0 9.8 %shard_map.189 = f32[8,3,8,16,128]{4,3,2,1,0:T(8,128)} custom-call(f32[16,2,16,768]{3,2,1,0:T(8,128)} %bitcast.23, bf16[2,2,256,256]{3,2,1,0:T(8,128)(2,1)} %constant.27.clone.tyi), custom_call_target="tpu_custom_call" | custom-call | tf_op jit(solution)/shard_map/pallas_call | solution.py:456
  129.9 29.2 %all_to_all.45 = f32[8,384,128]{2,1,0:T(8,128)} all-to-all(f32[8,384,128]{2,1,0:T(8,128)} %bitcast.24), channel_id=1, replica_groups=mesh['px'=16,'py'=8] {'py'}, dimensions={0} | all-to-all | bytes 3145728 | tf_op jit(solution)/shard_map/all_to_all | solution.py:413
  159.0 7.7 %shard_map.190 = (f32[3,16,32,256]{3,2,1,0:T(8,128)}, f32[3,32,256]{2,1,0:T(8,128)}, f32[3,32,256]{2,1,0:T(8,128)}, f32[3,16,256]{2,1,0:T(8,128)}, f32[3,16,256]{2,1,0:T(8,128)}) custom-call(f32[8,3,8,16,128]{4,3,2,1,0:T(8,128)} %bitcast.18, bf16[2,256,256]{2,1,0:T(8,128)(2,1)} %constant.28.clone.tzi), custom_call_target="tpu_custom_call" | custom-call | tf_op jit(solution)/shard_map/pallas_call | solution.py:458
  167.0 4.5 %collective-permute-start.5 = (f32[3,32,256]{2,1,0:T(8,128)}, f32[3,32,256]{2,1,0:T(8,128)S(1)}, u32[]{:S(2)}, u32[]{:S(2)}) collective-permute-start(f32[3,32,256]{2,1,0:T(8,128)} %get-tuple-element.23), channel_id=1, source_target_pairs={{8,0},{16,8},{24,16},{32,24},{40,32},{48,40},{56,48},{64,56},{72,6... | collective-permute-start | bytes 294920 | tf_op jit(solution)/shard_map/ppermute | solution.py:409
  171.5 0.9 copy.22.source
  172.4 2.1 shard_map.191
  174.5 5.0 %all-to-all-start.4 = ((s32[128,1,128]{2,1,0:T(1,128)}), s32[128,1,128]{2,1,0:T(1,128)S(1)}, u32[]{:S(2)}, u32[]{:S(2)}) async-start(s32[128,1,128]{2,1,0:T(1,128)} %bitcast.28), calls=%async_computation.4 | async-start | bytes 131072 | tf_op jit(solution)/shard_map/all_to_all | solution.py:413
  179.5 1.9 collective-permute-start.6
  181.4 7.6 %all-to-all-done.4 = s32[128,1,128]{2,1,0:T(1,128)S(1)} async-done(((s32[128,1,128]{2,1,0:T(1,128)}), s32[128,1,128]{2,1,0:T(1,128)S(1)}, u32[]{:S(2)}, u32[]{:S(2)}) %all-to-all-start.4) | async-done | bytes 65568 | tf_op jit(solution)/shard_map/all_to_all | solution.py:413
  189.7 9.0 %shard_map.192 = (f32[6,16,32,256]{3,2,1,0:T(8,128)}, f32[128,128]{1,0:T(8,128)}) custom-call(f32[3,16,32,256]{3,2,1,0:T(8,128)} %get-tuple-element.21.disp, f32[3,32,256]{2,1,0:T(8,128)} %copy-done.1, f32[3,32,256]{2,1,0:T(8,128)} %copy-done.2, f32[3,16,256]{2,1,0:T(8,128)} %copy-done.5, f32[3,16,256]{2,1,0:T(8,128)} %copy-done.6, ...), custom_call_target="tpu_custom_call" | custom-call | tf_op jit(solution)/shard_map/pallas_call | solution.py:466
  198.7 15.4 %all_to_all.46 = f32[128,1,128]{2,1,0:T(1,128)} all-to-all(f32[128,1,128]{2,1,0:T(1,128)} %bitcast.29), channel_id=1, replica_groups=mesh['px'=16,'py'=8] {'px','py'}, dimensions={0} | all-to-all | bytes 131072 | tf_op jit(solution)/shard_map/all_to_all | solution.py:413
  214.2 2.1 shard_map.193
  (29 shorter events, 1.7 us)
Async XLA Ops:
  6.8 12.1 %collective-permute-start = (f32[3,32,256]{2,1,0:T(8,128)}, f32[3,32,256]{2,1,0:T(8,128)S(1)}, u32[]{:S(2)}, u32[]{:S(2)}) collective-permute-start(f32[3,32,256]{2,1,0:T(8,128)} %get-tuple-element.17), channel_id=1, source_target_pairs={{0,8},{8,16},{16,24},{24,32},{32,40},{40,48},{48,56},{56,64},{64,7... | collective-permute-start | bytes 294920 | tf_op jit(solution)/shard_map/ppermute | solution.py:409
  8.9 10.0 %collective-permute-start.1 = (f32[3,32,256]{2,1,0:T(8,128)}, f32[3,32,256]{2,1,0:T(8,128)S(1)}, u32[]{:S(2)}, u32[]{:S(2)}) collective-permute-start(f32[3,32,256]{2,1,0:T(8,128)} %get-tuple-element.18), channel_id=1, source_target_pairs={{8,0},{16,8},{24,16},{32,24},{40,32},{48,40},{56,48},{64,56},{72,6... | collective-permute-start | bytes 294920 | tf_op jit(solution)/shard_map/ppermute | solution.py:409
  12.5 4.1 %collective-permute-start.2 = (f32[3,16,256]{2,1,0:T(8,128)}, f32[3,16,256]{2,1,0:T(8,128)S(1)}, u32[]{:S(2)}, u32[]{:S(2)}) collective-permute-start(f32[3,16,256]{2,1,0:T(8,128)} %get-tuple-element.19), channel_id=1, source_target_pairs={{0,1},{1,2},{2,3},{3,4},{4,5},{5,6},{6,7},{7,0},{8,9},{9,10},{10,1... | collective-permute-start | bytes 147464 | tf_op jit(solution)/shard_map/ppermute | solution.py:409
  15.2 3.7 %collective-permute-start.3 = (f32[3,16,256]{2,1,0:T(8,128)}, f32[3,16,256]{2,1,0:T(8,128)S(1)}, u32[]{:S(2)}, u32[]{:S(2)}) collective-permute-start(f32[3,16,256]{2,1,0:T(8,128)} %get-tuple-element.20), channel_id=1, source_target_pairs={{1,0},{2,1},{3,2},{4,3},{5,4},{6,5},{7,6},{0,7},{9,8},{10,9},{11,1... | collective-permute-start | bytes 147464 | tf_op jit(solution)/shard_map/ppermute | solution.py:409
  16.7 2.3 %copy-start.7 = (f32[3,16,256]{2,1,0:T(8,128)}, f32[3,16,256]{2,1,0:T(8,128)S(1)}, u32[]{:S(2)}) copy-start(f32[3,16,256]{2,1,0:T(8,128)S(1)} %collective-permute-done.2.ybefore) | copy-start | bytes 147460
  18.9 0.6 copy-start.8
  18.9 0.6 copy-start.3
  18.9 0.7 copy-start.4
  159.0 12.5 %copy-start.9 = (s32[512,1]{0,1:T(1,128)S(1)}, s32[512,1]{0,1:T(1,128)}, u32[]{:S(2)}) copy-start(s32[512,1]{0,1:T(1,128)} %param.21) | copy-start | bytes 6148
  166.7 22.3 %collective-permute-start.4 = (f32[3,32,256]{2,1,0:T(8,128)}, f32[3,32,256]{2,1,0:T(8,128)S(1)}, u32[]{:S(2)}, u32[]{:S(2)}) collective-permute-start(f32[3,32,256]{2,1,0:T(8,128)} %get-tuple-element.22), channel_id=1, source_target_pairs={{0,8},{8,16},{16,24},{24,32},{32,40},{40,48},{48,56},{56,64},{64,7... | collective-permute-start | bytes 294920 | tf_op jit(solution)/shard_map/ppermute | solution.py:409
  167.0 22.0 %collective-permute-start.5 = (f32[3,32,256]{2,1,0:T(8,128)}, f32[3,32,256]{2,1,0:T(8,128)S(1)}, u32[]{:S(2)}, u32[]{:S(2)}) collective-permute-start(f32[3,32,256]{2,1,0:T(8,128)} %get-tuple-element.23), channel_id=1, source_target_pairs={{8,0},{16,8},{24,16},{32,24},{40,32},{48,40},{56,48},{64,56},{72,6... | collective-permute-start | bytes 294920 | tf_op jit(solution)/shard_map/ppermute | solution.py:409
  174.5 14.5 %all-to-all-start.4 = ((s32[128,1,128]{2,1,0:T(1,128)}), s32[128,1,128]{2,1,0:T(1,128)S(1)}, u32[]{:S(2)}, u32[]{:S(2)}) async-start(s32[128,1,128]{2,1,0:T(1,128)} %bitcast.28), calls=%async_computation.4 | async-start | bytes 131072 | tf_op jit(solution)/shard_map/all_to_all | solution.py:413
  179.5 9.5 %collective-permute-start.6 = (f32[3,16,256]{2,1,0:T(8,128)}, f32[3,16,256]{2,1,0:T(8,128)S(1)}, u32[]{:S(2)}, u32[]{:S(2)}) collective-permute-start(f32[3,16,256]{2,1,0:T(8,128)} %get-tuple-element.24), channel_id=1, source_target_pairs={{0,1},{1,2},{2,3},{3,4},{4,5},{5,6},{6,7},{7,0},{8,9},{9,10},{10,1... | collective-permute-start | bytes 147464 | tf_op jit(solution)/shard_map/ppermute | solution.py:409
  181.4 7.6 %collective-permute-start.7 = (f32[3,16,256]{2,1,0:T(8,128)}, f32[3,16,256]{2,1,0:T(8,128)S(1)}, u32[]{:S(2)}, u32[]{:S(2)}) collective-permute-start(f32[3,16,256]{2,1,0:T(8,128)} %get-tuple-element.25), channel_id=1, source_target_pairs={{1,0},{2,1},{3,2},{4,3},{5,4},{6,5},{7,6},{0,7},{9,8},{10,9},{11,1... | collective-permute-start | bytes 147464 | tf_op jit(solution)/shard_map/ppermute | solution.py:409
  189.0 0.6 copy-start
  189.0 0.6 copy-start.5
  189.0 0.7 copy-start.6
  189.0 0.7 copy-start.1
  189.0 0.7 copy-start.2

commit v2 on v1

v2 whole, which is shorter than its diff:
```python
import functools

import jax
import jax.numpy as jnp
import ml_dtypes
import numpy as np
from jax import lax
from jax.experimental import pallas as pl
from jax.experimental.pallas import tpu as pltpu
from jax.sharding import PartitionSpec as P

F32 = jnp.float32
BF16 = jnp.bfloat16
REF_LAMBDA = 1.25
REF_SHEAR = 1.25
GRID = 256
HALF = 128
NPX = 16
NPY = 8
NX = 16
NY = 32
VMEM_LIMIT = 56 * 1024 * 1024
VM = pl.BlockSpec(memory_space=pltpu.VMEM)


def two_parts(table):
    table = np.asarray(table, np.float32)
    high = table.astype(ml_dtypes.bfloat16)
    low = (table - high.astype(np.float32)).astype(ml_dtypes.bfloat16)
    return np.stack([high, low])


def z_tables():
    z = np.arange(GRID)
    fwd = np.zeros((GRID, GRID))
    inv = np.zeros((GRID, GRID))
    for row in range(GRID):
        p, kzlo, ri, kzhi = row // 32, (row // 8) % 4, (row // 4) % 2, row % 4
        wave = 16 * p + 4 * kzhi + kzlo
        angle = 2 * np.pi * ((wave * z) % GRID) / GRID
        if wave == 0:
            line = np.ones(GRID) if ri == 0 else 1.0 - 2.0 * (z % 2)
            fwd[row], inv[row] = line, line / GRID
        else:
            line = np.cos(angle) if ri == 0 else -np.sin(angle)
            fwd[row], inv[row] = line, 2 * line / GRID
    step = np.roll(np.eye(GRID), 1, 1) - np.roll(np.eye(GRID), -1, 1)
    fwd = 0.5 * np.stack([fwd, fwd @ step])
    inv = np.concatenate([inv, inv @ step.T], axis=1)
    return fwd, inv


def half_tables():
    k = np.arange(HALF)
    fwd, inv = [], []
    for e in range(2):
        angle = 2 * np.pi * (((2 * k[:, None] + e) * k[None, :]) % GRID) / GRID
        cos, sin = np.cos(angle), np.sin(angle)
        fwd.append(np.block([[cos, sin], [-sin, cos]]))
        inv.append(np.block([[cos.T, -sin.T], [sin.T, cos.T]]) / GRID)
    return np.stack(fwd), np.stack(inv)


def sines():
    wave = np.arange(GRID)
    line = np.sin(2 * np.pi * wave / GRID)
    line[wave % HALF == 0] = 0.0
    return line


def wave_lines():
    line = sines()
    sx = np.stack([line[0::2], line[1::2]])[:, :, None] * np.ones((1, 1, 128))
    sy = np.concatenate([line[0::2], line[1::2]])[None, :]
    sz = line[:128, None] * np.ones((1, 128))
    return sx.astype(np.float32), sy.astype(np.float32), sz.astype(np.float32)


def tile_weights():
    v = np.arange(128, dtype=np.float64)
    weights = np.exp(-((v[None, :] - v[:, None]) ** 2) / (2.0 * 16.0**2))
    return weights / weights.sum(axis=1, keepdims=True)


def split(values):
    high = values.astype(BF16)
    low = (values - high.astype(F32)).astype(BF16)
    return high, low


def dot(a, b, dims=((1,), (0,))):
    return lax.dot_general(a, b, (dims, ((), ())), preferred_element_type=F32)


def dot3(a, b, dims=((1,), (0,))):
    (ah, al), (bh, bl) = a, b
    return dot(ah, bh, dims) + (dot(ah, bl, dims) + dot(al, bh, dims))


def swap_groups(values):
    count = len(values)
    width = 128 // count
    lane = lax.broadcasted_iota(jnp.int32, values[0].shape, values[0].ndim - 1)
    axis = values[0].ndim - 1
    values = list(values)
    step = 1
    while step < count:
        first = ((lane // (width * step)) % 2) == 0
        out = list(values)
        for i in range(count):
            if i & step == 0:
                low, high = values[i], values[i + step]
                out[i] = jnp.where(first, low, pltpu.roll(high, width * step, axis))
                out[i + step] = jnp.where(first, pltpu.roll(low, 128 - width * step, axis), high)
        values = out
        step *= 2
    return values


def call(body, out_shape, scratch=(), n_in=0, n_any=0, collective=None):
    multi = isinstance(out_shape, (list, tuple))
    remote = {} if collective is None else {"collective_id": collective, "has_side_effects": True}
    return pl.pallas_call(
        body,
        out_shape=out_shape,
        in_specs=[VM] * n_in + [pl.BlockSpec(memory_space=pl.ANY)] * n_any,
        out_specs=[VM] * len(out_shape) if multi else VM,
        scratch_shapes=list(scratch),
        compiler_params=pltpu.CompilerParams(vmem_limit_bytes=VMEM_LIMIT, **remote),
    )


def send(src, dst, sems, where):
    return pltpu.make_async_remote_copy(
        src_ref=src,
        dst_ref=dst,
        send_sem=sems[0],
        recv_sem=sems[1],
        device_id=where,
        device_id_type=pl.DeviceIdType.MESH,
    )


def greet(px, py):
    barrier = pltpu.get_barrier_semaphore()

    def row(d, carry):
        pl.semaphore_signal(
            barrier, inc=1, device_id=(px, lax.rem(py + d, NPY)), device_id_type=pl.DeviceIdType.MESH
        )
        return carry

    def column(d, carry):
        pl.semaphore_signal(
            barrier, inc=1, device_id=(lax.rem(px + d, NPX), py), device_id_type=pl.DeviceIdType.MESH
        )
        return carry

    lax.fori_loop(1, NPY, row, 0)
    lax.fori_loop(1, NPX, column, 0)
    pl.semaphore_wait(barrier, NPX + NPY - 2)


class Exchange:
    def __init__(self, axis, wire, got, sems, own_sem):
        self.count = NPX if axis == "px" else NPY
        self.axis, self.wire, self.got, self.sems, self.own_sem = axis, wire, got, sems, own_sem
        self.px, self.py = lax.axis_index("px"), lax.axis_index("py")
        self.me = self.px if axis == "px" else self.py

    def copy(self, d, c):
        peer = lax.rem(self.me + d, self.count)
        where = (peer, self.py) if self.axis == "px" else (self.px, peer)
        sems = (self.sems.at[0, c, d], self.sems.at[1, c, d])
        return send(self.wire.at[c, peer], self.got.at[c, self.me], sems, where)

    def own(self, c):
        return pltpu.make_async_copy(
            self.wire.at[c, self.me], self.got.at[c, self.me], self.own_sem.at[c]
        )

    def start(self, c):
        self.own(c).start()
        lax.fori_loop(1, self.count, lambda d, k: (self.copy(d, c).start(), k)[1], 0)

    def arrive(self, c):
        self.own(c).wait()
        lax.fori_loop(1, self.count, lambda d, k: (self.copy(d, c).wait_recv(), k)[1], 0)

    def finish(self, c):
        lax.fori_loop(1, self.count, lambda d, k: (self.copy(d, c).wait_send(), k)[1], 0)


def exchange_scratch(axis, parts, block, dtype=F32):
    count = NPX if axis == "px" else NPY
    return [
        pltpu.VMEM((parts, count) + block, dtype),
        pltpu.VMEM((parts, count) + block, dtype),
        pltpu.SemaphoreType.DMA((2, parts, count)),
        pltpu.SemaphoreType.DMA((parts,)),
    ]


def sds(shape, dtype=F32):
    return jax.ShapeDtypeStruct(shape, dtype)


def moduli_of(table, ids):
    lame, shear = [], []
    for half in range(2):
        index = ids[:, half * 128 : (half + 1) * 128]
        lame.append(jnp.take_along_axis(table, index, axis=1))
        shear.append(jnp.take_along_axis(table, index + 64, axis=1))
    return jnp.concatenate(lame, axis=1), jnp.concatenate(shear, axis=1)


def table_of(moduli_ref):
    row = jnp.concatenate([moduli_ref[0:1, :], moduli_ref[1:2, :]], axis=1)
    return jnp.broadcast_to(row, (NY, 128))


def polar_part(dist, ids, moduli, polar, xlo, xhi, ylo, yhi):
    table = table_of(moduli)

    def at_x(x, carry):
        lame, shear = moduli_of(table, ids[x])
        exx, eyy, ezz = dist[0, x], dist[4, x], dist[8, x]
        trace = lame * (exx + eyy + ezz)
        twice = shear + shear
        polar[0, x] = -(twice * exx + trace)
        polar[1, x] = -(twice * eyy + trace)
        polar[2, x] = -(twice * ezz + trace)
        polar[3, x] = -(shear * (dist[5, x] + dist[7, x]))
        polar[4, x] = -(shear * (dist[2, x] + dist[6, x]))
        polar[5, x] = -(shear * (dist[1, x] + dist[3, x]))
        return carry

    lax.fori_loop(0, NX, at_x, 0)
    for slot, comp in enumerate((0, 5, 4)):
        xlo[slot] = polar[comp, 0]
        xhi[slot] = polar[comp, NX - 1]
    for slot, comp in enumerate((5, 1, 3)):
        ylo[slot] = polar[comp, :, 0, :]
        yhi[slot] = polar[comp, :, NY - 1, :]


def row_of(device):
    return (device % NPY) * NPX + device // NPY


def request_part(source, tile, centre, asked, slot_out):
    src = jnp.broadcast_to(source[...], (512, 128))
    src = row_of(src).astype(F32)
    src_lane = jnp.transpose(src)[0:1, :]
    same = src[:, 0:1] == src_lane
    first = lax.broadcasted_iota(jnp.int32, (512, 512), 0)
    second = lax.broadcasted_iota(jnp.int32, (512, 512), 1)
    slot_lane = jnp.sum(jnp.where(same & (first < second), 1.0, 0.0), axis=0, keepdims=True)
    slot_out[...] = jnp.sum(jnp.where(same & (second < first), 1.0, 0.0), axis=1, keepdims=True)
    match = (src == lax.broadcasted_iota(jnp.int32, (512, 128), 1).astype(F32)).astype(F32).astype(BF16)
    row = lax.broadcasted_iota(jnp.int32, (8, 512), 0).astype(F32)
    here = row == slot_lane
    tile_v = tile[...]
    values = [tile_v // 8, tile_v % 8, centre[...]]
    rows = [jnp.where(here, v.astype(F32), 0.0) for v in values]
    stacked = jnp.concatenate(rows + [jnp.zeros((8, 512), F32)], axis=0).astype(BF16)
    got = dot(stacked, match)
    both = jnp.concatenate([got[0:8] * 8.0 + got[8:16], got[16:24], jnp.zeros((112, 128), F32)], axis=0)
    asked[...] = jnp.transpose(both).astype(jnp.int32)


def prepare_body(
    dist, ids, moduli, source, tile, centre, polar, xlo, xhi, ylo, yhi, asked, slot
):
    request_part(source, tile, centre, asked, slot)
    polar_part(dist, ids, moduli, polar, xlo, xhi, ylo, yhi)


def shift_y(values, before, after):
    row = lax.broadcasted_iota(jnp.int32, values.shape, 0)
    up = jnp.where(row == NY - 1, after, pltpu.roll(values, NY - 1, 0))
    down = jnp.where(row == 0, before, pltpu.roll(values, 1, 0))
    return up - down


def forward_z(c, polar, faces, tz, wire, force, swap):
    cx, cy, cz = ((0, 5, 4), (5, 1, 3), (4, 3, 2))[c]
    xbefore, xafter, ybefore, yafter = faces
    for x in range(NX):
        after = xafter[c] if x == NX - 1 else polar[cx, x + 1]
        before = xbefore[c] if x == 0 else polar[cx, x - 1]
        grad_y = shift_y(polar[cy, x], ybefore[c, x : x + 1], yafter[c, x : x + 1])
        for part, values in enumerate(((after - before) + grad_y, polar[cz, x])):
            hi, lo = split(values)
            force[0, part, x * NY : (x + 1) * NY, :] = hi
            force[1, part, x * NY : (x + 1) * NY, :] = lo
    last = ((1,), (1,))
    waves = dot3((tz[0, 0], tz[1, 0]), (force[0, 0], force[1, 0]), last)
    waves = waves + dot3((tz[0, 1], tz[1, 1]), (force[0, 1], force[1, 1]), last)
    for p in range(NPY):
        for xg in range(4):
            tiles = [
                waves[p * 32 + kzlo * 8 : p * 32 + kzlo * 8 + 8, xg * 128 : xg * 128 + 128]
                for kzlo in range(4)
            ]
            for x4, tile in enumerate(swap_groups(tiles)):
                x = xg * 4 + x4
                swap[p * 128 + x * 8 : p * 128 + x * 8 + 8, :] = tile
        for s in range(8):
            wire[c, p, s] = swap[pl.ds(p * 128 + s, NX, stride=8), :]


def forward_y(c, got, ty, wire, rows):
    for ri in range(2):
        for kzhi in range(4):
            s = ri * 4 + kzhi
            low = swap_groups([got[c, q, s] for q in range(4)])
            high = swap_groups([got[c, q + 4, s] for q in range(4)])
            for kzlo in range(4):
                row = (kzhi * 4 + kzlo) * NX
                for e in range(2):
                    hi, lo = split(low[kzlo] + high[kzlo] if e == 0 else low[kzlo] - high[kzlo])
                    rows[0, e, row : row + NX, ri * 128 : ri * 128 + 128] = hi
                    rows[1, e, row : row + NX, ri * 128 : ri * 128 + 128] = lo
    for e in range(2):
        out = dot3((rows[0, e], rows[1, e]), (ty[0, e], ty[1, e]))
        for kz in range(NX):
            wire[c, kz, :, e * 256 : e * 256 + 256] = out[kz * NX : kz * NX + NX, :]


def forward_x(c, got, tx, waves, rows):
    for q in range(8):
        a, b = got[c, q], got[c, q + 8]
        for ex in range(2):
            hi, lo = split(a + b if ex == 0 else a - b)
            for ri in range(2):
                row = ri * 128 + q * 16
                for e in range(2):
                    lane = e * 256 + ri * 128
                    rows[0, ex, row : row + 16, e * 128 : e * 128 + 128] = hi[:, lane : lane + 128]
                    rows[1, ex, row : row + 16, e * 128 : e * 128 + 128] = lo[:, lane : lane + 128]
    for ex in range(2):
        waves[ex, c] = dot3((tx[0, ex], tx[1, ex]), (rows[0, ex], rows[1, ex]))


def solve(waves, solved, sx, sy, sz, py, px):
    sy = sy[...]
    sz = sz[pl.ds(py * 16 + px, 1), :]
    sz = jnp.concatenate([sz, sz], axis=1)
    coupling = (REF_LAMBDA + REF_SHEAR) / (REF_LAMBDA + 2.0 * REF_SHEAR)
    rest = sy * sy + sz * sz
    for ex in range(2):
        wx = jnp.concatenate([sx[ex], sx[ex]], axis=1)
        squared = wx * wx + rest
        null = squared == 0.0
        inverse = jnp.where(null, 0.0, 1.0 / jnp.where(null, 1.0, squared))
        scale = inverse * (1.0 / REF_SHEAR)
        for ri in range(2):
            parts = [waves[ex, c, ri * 128 : ri * 128 + 128, :] for c in range(3)]
            common = coupling * inverse * (wx * parts[0] + sy * parts[1] + sz * parts[2])
            for c, line in enumerate((wx, sy, sz)):
                hi, lo = split(scale * (parts[c] - common * line))
                solved[0, ex, c, ri * 128 : ri * 128 + 128, :] = hi
                solved[1, ex, c, ri * 128 : ri * 128 + 128, :] = lo


def inverse_x(c, solved, txi, wire):
    backs = [dot3((txi[0, ex], txi[1, ex]), (solved[0, ex, c], solved[1, ex, c])) for ex in range(2)]
    for half, out in enumerate((backs[0] + backs[1], backs[0] - backs[1])):
        for q in range(8):
            for ri in range(2):
                row = ri * 128 + q * 16
                for e in range(2):
                    lane = e * 256 + ri * 128
                    wire[c, half * 8 + q, :, lane : lane + 128] = out[row : row + 16, e * 128 : e * 128 + 128]


def inverse_y(c, got, tyi, wire):
    outs = []
    for e in range(2):
        rows = jnp.concatenate([got[c, kz, :, e * 256 : e * 256 + 256] for kz in range(NX)], axis=0)
        outs.append(dot3(split(rows), (tyi[0, e], tyi[1, e])))
    for half, out in enumerate((outs[0] + outs[1], outs[0] - outs[1])):
        for ri in range(2):
            for kzhi in range(4):
                tiles = [
                    out[(kzhi * 4 + k) * NX : (kzhi * 4 + k + 1) * NX, ri * 128 : ri * 128 + 128]
                    for k in range(4)
                ]
                for q4, tile in enumerate(swap_groups(tiles)):
                    wire[c, half * 4 + q4, ri * 4 + kzhi] = tile


def inverse_z(c, got, tzi, disp, grad, yface, waves, swap):
    for p in range(NPY):
        for s in range(8):
            swap[p * 128 + s * 16 : p * 128 + s * 16 + 16, :] = got[c, p, s]
        for xg in range(4):
            tiles = [swap[pl.ds(p * 128 + xg * 4 + x4, 8, stride=16), :] for x4 in range(4)]
            for kzlo, tile in enumerate(swap_groups(tiles)):
                row = p * 32 + kzlo * 8
                waves[row : row + 8, xg * 128 : xg * 128 + 128] = tile
    turned = split(jnp.transpose(waves[...]))
    out = dot3(turned, (tzi[0, :, :256], tzi[1, :, :256]))
    for x in range(NX):
        disp[c, x] = out[x * NY : (x + 1) * NY, :]
        yface[0, c, x : x + 1] = out[x * NY : x * NY + 1, :]
        yface[1, c, x : x + 1] = out[x * NY + NY - 1 : x * NY + NY, :]
    out = dot3(turned, (tzi[0, :, 256:], tzi[1, :, 256:]))
    for x in range(NX):
        grad[c, x] = out[x * NY : (x + 1) * NY, :]


def faces_copies(px, py, sources, targets, sems):
    left, right = lax.rem(px + NPX - 1, NPX), lax.rem(px + 1, NPX)
    down, up = lax.rem(py + NPY - 1, NPY), lax.rem(py + 1, NPY)
    plan = ((0, 1, (left, py)), (1, 0, (right, py)), (2, 3, (px, down)), (3, 2, (px, up)))
    return [send(sources[a], targets[b], (sems.at[0, b], sems.at[1, b]), where) for a, b, where in plan]


def solve_body(
    polar, xlo, xhi, ylo, yhi, asked_out, sx, sy, sz, tz_h, ty_h, tx_h, txi_h, tyi_h, tzi_h,
    disp, grad, xbefore, xafter, ybefore, yafter, asked,
    w1, g1, s1, o1, w2, g2, s2, o2, w3, g3, s3, o3, w4, g4, s4, o4,
    wa, ga, sa, oa, wb, gb, sb, ob,
    fx, fy, face_sem, back_sem, hx, hy, yface,
    tz, ty, tx, txi, tyi, tzi, table_sem,
    force, swap, rows, waves, solved, lines,
):
    px, py = lax.axis_index("px"), lax.axis_index("py")
    tables = [
        pltpu.make_async_copy(src, dst, table_sem.at[i])
        for i, (src, dst) in enumerate(
            ((tz_h, tz), (ty_h, ty), (tx_h, tx), (txi_h, txi), (tyi_h, tyi), (tzi_h, tzi))
        )
    ]
    for table in tables:
        table.start()
    greet(px, py)
    halo = faces_copies(
        px, py, (xlo, xhi, ylo, yhi), (fx.at[0], fx.at[1], fy.at[0], fy.at[1]), face_sem
    )
    for copy in halo:
        copy.start()
    ex1 = Exchange("py", w1, g1, s1, o1)
    ex2 = Exchange("px", w2, g2, s2, o2)
    ex3 = Exchange("px", w3, g3, s3, o3)
    ex4 = Exchange("py", w4, g4, s4, o4)
    exa = Exchange("py", wa, ga, sa, oa)
    exb = Exchange("px", wb, gb, sb, ob)
    for p in range(NPY):
        wa[0, p] = asked_out[p * NPX : p * NPX + NPX, :]
    exa.start(0)
    tables[0].wait()
    for copy in halo:
        copy.wait_recv()
    for c in range(3):
        forward_z(c, polar, (fx.at[0], fx.at[1], fy.at[0], fy.at[1]), tz, w1, force, swap)
        ex1.start(c)
    exa.arrive(0)
    asked[...] = ga[0].reshape(128, 128)
    for p in range(NPX):
        wb[0, p] = asked[pl.ds(p, NPY, stride=NPX), :]
    exb.start(0)
    tables[1].wait()
    for c in range(3):
        ex1.arrive(c)
        forward_y(c, g1, ty, w2, rows)
        ex2.start(c)
    tables[2].wait()
    for c in range(3):
        ex2.arrive(c)
        forward_x(c, g2, tx, waves, rows)
    solve(waves, solved, sx, sy, sz, py, px)
    tables[3].wait()
    for c in range(3):
        inverse_x(c, solved, txi, w3)
        ex3.start(c)
    tables[4].wait()
    exb.arrive(0)
    for p in range(NPX):
        asked[p * NPY : p * NPY + NPY, :] = gb[0, p]
    for c in range(3):
        ex3.arrive(c)
        inverse_y(c, g3, tyi, w4)
        ex4.start(c)
    tables[5].wait()
    backs = []
    for c in range(3):
        ex4.arrive(c)
        inverse_z(c, g4, tzi, disp, grad, yface, lines, swap)
        back = faces_copies(
            px,
            py,
            (disp.at[c, 0], disp.at[c, NX - 1], yface.at[0, c], yface.at[1, c]),
            (hx.at[0, c], hx.at[1, c], hy.at[0, c], hy.at[1, c]),
            back_sem.at[c],
        )
        for copy in back:
            copy.start()
        backs += back
    for copy in backs:
        copy.wait_recv()
    xbefore[...] = hx[0]
    xafter[...] = hx[1]
    ybefore[...] = hy[0]
    yafter[...] = hy[1]
    for copy in halo + backs:
        copy.wait_send()
    exa.finish(0)
    exb.finish(0)
    for c in range(3):
        for ex in (ex1, ex2, ex3, ex4):
            ex.finish(c)


def stress_body(
    disp, grad, xbefore, xafter, ybefore, yafter, polar, ids, moduli, asked, weights,
    stress, reply, rows_h, rows_l,
):
    table = table_of(moduli)
    for x in range(NX):
        lame, shear = moduli_of(table, ids[x])
        gx, gy, gz = [], [], []
        for c in range(3):
            after = xafter[c] if x == NX - 1 else disp[c, x + 1]
            before = xbefore[c] if x == 0 else disp[c, x - 1]
            gx.append(after - before)
            gy.append(shift_y(disp[c, x], ybefore[c, x : x + 1], yafter[c, x : x + 1]))
            gz.append(grad[c, x])
        trace = (0.5 * lame) * (gx[0] + gy[1] + gz[2])
        half = 0.5 * shear
        parts = (
            shear * gx[0] + trace,
            shear * gy[1] + trace,
            shear * gz[2] + trace,
            half * (gz[1] + gy[2]),
            half * (gz[0] + gx[2]),
            half * (gy[0] + gx[1]),
        )
        for c, part in enumerate(parts):
            total = part + polar[c, x]
            stress[c, x] = total
            hi, lo = split(total)
            rows_h[x * NY : (x + 1) * NY, c * 256 : c * 256 + 256] = hi
            rows_l[x * NY : (x + 1) * NY, c * 256 : c * 256 + 256] = lo
    column = lax.broadcasted_iota(jnp.int32, (128, 512), 1)
    lane = lax.broadcasted_iota(jnp.int32, (128, 128), 1)
    lane256 = lax.broadcasted_iota(jnp.int32, (128, 256), 1)
    out = jnp.zeros((128, 128), F32)
    wh, wl = weights[0], weights[1]
    for k in range(8):
        tile = asked[:, k : k + 1]
        centre = asked[:, 8 + k : 9 + k]
        pick = (column == tile // 2).astype(F32).astype(BF16)
        picked = dot(pick, rows_h[...]) + dot(pick, rows_l[...])
        at = (lane == centre).astype(F32).astype(BF16)
        row = dot(at, wh) + dot(at, wl)
        weight = jnp.where(lane256 // 128 == tile % 2, jnp.concatenate([row, row], axis=1), 0.0)
        for c in range(6):
            value = jnp.sum(picked[:, c * 256 : c * 256 + 256] * weight, axis=1, keepdims=True)
            out = jnp.where(lane == c * 8 + k, value, out)
    reply[...] = out


def force_body(
    reply, source, slot, burgers, line, out, wa, ga, sa, oa, wb, gb, sb, ob, turn
):
    px, py = lax.axis_index("px"), lax.axis_index("py")
    greet(px, py)
    exa = Exchange("px", wa, ga, sa, oa)
    exb = Exchange("py", wb, gb, sb, ob)
    for p in range(NPX):
        wa[0, p] = reply[p * NPY : p * NPY + NPY, :]
    exa.start(0)
    src = row_of(jnp.broadcast_to(source[...], (512, 128)))
    match = (src == lax.broadcasted_iota(jnp.int32, (512, 128), 1)).astype(F32).astype(BF16)
    exa.arrive(0)
    turn[...] = ga[0].reshape(128, 128)
    for p in range(NPY):
        wb[0, p] = turn[pl.ds(p, NPX, stride=NPY), :]
    exb.start(0)
    exb.arrive(0)
    value = gb[0].reshape(128, 128)
    hi, lo = split(value)
    low = (value - hi.astype(F32) - lo.astype(F32)).astype(BF16)
    got = dot(match, hi) + (dot(match, lo) + dot(match, low))
    lane = lax.broadcasted_iota(jnp.int32, (512, 128), 1)
    slot_v = slot[...].astype(jnp.int32)
    mine = jnp.transpose(jnp.where(lane % 8 == slot_v, got, 0.0))
    t = [jnp.sum(mine[c * 8 : c * 8 + 8, :], axis=0, keepdims=True) for c in range(6)]
    b = [burgers[i : i + 1, :] for i in range(3)]
    v = [line[i : i + 1, :] for i in range(3)]
    push_x = t[0] * b[0] + t[5] * b[1] + t[4] * b[2]
    push_y = t[5] * b[0] + t[1] * b[1] + t[3] * b[2]
    push_z = t[4] * b[0] + t[3] * b[1] + t[2] * b[2]
    out[0:1, :] = push_y * v[2] - push_z * v[1]
    out[1:2, :] = push_z * v[0] - push_x * v[2]
    out[2:3, :] = push_x * v[1] - push_y * v[0]
    exa.finish(0)
    exb.finish(0)


FACE_X = sds((3, NY, GRID))
FACE_Y = sds((3, NX, GRID))
FIELD = sds((3, NX, NY, GRID))


def solve_scratch():
    half = pltpu.VMEM((2, 2, 256, 256), BF16)
    field = (8, NX, 128)
    wave = (NX, 512)
    return (
        exchange_scratch("py", 3, field)
        + exchange_scratch("px", 3, wave)
        + exchange_scratch("px", 3, wave)
        + exchange_scratch("py", 3, field)
        + exchange_scratch("py", 1, (NPX, 128), jnp.int32)
        + exchange_scratch("px", 1, (NPY, 128), jnp.int32)
        + [pltpu.VMEM((2, 3, NY, GRID), F32), pltpu.VMEM((2, 3, NX, GRID), F32)]
        + [pltpu.SemaphoreType.DMA((2, 4)), pltpu.SemaphoreType.DMA((3, 2, 4))]
        + [pltpu.VMEM((2, 3, NY, GRID), F32), pltpu.VMEM((2, 3, NX, GRID), F32)]
        + [pltpu.VMEM((2, 3, NX, GRID), F32)]
        + [half] * 5
        + [pltpu.VMEM((2, 256, 512), BF16), pltpu.SemaphoreType.DMA((6,))]
        + [pltpu.VMEM((2, 2, 512, 256), BF16), pltpu.VMEM((1024, 128), F32), half]
        + [pltpu.VMEM((2, 3, 256, 256), F32), pltpu.VMEM((2, 2, 3, 256, 256), BF16)]
        + [pltpu.VMEM((256, 512), F32)]
    )


def shards(dist, ids, moduli, seg_source, seg_tile, seg_center, burgers, line_vector):
    fwd_z, inv_z = z_tables()
    fwd_h, inv_h = half_tables()
    tz, tzi = two_parts(fwd_z), two_parts(inv_z)
    tx, txi = two_parts(fwd_h), two_parts(inv_h)
    ty = two_parts(fwd_h.transpose(0, 2, 1))
    tyi = two_parts(inv_h.transpose(0, 2, 1))
    sx, sy, sz = wave_lines()
    weights = two_parts(tile_weights())

    faces = (FACE_X, FACE_X, FACE_Y, FACE_Y)
    polar, xlo, xhi, ylo, yhi, asked, slot = call(
        prepare_body,
        (sds((6, NX, NY, GRID)),) + faces + (sds((128, 128), jnp.int32), sds((512, 1))),
        n_in=6,
    )(dist, ids, moduli, seg_source, seg_tile.reshape(1, 512), seg_center.reshape(1, 512))
    disp, grad, xbefore, xafter, ybefore, yafter, asked = call(
        solve_body,
        (FIELD, FIELD) + faces + (sds((128, 128), jnp.int32),),
        solve_scratch(),
        n_in=9,
        n_any=6,
        collective=0,
    )(polar, xlo, xhi, ylo, yhi, asked, sx, sy, sz, tz, ty, tx, txi, tyi, tzi)
    stress, reply = call(
        stress_body,
        (sds((6, NX, NY, GRID)), sds((128, 128))),
        [pltpu.VMEM((512, 1536), BF16)] * 2,
        n_in=11,
    )(disp, grad, xbefore, xafter, ybefore, yafter, polar, ids, moduli, asked, weights)
    seg_force = call(
        force_body,
        sds((3, 512)),
        exchange_scratch("px", 1, (NPY, 128))
        + exchange_scratch("py", 1, (NPX, 128))
        + [pltpu.VMEM((128, 128), F32)],
        n_in=5,
        collective=1,
    )(reply, seg_source, slot, burgers, line_vector)
    return stress, seg_force


def solution(mesh):
    return jax.shard_map(
        shards,
        mesh=mesh,
        in_specs=(
            P(None, "px", "py", None),
            P("px", "py", None),
            P(),
            P(("px", "py"), None),
            P(("px", "py")),
            P(("px", "py")),
            P(None, ("px", "py")),
            P(None, ("px", "py")),
        ),
        out_specs=(P(None, "px", "py", None), P(None, ("px", "py"))),
        check_vma=False,
    )
```

time: 217 us -> 125 us (0.58)
  blocking collectives: 120 us -> 0 us
  Pallas kernels: 62 us -> 122 us
  starting transfers between devices: 20.1 us -> 0 us
  waiting for transfers between devices: 11.3 us -> 0 us
    all_to_all x5 -> x0, blocking collectives: 120 us -> none  [exchange(): return lax.all_to_all(values, axis, split_axis=0, concat_axis=0, tiled=True)]
    pallas_call x8 -> x3, Pallas kernels: 53.1 us -> 113 us  [the longest x1 90.7 us: shards(): call(solve_body, (FIELD, FIELD) + faces + (sds((128, 128), jnp.int32),),...]
    ppermute x8 -> x0, starting transfers between devices: 15.1 us -> none  [neighbours(): return (lax.ppermute(high, axis, ahead), lax.ppermute(low, axis, back))]
    all_to_all x1 -> x0, waiting for transfers between devices: 7.59 us -> none  [exchange(): return lax.all_to_all(values, axis, split_axis=0, concat_axis=0, tiled=True)]
    all_to_all x1 -> x0, starting transfers between devices: 5 us -> none  [exchange(): return lax.all_to_all(values, axis, split_axis=0, concat_axis=0, tiled=True)]
    ppermute x8 -> x0, waiting for transfers between devices: 3.74 us -> none  [neighbours(): return (lax.ppermute(high, axis, ahead), lax.ppermute(low, axis, back))]
  transfers between devices with their start and end apart: 9 -> 0, of which waited for: 3 -> 0; matrix products, arithmetic and copies ran while one was open for 0% -> 0% of each run, Pallas kernels for 1% -> 0%
where the time goes in v2:
time: 125 us
  Pallas kernels  122 us (98%)
  local copies, waits for them, and re-layouts  2.84 us (2%)
    pallas_call x1, Pallas kernels, shards(): call(solve_body, (FIELD, FIELD) + faces + (sds((128, 128), jnp.int32),),...  90.7 us
    pallas_call x1, Pallas kernels, shards(): call(force_body, sds((3, 512)), exchange_scratch('px', 1, (NPY, 128)) + e...  15.1 us
    pallas_call x1, Pallas kernels, shards(): call(stress_body, (sds((6, NX, NY, GRID)), sds((128, 128))), [pltpu.VMEM(...  9.12 us
    pallas_call x1, Pallas kernels, shards(): call(prepare_body, (sds((6, NX, NY, GRID)),) + faces + (sds((128, 128), j...  6.81 us
    unnamed x2, local copies, waits for them, and re-layouts  2.84 us

profile of v2, /device:TPU:1, one launch (start us, length us, event | category | flops | bytes accessed | tf_op | source)
XLA Modules:
  0.0 125.2 jit_solution(8023097756363594601)
XLA Ops:
  0.6 1.5 %copy.20.source = s32[512,1]{1,0:T(8,128)} copy(s32[512,1]{0,1:T(1,128)} %param.21) | data formatting | bytes 4096 | tf_op args[3]
  2.2 6.8 %shard_map.185 = (f32[6,16,32,256]{3,2,1,0:T(8,128)}, f32[3,32,256]{2,1,0:T(8,128)}, f32[3,32,256]{2,1,0:T(8,128)}, f32[3,16,256]{2,1,0:T(8,128)}, f32[3,16,256]...) custom-call(f32[9,16,32,256]{3,2,1,0:T(8,128)} %dist.1, s32[16,32,256]{2,1,0:T(8,128)} %ids.3, f32[2,64]{1,0:T(2,128)} %moduli.3, ...), custom_call_target="tpu_custom_call" | custom-call | tf_op jit(solution)/shard_map/pallas_call | solution.py:643
  9.0 90.7 %shard_map.186 = (f32[3,16,32,256]{3,2,1,0:T(8,128)}, f32[3,16,32,256]{3,2,1,0:T(8,128)}, f32[3,32,256]{2,1,0:T(8,128)}, f32[3,32,256]{2,1,0:T(8,128)}, f32[3,16...) custom-call(f32[6,16,32,256]{3,2,1,0:T(8,128)} %get-tuple-element.18.polar, ...), custom_call_target="tpu_custom_call" | custom-call | tf_op jit(solution)/shard_map/pallas_call | solution.py:648
  99.7 9.1 %shard_map.187 = (f32[6,16,32,256]{3,2,1,0:T(8,128)}, f32[128,128]{1,0:T(8,128)}) custom-call(f32[3,16,32,256]{3,2,1,0:T(8,128)} %get-tuple-element.24.disp, f32[3,16,32,256]{3,2,1,0:T(8,128)} %get-tuple-element.25.grad, f32[3,32,256]{2,1,0:T(8,128)} %get-tuple-element.26.xbefore, f32[3,32,256]{2,1,0:T(8,128)} %get-tuple-element.27.xafter, ...), custom_call_target="tpu_custom_call" | custom-call | tf_op jit(solution)/shard_map/pallas_call | solution.py:656
  108.8 15.1 %shard_map.188 = f32[3,512]{1,0:T(4,128)} custom-call(f32[128,128]{1,0:T(8,128)} %get-tuple-element.32.reply, s32[512,1]{1,0:T(8,128)} %copy.20.source, f32[512,1]{1,0:T(8,128)} %get-tuple-element.33.slot, f32[3,512]{1,0:T(4,128)} %burgers.1, f32[3,512]{1,0:T(4,128)} %line.1), custom_call_target="tpu_custom_call" | custom-call | tf_op jit(solution)/shard_map/pallas_call | solution.py:662
  123.9 1.3 %copy.23 = f32[3,512]{1,0:T(4,128)} copy(f32[3,512]{1,0:T(4,128)} %shard_map.188) | data formatting | bytes 12288

commit v3 on v2

v3 whole, which is shorter than its diff:
```python
import functools

import jax
import jax.numpy as jnp
import ml_dtypes
import numpy as np
from jax import lax
from jax.experimental import pallas as pl
from jax.experimental.pallas import tpu as pltpu
from jax.sharding import PartitionSpec as P

F32 = jnp.float32
BF16 = jnp.bfloat16
REF_LAMBDA = 1.25
REF_SHEAR = 1.25
GRID = 256
HALF = 128
NPX = 16
NPY = 8
NX = 16
NY = 32
VMEM_LIMIT = 60 * 1024 * 1024
VM = pl.BlockSpec(memory_space=pltpu.VMEM)


def two_parts(table):
    table = np.asarray(table, np.float32)
    high = table.astype(ml_dtypes.bfloat16)
    low = (table - high.astype(np.float32)).astype(ml_dtypes.bfloat16)
    return np.stack([high, low])


def z_tables():
    z = np.arange(GRID)
    fwd = np.zeros((GRID, GRID))
    inv = np.zeros((GRID, GRID))
    for row in range(GRID):
        p, kzlo, ri, kzhi = row // 32, (row // 8) % 4, (row // 4) % 2, row % 4
        wave = 16 * p + 4 * kzhi + kzlo
        angle = 2 * np.pi * ((wave * z) % GRID) / GRID
        if wave == 0:
            line = np.ones(GRID) if ri == 0 else 1.0 - 2.0 * (z % 2)
            fwd[row], inv[row] = line, line / GRID
        else:
            line = np.cos(angle) if ri == 0 else -np.sin(angle)
            fwd[row], inv[row] = line, 2 * line / GRID
    step = np.roll(np.eye(GRID), 1, 1) - np.roll(np.eye(GRID), -1, 1)
    fwd = 0.5 * np.stack([fwd, fwd @ step])
    inv = np.concatenate([inv, inv @ step.T], axis=1)
    return fwd, inv


def half_tables():
    k = np.arange(HALF)
    fwd, inv = [], []
    for e in range(2):
        angle = 2 * np.pi * (((2 * k[:, None] + e) * k[None, :]) % GRID) / GRID
        cos, sin = np.cos(angle), np.sin(angle)
        fwd.append(np.block([[cos, sin], [-sin, cos]]))
        inv.append(np.block([[cos.T, -sin.T], [sin.T, cos.T]]) / GRID)
    return np.stack(fwd), np.stack(inv)


def sines():
    wave = np.arange(GRID)
    line = np.sin(2 * np.pi * wave / GRID)
    line[wave % HALF == 0] = 0.0
    return line


def wave_lines():
    line = sines()
    sx = np.stack([line[0::2], line[1::2]])[:, :, None] * np.ones((1, 1, 128))
    sy = np.concatenate([line[0::2], line[1::2]])[None, :]
    sz = line[:128, None] * np.ones((1, 128))
    return sx.astype(np.float32), sy.astype(np.float32), sz.astype(np.float32)


def tile_weights():
    v = np.arange(128, dtype=np.float64)
    weights = np.exp(-((v[None, :] - v[:, None]) ** 2) / (2.0 * 16.0**2))
    return weights / weights.sum(axis=1, keepdims=True)


def split(values):
    high = values.astype(BF16)
    low = (values - high.astype(F32)).astype(BF16)
    return high, low


def dot(a, b, dims=((1,), (0,))):
    return lax.dot_general(a, b, (dims, ((), ())), preferred_element_type=F32)


def dot3(a, b, dims=((1,), (0,))):
    (ah, al), (bh, bl) = a, b
    return dot(ah, bh, dims) + (dot(ah, bl, dims) + dot(al, bh, dims))


def swap_groups(values):
    count = len(values)
    width = 128 // count
    lane = lax.broadcasted_iota(jnp.int32, values[0].shape, values[0].ndim - 1)
    axis = values[0].ndim - 1
    values = list(values)
    step = 1
    while step < count:
        first = ((lane // (width * step)) % 2) == 0
        out = list(values)
        for i in range(count):
            if i & step == 0:
                low, high = values[i], values[i + step]
                out[i] = jnp.where(first, low, pltpu.roll(high, width * step, axis))
                out[i + step] = jnp.where(first, pltpu.roll(low, 128 - width * step, axis), high)
        values = out
        step *= 2
    return values


def send(src, dst, sems, where):
    return pltpu.make_async_remote_copy(
        src_ref=src,
        dst_ref=dst,
        send_sem=sems[0],
        recv_sem=sems[1],
        device_id=where,
        device_id_type=pl.DeviceIdType.MESH,
    )


def greet(px, py):
    barrier = pltpu.get_barrier_semaphore()
    for d in range(1, NPY):
        where = (px, lax.rem(py + d, NPY))
        pl.semaphore_signal(barrier, inc=1, device_id=where, device_id_type=pl.DeviceIdType.MESH)
    for d in range(1, NPX):
        where = (lax.rem(px + d, NPX), py)
        pl.semaphore_signal(barrier, inc=1, device_id=where, device_id_type=pl.DeviceIdType.MESH)


class Exchange:
    def __init__(self, axis, wire, got, sems, own_sem):
        self.count = NPX if axis == "px" else NPY
        self.axis, self.wire, self.got, self.sems, self.own_sem = axis, wire, got, sems, own_sem
        self.px, self.py = lax.axis_index("px"), lax.axis_index("py")
        self.me = self.px if axis == "px" else self.py

    def own(self, part):
        return pltpu.make_async_copy(
            self.wire.at[part, self.me], self.got.at[part, self.me], self.own_sem.at[part]
        )

    def start(self, part):
        for d in range(1, self.count):
            peer = lax.rem(self.me + d, self.count)
            where = (peer, self.py) if self.axis == "px" else (self.px, peer)
            sems = (self.sems.at[0, part], self.sems.at[1, part])
            send(self.wire.at[part, peer], self.got.at[part, self.me], sems, where).start()
        self.own(part).start()

    def all(self, side, part):
        block = self.got.at[part, pl.ds(0, self.count - 1)]
        return pltpu.make_async_copy(block, block, self.sems.at[side, part])

    def arrive(self, part):
        self.own(part).wait()
        self.all(1, part).wait()

    def finish(self, part):
        self.all(0, part).wait()


def exchange_scratch(axis, parts, block, dtype=F32):
    count = NPX if axis == "px" else NPY
    return [
        pltpu.VMEM((parts, count) + block, dtype),
        pltpu.VMEM((parts, count) + block, dtype),
        pltpu.SemaphoreType.DMA((2, parts)),
        pltpu.SemaphoreType.DMA((parts,)),
    ]


def sds(shape, dtype=F32):
    return jax.ShapeDtypeStruct(shape, dtype)


def moduli_of(table, ids):
    lame, shear = [], []
    for half in range(2):
        index = ids[:, half * 128 : (half + 1) * 128]
        lame.append(jnp.take_along_axis(table, index, axis=1))
        shear.append(jnp.take_along_axis(table, index + 64, axis=1))
    return jnp.concatenate(lame, axis=1), jnp.concatenate(shear, axis=1)


def table_of(moduli_ref):
    row = jnp.concatenate([moduli_ref[0:1, :], moduli_ref[1:2, :]], axis=1)
    return jnp.broadcast_to(row, (NY, 128))


def polar_part(first, count, dist, ids, table, polar, moduli):
    def at_x(x, carry):
        lame, shear = moduli_of(table, ids[x])
        moduli[0, x] = lame
        moduli[1, x] = shear
        exx, eyy, ezz = dist[0, x], dist[4, x], dist[8, x]
        trace = lame * (exx + eyy + ezz)
        twice = shear + shear
        polar[0, x] = -(twice * exx + trace)
        polar[1, x] = -(twice * eyy + trace)
        polar[2, x] = -(twice * ezz + trace)
        polar[3, x] = -(shear * (dist[5, x] + dist[7, x]))
        polar[4, x] = -(shear * (dist[2, x] + dist[6, x]))
        polar[5, x] = -(shear * (dist[1, x] + dist[3, x]))
        return carry

    lax.fori_loop(first, first + count, at_x, 0)


def row_of(device):
    return (device % NPY) * NPX + device // NPY


def request_part(source, tile, centre, asked):
    src_lane = row_of(source[...]).astype(F32)
    src = jnp.transpose(jnp.broadcast_to(src_lane, (128, 512)))
    same = src[:, 0:1] == src_lane
    first = lax.broadcasted_iota(jnp.int32, (512, 512), 0)
    second = lax.broadcasted_iota(jnp.int32, (512, 512), 1)
    slot_lane = jnp.sum(jnp.where(same & (first < second), 1.0, 0.0), axis=0, keepdims=True)
    match = (src == lax.broadcasted_iota(jnp.int32, (512, 128), 1).astype(F32)).astype(F32).astype(BF16)
    row = lax.broadcasted_iota(jnp.int32, (8, 512), 0).astype(F32)
    here = row == slot_lane
    tile_v = tile[...]
    values = [tile_v // 8, tile_v % 8, centre[...]]
    rows = [jnp.where(here, v.astype(F32), 0.0) for v in values]
    stacked = jnp.concatenate(rows + [jnp.zeros((8, 512), F32)], axis=0).astype(BF16)
    got = dot(stacked, match)
    both = jnp.concatenate([got[0:8] * 8.0 + got[8:16], got[16:24], jnp.zeros((112, 128), F32)], axis=0)
    asked[...] = jnp.transpose(both).astype(jnp.int32)
    return slot_lane


def shift_y(values, before, after):
    row = lax.broadcasted_iota(jnp.int32, values.shape, 0)
    up = jnp.where(row == NY - 1, after, pltpu.roll(values, NY - 1, 0))
    down = jnp.where(row == 0, before, pltpu.roll(values, 1, 0))
    return up - down


LAST = ((1,), (1,))


def forward_z_local(c, polar, tz, waves, force):
    for x in range(NX):
        hi, lo = split(polar[4 - c, x])
        force[0, x * NY : (x + 1) * NY, :] = hi
        force[1, x * NY : (x + 1) * NY, :] = lo
    waves[c, 0] = dot3((tz[0, 1], tz[1, 1]), (force[0, :256], force[1, :256]), LAST)
    waves[c, 1] = dot3((tz[0, 1], tz[1, 1]), (force[0, 256:], force[1, 256:]), LAST)


def forward_z(c, xh, polar, faces, tz, base, wire, force, swap):
    cx = (6 - c) * ((c + 1) // 2)
    cy = 5 - c - 3 * lax.rem(c, 2)
    part = c * 2 + xh
    fx, fy = faces
    for i in range(8):
        x = xh * 8 + i
        after = polar[cx, lax.rem(x + 1, NX)]
        before = polar[cx, lax.rem(x + NX - 1, NX)]
        if i == 0:
            before = jnp.where(xh == 0, fx[0, c], before)
        if i == 7:
            after = jnp.where(xh == 1, fx[1, c], after)
        ends = [fy[side, c, pl.ds(pl.multiple_of(xh * 8, 8), 8), :] for side in range(2)]
        grad_y = shift_y(polar[cy, x], ends[0][i : i + 1], ends[1][i : i + 1])
        hi, lo = split((after - before) + grad_y)
        force[0, i * NY : (i + 1) * NY, :] = hi
        force[1, i * NY : (i + 1) * NY, :] = lo
    waves = base[c, xh] + dot3((tz[0, 0], tz[1, 0]), (force[0, :256], force[1, :256]), LAST)
    for p in range(NPY):
        for xg in range(2):
            tiles = [
                waves[p * 32 + kzlo * 8 : p * 32 + kzlo * 8 + 8, xg * 128 : xg * 128 + 128]
                for kzlo in range(4)
            ]
            for x4, tile in enumerate(swap_groups(tiles)):
                row = p * 64 + (xg * 4 + x4) * 8
                swap[row : row + 8, :] = tile
        for s in range(8):
            wire[part, p, s] = swap[pl.ds(p * 64 + s, 8, stride=8), :]


def forward_y(part, got, ty, wire, rows):
    for ri in range(2):
        for kzhi in range(4):
            s = ri * 4 + kzhi
            low = swap_groups([got[part, q, s] for q in range(4)])
            high = swap_groups([got[part, q + 4, s] for q in range(4)])
            for kzlo in range(4):
                row = (kzhi * 4 + kzlo) * 8
                rows[0, row : row + 8, ri * 128 : ri * 128 + 128] = low[kzlo] + high[kzlo]
                rows[1, row : row + 8, ri * 128 : ri * 128 + 128] = low[kzlo] - high[kzlo]
    for e in range(2):
        out = dot3(split(rows[e]), (ty[0, e], ty[1, e]))
        for kz in range(NX):
            wire[part, kz, :, e * 256 : e * 256 + 256] = out[kz * 8 : kz * 8 + 8, :]


def forward_x(c, got, tx, waves, rows):
    for q in range(8):
        a = jnp.concatenate([got[2 * c, q], got[2 * c + 1, q]], axis=0)
        b = jnp.concatenate([got[2 * c, q + 8], got[2 * c + 1, q + 8]], axis=0)
        for ex in range(2):
            hi, lo = split(a + b if ex == 0 else a - b)
            for ri in range(2):
                row = ri * 128 + q * 16
                for e in range(2):
                    lane = e * 256 + ri * 128
                    rows[0, ex, row : row + 16, e * 128 : e * 128 + 128] = hi[:, lane : lane + 128]
                    rows[1, ex, row : row + 16, e * 128 : e * 128 + 128] = lo[:, lane : lane + 128]
    for ex in range(2):
        waves[ex, c] = dot3((tx[0, ex], tx[1, ex]), (rows[0, ex], rows[1, ex]))


def solve(waves, solved, sx, sy, sz, py, px):
    sy = sy[...]
    sz = sz[pl.ds(py * 16 + px, 1), :]
    sz = jnp.concatenate([sz, sz], axis=1)
    coupling = (REF_LAMBDA + REF_SHEAR) / (REF_LAMBDA + 2.0 * REF_SHEAR)
    rest = sy * sy + sz * sz
    for ex in range(2):
        wx = jnp.concatenate([sx[ex], sx[ex]], axis=1)
        squared = wx * wx + rest
        null = squared == 0.0
        inverse = jnp.where(null, 0.0, 1.0 / jnp.where(null, 1.0, squared))
        scale = inverse * (1.0 / REF_SHEAR)
        for ri in range(2):
            parts = [waves[ex, c, ri * 128 : ri * 128 + 128, :] for c in range(3)]
            common = coupling * inverse * (wx * parts[0] + sy * parts[1] + sz * parts[2])
            for c, line in enumerate((wx, sy, sz)):
                hi, lo = split(scale * (parts[c] - common * line))
                solved[0, ex, c, ri * 128 : ri * 128 + 128, :] = hi
                solved[1, ex, c, ri * 128 : ri * 128 + 128, :] = lo


def inverse_x(c, solved, txi, wire):
    backs = [dot3((txi[0, ex], txi[1, ex]), (solved[0, ex, c], solved[1, ex, c])) for ex in range(2)]
    for half, out in enumerate((backs[0] + backs[1], backs[0] - backs[1])):
        for q in range(8):
            for xh in range(2):
                for ri in range(2):
                    row = ri * 128 + q * 16 + xh * 8
                    for e in range(2):
                        lane = e * 256 + ri * 128
                        wire[2 * c + xh, half * 8 + q, :, lane : lane + 128] = out[
                            row : row + 8, e * 128 : e * 128 + 128
                        ]


def inverse_y(part, got, tyi, wire):
    outs = []
    for e in range(2):
        rows = jnp.concatenate([got[part, kz, :, e * 256 : e * 256 + 256] for kz in range(NX)], axis=0)
        outs.append(dot3(split(rows), (tyi[0, e], tyi[1, e])))
    for half, out in enumerate((outs[0] + outs[1], outs[0] - outs[1])):
        for ri in range(2):
            for kzhi in range(4):
                tiles = [
                    out[(kzhi * 4 + k) * 8 : (kzhi * 4 + k + 1) * 8, ri * 128 : ri * 128 + 128]
                    for k in range(4)
                ]
                for q4, tile in enumerate(swap_groups(tiles)):
                    wire[part, half * 4 + q4, ri * 4 + kzhi] = tile


def inverse_z(c, xh, got, tzi, disp, grad, yface, waves, swap):
    part = c * 2 + xh
    for p in range(NPY):
        for s in range(8):
            swap[p * 64 + s * 8 : p * 64 + s * 8 + 8, :] = got[part, p, s]
        for xg in range(2):
            tiles = [swap[pl.ds(p * 64 + xg * 4 + x4, 8, stride=8), :] for x4 in range(4)]
            for kzlo, tile in enumerate(swap_groups(tiles)):
                row = p * 32 + kzlo * 8
                waves[row : row + 8, xg * 128 : xg * 128 + 128] = tile
    turned = split(jnp.transpose(waves[...]))
    out = dot3(turned, (tzi[0, :, :256], tzi[1, :, :256]))
    for i in range(8):
        x = xh * 8 + i
        disp[c, x] = out[i * NY : (i + 1) * NY, :]
        yface[xh, 0, c, i : i + 1] = out[i * NY : i * NY + 1, :]
        yface[xh, 1, c, i : i + 1] = out[i * NY + NY - 1 : i * NY + NY, :]
    out = dot3(turned, (tzi[0, :, 256:], tzi[1, :, 256:]))
    for i in range(8):
        grad[c, xh * 8 + i] = out[i * NY : (i + 1) * NY, :]


def stress_part(first, count, disp, grad, hx, hy, polar, moduli, stress, rows):
    xh = first // 8

    def at_x(x, carry):
        lame, shear = moduli[0, x], moduli[1, x]
        gx, gy, gz = [], [], []
        i = x - xh * 8
        for c in range(3):
            after = hx[1, c] if first == NX - 1 else disp[c, x + 1]
            before = hx[0, c] if first == 0 else disp[c, x - 1]
            gx.append(after - before)
            gy.append(shift_y(disp[c, x], hy[xh, 0, c, pl.ds(i, 1), :], hy[xh, 1, c, pl.ds(i, 1), :]))
            gz.append(grad[c, x])
        trace = (0.5 * lame) * (gx[0] + gy[1] + gz[2])
        half = 0.5 * shear
        parts = (
            shear * gx[0] + trace,
            shear * gy[1] + trace,
            shear * gz[2] + trace,
            half * (gz[1] + gy[2]),
            half * (gz[0] + gx[2]),
            half * (gy[0] + gx[1]),
        )
        row = pl.ds(pl.multiple_of(x * NY, NY), NY)
        for c, part in enumerate(parts):
            total = part + polar[c, x]
            stress[c, x] = total
            hi, lo = split(total)
            rows[0, row, c * 256 : c * 256 + 256] = hi
            rows[1, row, c * 256 : c * 256 + 256] = lo
        return carry

    lax.fori_loop(first, first + count, at_x, 0)


def reply_part(xh, asked, weights, rows, reply):
    column = lax.broadcasted_iota(jnp.int32, (128, 256), 1) + xh * 256
    lane = lax.broadcasted_iota(jnp.int32, (128, 128), 1)
    lane256 = lax.broadcasted_iota(jnp.int32, (128, 256), 1)
    out = reply[...] if xh else jnp.zeros((128, 128), F32)
    wh, wl = weights[0], weights[1]
    for k in range(8):
        tile = asked[:, k : k + 1]
        centre = asked[:, 8 + k : 9 + k]
        pick = (column == tile // 2).astype(F32).astype(BF16)
        here = slice(xh * 256, xh * 256 + 256)
        picked = dot(pick, rows[0, here, :]) + dot(pick, rows[1, here, :])
        at = (lane == centre).astype(F32).astype(BF16)
        row = dot(at, wh) + dot(at, wl)
        weight = jnp.where(lane256 // 128 == tile % 2, jnp.concatenate([row, row], axis=1), 0.0)
        for c in range(6):
            value = jnp.sum(picked[:, c * 256 : c * 256 + 256] * weight, axis=1, keepdims=True)
            out = out + jnp.where(lane == c * 8 + k, value, 0.0)
    reply[...] = out


def force_part(reply, source, slot, burgers, line, out):
    match = lax.broadcasted_iota(jnp.int32, (128, 512), 0) == row_of(source[...])
    match = match.astype(F32).astype(BF16)
    hi, lo = split(reply)
    low = (reply - hi.astype(F32) - lo.astype(F32)).astype(BF16)
    first = ((0,), (0,))
    got = dot(hi, match, first) + (dot(lo, match, first) + dot(low, match, first))
    lane = lax.broadcasted_iota(jnp.int32, (128, 512), 0)
    mine = jnp.where((lane % 8).astype(F32) == slot[...], got, 0.0)
    t = [jnp.sum(mine[c * 8 : c * 8 + 8, :], axis=0, keepdims=True) for c in range(6)]
    b = [burgers[i : i + 1, :] for i in range(3)]
    v = [line[i : i + 1, :] for i in range(3)]
    push_x = t[0] * b[0] + t[5] * b[1] + t[4] * b[2]
    push_y = t[5] * b[0] + t[1] * b[1] + t[3] * b[2]
    push_z = t[4] * b[0] + t[3] * b[1] + t[2] * b[2]
    out[0:1, :] = push_y * v[2] - push_z * v[1]
    out[1:2, :] = push_z * v[0] - push_x * v[2]
    out[2:3, :] = push_x * v[1] - push_y * v[0]


def scratch_plan():
    half = pltpu.VMEM((2, 2, 256, 256), BF16)
    sem = pltpu.SemaphoreType.DMA
    plan = {
        "dist": pltpu.VMEM((9, NX, NY, GRID), F32),
        "ids": pltpu.VMEM((NX, NY, GRID), jnp.int32),
        "load_sem": sem((2, 4)),
        "polar": pltpu.VMEM((6, NX, NY, GRID), F32),
        "moduli": pltpu.VMEM((2, NX, NY, GRID), F32),
        "tz": half,
        "ty": half,
        "tx": half,
        "txi": half,
        "tyi": half,
        "tzi": pltpu.VMEM((2, 256, 512), BF16),
        "table_sem": sem((6,)),
        "ox": pltpu.VMEM((2, 3, NY, GRID), F32),
        "oy": pltpu.VMEM((2, 3, NX, GRID), F32),
        "fx": pltpu.VMEM((2, 3, NY, GRID), F32),
        "fy": pltpu.VMEM((2, 3, NX, GRID), F32),
        "face_sem": sem((2, 4)),
        "hx": pltpu.VMEM((2, 3, NY, GRID), F32),
        "hy": pltpu.VMEM((2, 2, 3, 8, GRID), F32),
        "yface": pltpu.VMEM((2, 2, 3, 8, GRID), F32),
        "back_sem": sem((2, 6)),
        "base": pltpu.VMEM((3, 2, 256, 256), F32),
        "force": pltpu.VMEM((2, 512, 256), BF16),
        "swap": pltpu.VMEM((512, 128), F32),
        "yrows": pltpu.VMEM((2, 128, 256), F32),
        "xrows": half,
        "waves": pltpu.VMEM((2, 3, 256, 256), F32),
        "solved": pltpu.VMEM((2, 2, 3, 256, 256), BF16),
        "lines": pltpu.VMEM((256, 256), F32),
        "disp": pltpu.VMEM((3, NX, NY, GRID), F32),
        "grad": pltpu.VMEM((3, NX, NY, GRID), F32),
        "stress": pltpu.VMEM((6, NX, NY, GRID), F32),
        "store_sem": sem((2,)),
        "rows": pltpu.VMEM((2, 512, 1536), BF16),
        "asked": pltpu.VMEM((128, 128), jnp.int32),
        "slot": pltpu.VMEM((1, 512), F32),
        "reply": pltpu.VMEM((128, 128), F32),
    }
    exchanges = {
        "ex1": ("py", 6, (8, 8, 128), F32),
        "ex2": ("px", 6, (8, 512), F32),
        "ex3": ("px", 6, (8, 512), F32),
        "ex4": ("py", 6, (8, 8, 128), F32),
        "exa": ("py", 1, (NPX, 128), jnp.int32),
        "exb": ("px", 1, (NPY, 128), jnp.int32),
        "exc": ("px", 1, (NPY, 128), F32),
        "exd": ("py", 1, (NPX, 128), F32),
    }
    return plan, exchanges


class Names:
    pass


def whole_body(*refs):
    plan, exchanges = scratch_plan()
    n_in, n_out = 18, 2
    (
        moduli_in, source, tile, centre, burgers, line, sx, sy, sz, weights,
        dist_h, ids_h, tz_h, ty_h, tx_h, txi_h, tyi_h, tzi_h,
    ) = refs[:n_in]
    stress_h, seg_force = refs[n_in : n_in + n_out]
    rest = list(refs[n_in + n_out :])
    r = Names()
    for name in plan:
        setattr(r, name, rest.pop(0))
    for name, (axis, _, _, _) in exchanges.items():
        setattr(r, name, Exchange(axis, rest.pop(0), rest.pop(0), rest.pop(0), rest.pop(0)))

    px, py = lax.axis_index("px"), lax.axis_index("py")
    greet(px, py)
    loads = []
    for g in range(4):
        here = pl.ds(g * 4, 4)
        loads.append(
            (
                pltpu.make_async_copy(dist_h.at[:, here], r.dist.at[:, here], r.load_sem.at[0, g]),
                pltpu.make_async_copy(ids_h.at[here], r.ids.at[here], r.load_sem.at[1, g]),
            )
        )
        for load in loads[-1]:
            load.start()
    pairs = ((tz_h, r.tz), (ty_h, r.ty), (tx_h, r.tx), (txi_h, r.txi), (tyi_h, r.tyi), (tzi_h, r.tzi))
    tables = [pltpu.make_async_copy(a, b, r.table_sem.at[i]) for i, (a, b) in enumerate(pairs)]
    for table in tables:
        table.start()

    slot = request_part(source, tile, centre, r.asked)
    r.slot[...] = slot
    for p in range(NPY):
        r.exa.wire[0, p] = r.asked[p * NPX : p * NPX + NPX, :]
    lookup = table_of(moduli_in)
    for g in range(4):
        for load in loads[g]:
            load.wait()
        polar_part(g * 4, 4, r.dist, r.ids, lookup, r.polar, r.moduli)
    for side in range(2):
        for k, comp in enumerate((0, 5, 4)):
            r.ox[side, k] = r.polar[comp, side * (NX - 1)]
        for k, comp in enumerate((5, 1, 3)):
            r.oy[side, k] = r.polar[comp, :, side * (NY - 1), :]

    left, right = lax.rem(px + NPX - 1, NPX), lax.rem(px + 1, NPX)
    down, up = lax.rem(py + NPY - 1, NPY), lax.rem(py + 1, NPY)
    sides = [(left, py), (right, py), (px, down), (px, up)]

    def face(src, dst, sems, to, k):
        return send(src, dst, (sems.at[0, k], sems.at[1, k]), sides[to])

    halo = [
        face(r.ox.at[0], r.fx.at[1], r.face_sem, 0, 1),
        face(r.ox.at[1], r.fx.at[0], r.face_sem, 1, 0),
        face(r.oy.at[0], r.fy.at[1], r.face_sem, 2, 3),
        face(r.oy.at[1], r.fy.at[0], r.face_sem, 3, 2),
    ]
    pl.semaphore_wait(pltpu.get_barrier_semaphore(), NPX + NPY - 2)
    for copy in halo:
        copy.start()
    r.exa.start(0)
    tables[0].wait()

    def local(c, carry):
        forward_z_local(c, r.polar, r.tz, r.base, r.force)
        return carry

    lax.fori_loop(0, 3, local, 0)
    for copy in halo:
        copy.wait_recv()

    def step_z(j, carry):
        c, xh = j // 2, lax.rem(j, 2)
        forward_z(c, xh, r.polar, (r.fx, r.fy), r.tz, r.base, r.ex1.wire, r.force, r.swap)
        r.ex1.start(j)
        return carry

    lax.fori_loop(0, 6, step_z, 0)
    tables[1].wait()

    def step_y(j, carry):
        r.ex1.arrive(j)
        forward_y(j, r.ex1.got, r.ty, r.ex2.wire, r.yrows)
        r.ex2.start(j)
        return carry

    lax.fori_loop(0, 6, step_y, 0)
    r.exa.arrive(0)
    r.asked[...] = r.exa.got[0].reshape(128, 128)
    for p in range(NPX):
        r.exb.wire[0, p] = r.asked[pl.ds(p, NPY, stride=NPX), :]
    tables[2].wait()

    def step_x(c, carry):
        r.ex2.arrive(2 * c)
        r.ex2.arrive(2 * c + 1)
        forward_x(c, r.ex2.got, r.tx, r.waves, r.xrows)
        return carry

    lax.fori_loop(0, 3, step_x, 0)
    solve(r.waves, r.solved, sx, sy, sz, py, px)
    tables[3].wait()

    def step_xi(c, carry):
        inverse_x(c, r.solved, r.txi, r.ex3.wire)
        r.ex3.start(2 * c)
        return carry

    lax.fori_loop(0, 3, step_xi, 0)
    for c in range(3):
        r.ex3.start(2 * c + 1)
    r.exb.start(0)
    tables[4].wait()

    def step_yi(j, carry):
        part = lax.rem(j, 3) * 2 + j // 3
        r.ex3.arrive(part)
        inverse_y(part, r.ex3.got, r.tyi, r.ex4.wire)
        r.ex4.start(part)
        return carry

    lax.fori_loop(0, 6, step_yi, 0)
    r.exb.arrive(0)
    for p in range(NPX):
        r.asked[p * NPY : p * NPY + NPY, :] = r.exb.got[0, p]
    tables[5].wait()

    def back_half(xh):
        def step_zi(c, carry):
            r.ex4.arrive(c * 2 + xh)
            inverse_z(c, xh, r.ex4.got, r.tzi, r.disp, r.grad, r.yface, r.lines, r.swap)
            return carry

        lax.fori_loop(0, 3, step_zi, 0)
        x_side = NX - 1 if xh else 0
        copies = [
            face(r.disp.at[:, x_side], r.hx.at[1 - xh], r.back_sem, xh, 3 * xh),
            face(r.yface.at[xh, 0], r.hy.at[xh, 1], r.back_sem, 2, 3 * xh + 1),
            face(r.yface.at[xh, 1], r.hy.at[xh, 0], r.back_sem, 3, 3 * xh + 2),
        ]
        for copy in copies:
            copy.start()
        return copies

    def store(xh):
        here = pl.ds(xh * 8, 8)
        return pltpu.make_async_copy(r.stress.at[:, here], stress_h.at[:, here], r.store_sem.at[xh])

    def stress(first, count):
        stress_part(
            first, count, r.disp, r.grad, r.hx, r.hy, r.polar, r.moduli, r.stress, r.rows
        )

    backs = back_half(0)
    for copy in backs[1:]:
        copy.wait_recv()
    stress(1, 6)
    backs += back_half(1)
    stress(7, 1)
    backs[3].wait_recv()
    stress(0, 1)
    store(0).start()
    reply_part(0, r.asked, weights, r.rows, r.reply)
    backs[0].wait_recv()
    for copy in backs[4:]:
        copy.wait_recv()
    stress(8, 7)
    stress(15, 1)
    store(1).start()
    reply_part(1, r.asked, weights, r.rows, r.reply)
    for p in range(NPX):
        r.exc.wire[0, p] = r.reply[p * NPY : p * NPY + NPY, :]
    r.exc.start(0)
    for copy in halo + backs:
        copy.wait_send()
    for part in range(6):
        for ex in (r.ex1, r.ex2, r.ex3, r.ex4):
            ex.finish(part)
    r.exa.finish(0)
    r.exb.finish(0)
    r.exc.arrive(0)
    r.reply[...] = r.exc.got[0].reshape(128, 128)
    for p in range(NPY):
        r.exd.wire[0, p] = r.reply[pl.ds(p, NPX, stride=NPY), :]
    r.exd.start(0)
    store(0).wait()
    store(1).wait()
    r.exd.arrive(0)
    force_part(r.exd.got[0].reshape(128, 128), source, r.slot, burgers, line, seg_force)
    r.exc.finish(0)
    r.exd.finish(0)


def shards(dist, ids, moduli, seg_source, seg_tile, seg_center, burgers, line_vector):
    fwd_z, inv_z = z_tables()
    fwd_h, inv_h = half_tables()
    tz, tzi = two_parts(fwd_z), two_parts(inv_z)
    tx, txi = two_parts(fwd_h), two_parts(inv_h)
    ty = two_parts(fwd_h.transpose(0, 2, 1))
    tyi = two_parts(inv_h.transpose(0, 2, 1))
    sx, sy, sz = wave_lines()
    weights = two_parts(tile_weights())
    plan, exchanges = scratch_plan()
    scratch = list(plan.values())
    for axis, parts, block, dtype in exchanges.values():
        scratch += exchange_scratch(axis, parts, block, dtype)
    hbm = pl.BlockSpec(memory_space=pl.ANY)
    return tuple(
        pl.pallas_call(
            whole_body,
            out_shape=(sds((6, NX, NY, GRID)), sds((3, 512))),
            in_specs=[VM] * 10 + [hbm] * 8,
            out_specs=(hbm, VM),
            scratch_shapes=scratch,
            compiler_params=pltpu.CompilerParams(
                vmem_limit_bytes=VMEM_LIMIT, collective_id=0, has_side_effects=True
            ),
        )(
            moduli,
            seg_source.reshape(1, 512),
            seg_tile.reshape(1, 512),
            seg_center.reshape(1, 512),
            burgers,
            line_vector,
            sx,
            sy,
            sz,
            weights,
            dist,
            ids,
            tz,
            ty,
            tx,
            txi,
            tyi,
            tzi,
        )
    )


def solution(mesh):
    return jax.shard_map(
        shards,
        mesh=mesh,
        in_specs=(
            P(None, "px", "py", None),
            P("px", "py", None),
            P(),
            P(("px", "py"), None),
            P(("px", "py")),
            P(("px", "py")),
            P(None, ("px", "py")),
            P(None, ("px", "py")),
        ),
        out_specs=(P(None, "px", "py", None), P(None, ("px", "py"))),
        check_vma=False,
    )
```

time: 125 us -> 97.9 us (0.78)
  Pallas kernels: 122 us -> 92.6 us
  local copies, waits for them, and re-layouts: 2.84 us -> 4.58 us
    pallas_call x4 -> x1, Pallas kernels: 122 us -> 92.6 us  [shards(): pl.pallas_call(whole_body, out_shape=(sds((6, NX, NY, GRID)), sds((3, 512...]
    unnamed x2 -> x4, local copies, waits for them, and re-layouts: 2.84 us -> 4.58 us
where the time goes in v3:
time: 97.9 us; the launch traced here: 97.8 us
  Pallas kernels  92.6 us (95%)
  local copies, waits for them, and re-layouts  4.58 us (5%)
    pallas_call x1, Pallas kernels, shards(): pl.pallas_call(whole_body, out_shape=(sds((6, NX, NY, GRID)), sds((3, 512...  92.6 us
    unnamed x4, local copies, waits for them, and re-layouts  4.58 us

profile of v3, /device:TPU:1, one launch (start us, length us, event | category | flops | bytes accessed | tf_op | source)
XLA Modules:
  0.0 97.8 jit_solution(6967259301124676608)
XLA Ops:
  0.6 92.6 %shard_map.185 = (f32[6,16,32,256]{3,2,1,0:T(8,128)}, f32[3,512]{1,0:T(4,128)}) custom-call(f32[2,64]{1,0:T(2,128)} %refs_0_.1, s32[1,512]{1,0:T(1,128)} %bitcast.3, s32[1,512]{1,0:T(1,128)} %bitcast.4, s32[1,512]{1,0:T(1,128)} %bitcast.5, f32[3,512]{1,0:T(4,128)} %refs_4_.1, f32[3,512]{1,0:T(4,128)} %refs_5_.1, f32[2,128,128]{2,1,0:T(8,128)} %constant.20.clone.refs_6_, ...), custom_call_target="tpu_custom_call" | custom-call | tf_op jit(solution)/shard_map/pallas_call | solution.py:747
  93.2 0.0 copy-start
  93.2 4.0 %copy.22 = f32[6,16,32,256]{3,2,1,0:T(8,128)} copy(f32[6,16,32,256]{3,2,1,0:T(8,128)} %get-tuple-element.4) | data formatting | bytes 6291456
  97.2 0.0 copy-done
  97.2 0.6 copy.23
Async XLA Ops:
  93.2 4.0 %copy-start = (f32[3,512]{1,0:T(4,128)S(1)}, f32[3,512]{1,0:T(4,128)}, u32[]{:S(2)}) copy-start(f32[3,512]{1,0:T(4,128)} %get-tuple-element.5) | copy-start | bytes 18436

commit v4 on v3

--- a/solution.py
+++ b/solution.py
@@ -17,6 +17,7 @@
 HALF = 128
 NPX = 16
 NPY = 8
+DEVICES = NPX * NPY
 NX = 16
 NY = 32
 VMEM_LIMIT = 60 * 1024 * 1024
@@ -35,8 +36,7 @@
     fwd = np.zeros((GRID, GRID))
     inv = np.zeros((GRID, GRID))
     for row in range(GRID):
-        p, kzlo, ri, kzhi = row // 32, (row // 8) % 4, (row // 4) % 2, row % 4
-        wave = 16 * p + 4 * kzhi + kzlo
+        wave, ri = row // 2, row % 2
         angle = 2 * np.pi * ((wave * z) % GRID) / GRID
         if wave == 0:
             line = np.ones(GRID) if ri == 0 else 1.0 - 2.0 * (z % 2)
@@ -59,6 +59,12 @@
         fwd.append(np.block([[cos, sin], [-sin, cos]]))
         inv.append(np.block([[cos.T, -sin.T], [sin.T, cos.T]]) / GRID)
     return np.stack(fwd), np.stack(inv)
+
+
+def x_order():
+    index = np.arange(HALF).reshape(8, 4, 4)
+    order = index.transpose(1, 0, 2).reshape(-1)
+    return np.concatenate([order, order + HALF])
 
 
 def sines():
@@ -128,14 +134,64 @@
     )
 
 
+def peers(px, py):
+    me = px * NPY + py
+    return [lax.rem(me + (53 * k) % DEVICES, DEVICES) for k in range(1, DEVICES)]
+
+
+def place(device):
+    return (device // NPY, lax.rem(device, NPY))
+
+
 def greet(px, py):
     barrier = pltpu.get_barrier_semaphore()
-    for d in range(1, NPY):
-        where = (px, lax.rem(py + d, NPY))
-        pl.semaphore_signal(barrier, inc=1, device_id=where, device_id_type=pl.DeviceIdType.MESH)
-    for d in range(1, NPX):
-        where = (lax.rem(px + d, NPX), py)
-        pl.semaphore_signal(barrier, inc=1, device_id=where, device_id_type=pl.DeviceIdType.MESH)
+    for peer in peers(px, py):
+        pl.semaphore_signal(
+            barrier, inc=1, device_id=place(peer), device_id_type=pl.DeviceIdType.MESH
+        )
+
+
+class Turn:
+    def __init__(self, wire, got, sems, own_sem):
+        self.wire, self.got, self.sems, self.own_sem = wire, got, sems, own_sem
+        self.px, self.py = lax.axis_index("px"), lax.axis_index("py")
+        self.me = self.px * NPY + self.py
+
+    def rows(self, ref, part, device):
+        return ref.at[part, pl.ds(pl.multiple_of(device * 8, 8), 8)]
+
+    def own(self, part):
+        return pltpu.make_async_copy(
+            self.rows(self.wire, part, self.me), self.rows(self.got, part, self.me), self.own_sem.at[part]
+        )
+
+    def start(self, part):
+        sems = (self.sems.at[0, part], self.sems.at[1, part])
+        for peer in peers(self.px, self.py):
+            send(
+                self.rows(self.wire, part, peer), self.rows(self.got, part, self.me), sems, place(peer)
+            ).start()
+        self.own(part).start()
+
+    def all(self, side, part):
+        block = self.got.at[part, pl.ds(0, 8 * DEVICES - 8)]
+        return pltpu.make_async_copy(block, block, self.sems.at[side, part])
+
+    def arrive(self, part):
+        self.own(part).wait()
+        self.all(1, part).wait()
+
+    def finish(self, part):
+        self.all(0, part).wait()
+
+
+def turn_scratch():
+    return [
+        pltpu.VMEM((3, 8 * DEVICES, 128), F32),
+        pltpu.VMEM((3, 8 * DEVICES, 128), F32),
+        pltpu.SemaphoreType.DMA((2, 3)),
+        pltpu.SemaphoreType.DMA((3,)),
+    ]
 
 
 class Exchange:
@@ -256,77 +312,55 @@
         hi, lo = split(polar[4 - c, x])
         force[0, x * NY : (x + 1) * NY, :] = hi
         force[1, x * NY : (x + 1) * NY, :] = lo
-    waves[c, 0] = dot3((tz[0, 1], tz[1, 1]), (force[0, :256], force[1, :256]), LAST)
-    waves[c, 1] = dot3((tz[0, 1], tz[1, 1]), (force[0, 256:], force[1, 256:]), LAST)
-
-
-def forward_z(c, xh, polar, faces, tz, base, wire, force, swap):
+    waves[c] = dot3((tz[0, 1], tz[1, 1]), (force[0], force[1]), LAST)
+
+
+def forward_z(c, polar, faces, tz, base, wire, force):
     cx = (6 - c) * ((c + 1) // 2)
     cy = 5 - c - 3 * lax.rem(c, 2)
-    part = c * 2 + xh
     fx, fy = faces
-    for i in range(8):
-        x = xh * 8 + i
-        after = polar[cx, lax.rem(x + 1, NX)]
-        before = polar[cx, lax.rem(x + NX - 1, NX)]
-        if i == 0:
-            before = jnp.where(xh == 0, fx[0, c], before)
-        if i == 7:
-            after = jnp.where(xh == 1, fx[1, c], after)
-        ends = [fy[side, c, pl.ds(pl.multiple_of(xh * 8, 8), 8), :] for side in range(2)]
-        grad_y = shift_y(polar[cy, x], ends[0][i : i + 1], ends[1][i : i + 1])
+    for x in range(NX):
+        after = fx[1, c] if x == NX - 1 else polar[cx, x + 1]
+        before = fx[0, c] if x == 0 else polar[cx, x - 1]
+        grad_y = shift_y(polar[cy, x], fy[0, c, x : x + 1, :], fy[1, c, x : x + 1, :])
         hi, lo = split((after - before) + grad_y)
-        force[0, i * NY : (i + 1) * NY, :] = hi
-        force[1, i * NY : (i + 1) * NY, :] = lo
-    waves = base[c, xh] + dot3((tz[0, 0], tz[1, 0]), (force[0, :256], force[1, :256]), LAST)
-    for p in range(NPY):
-        for xg in range(2):
-            tiles = [
-                waves[p * 32 + kzlo * 8 : p * 32 + kzlo * 8 + 8, xg * 128 : xg * 128 + 128]
-                for kzlo in range(4)
+        force[0, x * NY : (x + 1) * NY, :] = hi
+        force[1, x * NY : (x + 1) * NY, :] = lo
+    waves = base[c] + dot3((tz[0, 0], tz[1, 0]), (force[0], force[1]), LAST)
+    for t in range(32):
+        for xg in range(4):
+            wire[c, pl.ds(32 * t + xg, 8, stride=4), :] = waves[
+                8 * t : 8 * t + 8, xg * 128 : xg * 128 + 128
             ]
-            for x4, tile in enumerate(swap_groups(tiles)):
-                row = p * 64 + (xg * 4 + x4) * 8
-                swap[row : row + 8, :] = tile
-        for s in range(8):
-            wire[part, p, s] = swap[pl.ds(p * 64 + s, 8, stride=8), :]
-
-
-def forward_y(part, got, ty, wire, rows):
-    for ri in range(2):
-        for kzhi in range(4):
-            s = ri * 4 + kzhi
-            low = swap_groups([got[part, q, s] for q in range(4)])
-            high = swap_groups([got[part, q + 4, s] for q in range(4)])
-            for kzlo in range(4):
-                row = (kzhi * 4 + kzlo) * 8
-                rows[0, row : row + 8, ri * 128 : ri * 128 + 128] = low[kzlo] + high[kzlo]
-                rows[1, row : row + 8, ri * 128 : ri * 128 + 128] = low[kzlo] - high[kzlo]
+
+
+def forward_plane(c, got, ty, tx, waves, yrows, xrows):
+    for q in range(NPX):
+        row = q * 64
+        low = swap_groups([got[c, row + p * 8 : row + p * 8 + 8, :] for p in range(4)])
+        high = swap_groups([got[c, row + p * 8 : row + p * 8 + 8, :] for p in range(4, 8)])
+        for x4 in range(4):
+            to = pl.ds(q * 4 + x4, 8, stride=64)
+            yrows[0, to, :] = low[x4] + high[x4]
+            yrows[1, to, :] = low[x4] - high[x4]
     for e in range(2):
-        out = dot3(split(rows[e]), (ty[0, e], ty[1, e]))
-        for kz in range(NX):
-            wire[part, kz, :, e * 256 : e * 256 + 256] = out[kz * 8 : kz * 8 + 8, :]
-
-
-def forward_x(c, got, tx, waves, rows):
-    for q in range(8):
-        a = jnp.concatenate([got[2 * c, q], got[2 * c + 1, q]], axis=0)
-        b = jnp.concatenate([got[2 * c, q + 8], got[2 * c + 1, q + 8]], axis=0)
-        for ex in range(2):
-            hi, lo = split(a + b if ex == 0 else a - b)
-            for ri in range(2):
-                row = ri * 128 + q * 16
-                for e in range(2):
-                    lane = e * 256 + ri * 128
-                    rows[0, ex, row : row + 16, e * 128 : e * 128 + 128] = hi[:, lane : lane + 128]
-                    rows[1, ex, row : row + 16, e * 128 : e * 128 + 128] = lo[:, lane : lane + 128]
+        rows = jnp.concatenate([yrows[e, :256, :], yrows[e, 256:, :]], axis=1)
+        out = dot3(split(rows), (ty[0, e], ty[1, e]))
+        for xg in range(4):
+            a, b = out[xg * 64 : xg * 64 + 32, :], out[xg * 64 + 32 : xg * 64 + 64, :]
+            for ex in range(2):
+                hi, lo = split(a + b if ex == 0 else a - b)
+                for ri in range(2):
+                    to = slice(ri * 128 + xg * 32, ri * 128 + xg * 32 + 32)
+                    xrows[0, ex, to, e * 128 : e * 128 + 128] = hi[:, ri * 128 : ri * 128 + 128]
+                    xrows[1, ex, to, e * 128 : e * 128 + 128] = lo[:, ri * 128 : ri * 128 + 128]
     for ex in range(2):
-        waves[ex, c] = dot3((tx[0, ex], tx[1, ex]), (rows[0, ex], rows[1, ex]))
-
-
-def solve(waves, solved, sx, sy, sz, py, px):
+        waves[ex, c] = dot3((tx[0, ex], tx[1, ex]), (xrows[0, ex], xrows[1, ex]))
+
+
+def solve(waves, solved, sx, sy, sz, kz):
     sy = sy[...]
-    sz = sz[pl.ds(py * 16 + px, 1), :]
+    sz = sz[pl.ds(kz, 1), :]
     sz = jnp.concatenate([sz, sz], axis=1)
     coupling = (REF_LAMBDA + REF_SHEAR) / (REF_LAMBDA + 2.0 * REF_SHEAR)
     rest = sy * sy + sz * sz
@@ -345,70 +379,57 @@
                 solved[1, ex, c, ri * 128 : ri * 128 + 128, :] = lo
 
 
-def inverse_x(c, solved, txi, wire):
+def inverse_plane(c, solved, txi, tyi, wire, yrows):
     backs = [dot3((txi[0, ex], txi[1, ex]), (solved[0, ex, c], solved[1, ex, c])) for ex in range(2)]
-    for half, out in enumerate((backs[0] + backs[1], backs[0] - backs[1])):
-        for q in range(8):
-            for xh in range(2):
-                for ri in range(2):
-                    row = ri * 128 + q * 16 + xh * 8
-                    for e in range(2):
-                        lane = e * 256 + ri * 128
-                        wire[2 * c + xh, half * 8 + q, :, lane : lane + 128] = out[
-                            row : row + 8, e * 128 : e * 128 + 128
-                        ]
-
-
-def inverse_y(part, got, tyi, wire):
+    halves = (backs[0] + backs[1], backs[0] - backs[1])
     outs = []
     for e in range(2):
-        rows = jnp.concatenate([got[part, kz, :, e * 256 : e * 256 + 256] for kz in range(NX)], axis=0)
-        outs.append(dot3(split(rows), (tyi[0, e], tyi[1, e])))
+        lane = slice(e * 128, e * 128 + 128)
+        sides = []
+        for ri in range(2):
+            blocks = []
+            for xg in range(4):
+                row = ri * 128 + xg * 32
+                blocks += [halves[0][row : row + 32, lane], halves[1][row : row + 32, lane]]
+            sides.append(jnp.concatenate(blocks, axis=0))
+        outs.append(dot3(split(jnp.concatenate(sides, axis=1)), (tyi[0, e], tyi[1, e])))
     for half, out in enumerate((outs[0] + outs[1], outs[0] - outs[1])):
-        for ri in range(2):
-            for kzhi in range(4):
-                tiles = [
-                    out[(kzhi * 4 + k) * 8 : (kzhi * 4 + k + 1) * 8, ri * 128 : ri * 128 + 128]
-                    for k in range(4)
-                ]
-                for q4, tile in enumerate(swap_groups(tiles)):
-                    wire[part, half * 4 + q4, ri * 4 + kzhi] = tile
-
-
-def inverse_z(c, xh, got, tzi, disp, grad, yface, waves, swap):
-    part = c * 2 + xh
-    for p in range(NPY):
-        for s in range(8):
-            swap[p * 64 + s * 8 : p * 64 + s * 8 + 8, :] = got[part, p, s]
-        for xg in range(2):
-            tiles = [swap[pl.ds(p * 64 + xg * 4 + x4, 8, stride=8), :] for x4 in range(4)]
-            for kzlo, tile in enumerate(swap_groups(tiles)):
-                row = p * 32 + kzlo * 8
-                waves[row : row + 8, xg * 128 : xg * 128 + 128] = tile
-    turned = split(jnp.transpose(waves[...]))
-    out = dot3(turned, (tzi[0, :, :256], tzi[1, :, :256]))
-    for i in range(8):
-        x = xh * 8 + i
-        disp[c, x] = out[i * NY : (i + 1) * NY, :]
-        yface[xh, 0, c, i : i + 1] = out[i * NY : i * NY + 1, :]
-        yface[xh, 1, c, i : i + 1] = out[i * NY + NY - 1 : i * NY + NY, :]
-    out = dot3(turned, (tzi[0, :, 256:], tzi[1, :, 256:]))
-    for i in range(8):
-        grad[c, xh * 8 + i] = out[i * NY : (i + 1) * NY, :]
+        yrows[half, :256, :] = out[:, :128]
+        yrows[half, 256:, :] = out[:, 128:]
+    for q in range(NPX):
+        for half in range(2):
+            tiles = [yrows[half, pl.ds(q * 4 + x4, 8, stride=64), :] for x4 in range(4)]
+            for p, tile in enumerate(swap_groups(tiles)):
+                row = q * 64 + half * 32 + p * 8
+                wire[c, row : row + 8, :] = tile
+
+
+def inverse_z(c, got, tzi, disp, grad, yface, lines):
+    for xg in range(4):
+        turned = jnp.transpose(got[c, pl.ds(xg, 256, stride=4), :])
+        hi, lo = split(turned)
+        lines[0, xg * 128 : xg * 128 + 128, :] = hi
+        lines[1, xg * 128 : xg * 128 + 128, :] = lo
+    pair = (lines[0], lines[1])
+    out = dot3(pair, (tzi[0, :, :256], tzi[1, :, :256]))
+    for x in range(NX):
+        disp[c, x] = out[x * NY : (x + 1) * NY, :]
+        yface[0, c, x : x + 1] = out[x * NY : x * NY + 1, :]
+        yface[1, c, x : x + 1] = out[x * NY + NY - 1 : x * NY + NY, :]
+    out = dot3(pair, (tzi[0, :, 256:], tzi[1, :, 256:]))
+    for x in range(NX):
+        grad[c, x] = out[x * NY : (x + 1) * NY, :]
 
 
 def stress_part(first, count, disp, grad, hx, hy, polar, moduli, stress, rows):
-    xh = first // 8
-
     def at_x(x, carry):
         lame, shear = moduli[0, x], moduli[1, x]
         gx, gy, gz = [], [], []
-        i = x - xh * 8
         for c in range(3):
             after = hx[1, c] if first == NX - 1 else disp[c, x + 1]
             before = hx[0, c] if first == 0 else disp[c, x - 1]
             gx.append(after - before)
-            gy.append(shift_y(disp[c, x], hy[xh, 0, c, pl.ds(i, 1), :], hy[xh, 1, c, pl.ds(i, 1), :]))
+            gy.append(shift_y(disp[c, x], hy[0, c, pl.ds(x, 1), :], hy[1, c, pl.ds(x, 1), :]))
             gz.append(grad[c, x])
         trace = (0.5 * lame) * (gx[0] + gy[1] + gz[2])
         half = 0.5 * shear
@@ -432,24 +453,23 @@
     lax.fori_loop(first, first + count, at_x, 0)
 
 
-def reply_part(xh, asked, weights, rows, reply):
-    column = lax.broadcasted_iota(jnp.int32, (128, 256), 1) + xh * 256
+def reply_part(asked, weights, rows, reply):
+    column = lax.broadcasted_iota(jnp.int32, (128, 512), 1)
     lane = lax.broadcasted_iota(jnp.int32, (128, 128), 1)
     lane256 = lax.broadcasted_iota(jnp.int32, (128, 256), 1)
-    out = reply[...] if xh else jnp.zeros((128, 128), F32)
+    out = jnp.zeros((128, 128), F32)
     wh, wl = weights[0], weights[1]
     for k in range(8):
         tile = asked[:, k : k + 1]
         centre = asked[:, 8 + k : 9 + k]
         pick = (column == tile // 2).astype(F32).astype(BF16)
-        here = slice(xh * 256, xh * 256 + 256)
-        picked = dot(pick, rows[0, here, :]) + dot(pick, rows[1, here, :])
+        picked = dot(pick, rows[0]) + dot(pick, rows[1])
         at = (lane == centre).astype(F32).astype(BF16)
         row = dot(at, wh) + dot(at, wl)
         weight = jnp.where(lane256 // 128 == tile % 2, jnp.concatenate([row, row], axis=1), 0.0)
         for c in range(6):
             value = jnp.sum(picked[:, c * 256 : c * 256 + 256] * weight, axis=1, keepdims=True)
-            out = out + jnp.where(lane == c * 8 + k, value, 0.0)
+            out = jnp.where(lane == c * 8 + k, value, out)
     reply[...] = out
 
 
@@ -495,31 +515,26 @@
         "fy": pltpu.VMEM((2, 3, NX, GRID), F32),
         "face_sem": sem((2, 4)),
         "hx": pltpu.VMEM((2, 3, NY, GRID), F32),
-        "hy": pltpu.VMEM((2, 2, 3, 8, GRID), F32),
-        "yface": pltpu.VMEM((2, 2, 3, 8, GRID), F32),
-        "back_sem": sem((2, 6)),
-        "base": pltpu.VMEM((3, 2, 256, 256), F32),
+        "hy": pltpu.VMEM((2, 3, NX, GRID), F32),
+        "yface": pltpu.VMEM((2, 3, NX, GRID), F32),
+        "back_sem": sem((3, 2, 4)),
+        "base": pltpu.VMEM((3, 256, 512), F32),
         "force": pltpu.VMEM((2, 512, 256), BF16),
-        "swap": pltpu.VMEM((512, 128), F32),
-        "yrows": pltpu.VMEM((2, 128, 256), F32),
+        "yrows": pltpu.VMEM((2, 512, 128), F32),
         "xrows": half,
         "waves": pltpu.VMEM((2, 3, 256, 256), F32),
         "solved": pltpu.VMEM((2, 2, 3, 256, 256), BF16),
-        "lines": pltpu.VMEM((256, 256), F32),
+        "lines": pltpu.VMEM((2, 512, 256), BF16),
         "disp": pltpu.VMEM((3, NX, NY, GRID), F32),
         "grad": pltpu.VMEM((3, NX, NY, GRID), F32),
         "stress": pltpu.VMEM((6, NX, NY, GRID), F32),
-        "store_sem": sem((2,)),
+        "store_sem": sem((1,)),
         "rows": pltpu.VMEM((2, 512, 1536), BF16),
         "asked": pltpu.VMEM((128, 128), jnp.int32),
         "slot": pltpu.VMEM((1, 512), F32),
         "reply": pltpu.VMEM((128, 128), F32),
     }
     exchanges = {
-        "ex1": ("py", 6, (8, 8, 128), F32),
-        "ex2": ("px", 6, (8, 512), F32),
-        "ex3": ("px", 6, (8, 512), F32),
-        "ex4": ("py", 6, (8, 8, 128), F32),
         "exa": ("py", 1, (NPX, 128), jnp.int32),
         "exb": ("px", 1, (NPY, 128), jnp.int32),
         "exc": ("px", 1, (NPY, 128), F32),
@@ -546,6 +561,9 @@
         setattr(r, name, rest.pop(0))
     for name, (axis, _, _, _) in exchanges.items():
         setattr(r, name, Exchange(axis, rest.pop(0), rest.pop(0), rest.pop(0), rest.pop(0)))
+
+    r.there = Turn(rest.pop(0), rest.pop(0), rest.pop(0), rest.pop(0))
+    r.back = Turn(rest.pop(0), rest.pop(0), rest.pop(0), rest.pop(0))
 
     px, py = lax.axis_index("px"), lax.axis_index("py")
     greet(px, py)
@@ -593,7 +611,7 @@
         face(r.oy.at[0], r.fy.at[1], r.face_sem, 2, 3),
         face(r.oy.at[1], r.fy.at[0], r.face_sem, 3, 2),
     ]
-    pl.semaphore_wait(pltpu.get_barrier_semaphore(), NPX + NPY - 2)
+    pl.semaphore_wait(pltpu.get_barrier_semaphore(), DEVICES - 1)
     for copy in halo:
         copy.start()
     r.exa.start(0)
@@ -607,113 +625,72 @@
     for copy in halo:
         copy.wait_recv()
 
-    def step_z(j, carry):
-        c, xh = j // 2, lax.rem(j, 2)
-        forward_z(c, xh, r.polar, (r.fx, r.fy), r.tz, r.base, r.ex1.wire, r.force, r.swap)
-        r.ex1.start(j)
-        return carry
-
-    lax.fori_loop(0, 6, step_z, 0)
-    tables[1].wait()
-
-    def step_y(j, carry):
-        r.ex1.arrive(j)
-        forward_y(j, r.ex1.got, r.ty, r.ex2.wire, r.yrows)
-        r.ex2.start(j)
-        return carry
-
-    lax.fori_loop(0, 6, step_y, 0)
+    for c in range(3):
+        forward_z(c, r.polar, (r.fx, r.fy), r.tz, r.base, r.there.wire, r.force)
+        r.there.start(c)
     r.exa.arrive(0)
     r.asked[...] = r.exa.got[0].reshape(128, 128)
     for p in range(NPX):
         r.exb.wire[0, p] = r.asked[pl.ds(p, NPY, stride=NPX), :]
+    tables[1].wait()
     tables[2].wait()
 
-    def step_x(c, carry):
-        r.ex2.arrive(2 * c)
-        r.ex2.arrive(2 * c + 1)
-        forward_x(c, r.ex2.got, r.tx, r.waves, r.xrows)
+    def step_plane(c, carry):
+        r.there.arrive(c)
+        forward_plane(c, r.there.got, r.ty, r.tx, r.waves, r.yrows, r.xrows)
         return carry
 
-    lax.fori_loop(0, 3, step_x, 0)
-    solve(r.waves, r.solved, sx, sy, sz, py, px)
+    lax.fori_loop(0, 3, step_plane, 0)
+    solve(r.waves, r.solved, sx, sy, sz, px * NPY + py)
     tables[3].wait()
-
-    def step_xi(c, carry):
-        inverse_x(c, r.solved, r.txi, r.ex3.wire)
-        r.ex3.start(2 * c)
+    tables[4].wait()
+
+    def step_back(c, carry):
+        inverse_plane(c, r.solved, r.txi, r.tyi, r.back.wire, r.yrows)
+        r.back.start(c)
         return carry
 
-    lax.fori_loop(0, 3, step_xi, 0)
-    for c in range(3):
-        r.ex3.start(2 * c + 1)
+    lax.fori_loop(0, 3, step_back, 0)
     r.exb.start(0)
-    tables[4].wait()
-
-    def step_yi(j, carry):
-        part = lax.rem(j, 3) * 2 + j // 3
-        r.ex3.arrive(part)
-        inverse_y(part, r.ex3.got, r.tyi, r.ex4.wire)
-        r.ex4.start(part)
-        return carry
-
-    lax.fori_loop(0, 6, step_yi, 0)
+    tables[5].wait()
     r.exb.arrive(0)
     for p in range(NPX):
         r.asked[p * NPY : p * NPY + NPY, :] = r.exb.got[0, p]
-    tables[5].wait()
-
-    def back_half(xh):
-        def step_zi(c, carry):
-            r.ex4.arrive(c * 2 + xh)
-            inverse_z(c, xh, r.ex4.got, r.tzi, r.disp, r.grad, r.yface, r.lines, r.swap)
-            return carry
-
-        lax.fori_loop(0, 3, step_zi, 0)
-        x_side = NX - 1 if xh else 0
-        copies = [
-            face(r.disp.at[:, x_side], r.hx.at[1 - xh], r.back_sem, xh, 3 * xh),
-            face(r.yface.at[xh, 0], r.hy.at[xh, 1], r.back_sem, 2, 3 * xh + 1),
-            face(r.yface.at[xh, 1], r.hy.at[xh, 0], r.back_sem, 3, 3 * xh + 2),
+
+    def faces_back(c):
+        sems = r.back_sem.at[c]
+        return [
+            face(r.disp.at[c, 0], r.hx.at[1, c], sems, 0, 1),
+            face(r.disp.at[c, NX - 1], r.hx.at[0, c], sems, 1, 0),
+            face(r.yface.at[0, c], r.hy.at[1, c], sems, 2, 3),
+            face(r.yface.at[1, c], r.hy.at[0, c], sems, 3, 2),
         ]
-        for copy in copies:
+
+    backs = []
+    for c in range(3):
+        r.back.arrive(c)
+        inverse_z(c, r.back.got, r.tzi, r.disp, r.grad, r.yface, r.lines)
+        backs += faces_back(c)
+        for copy in backs[4 * c :]:
             copy.start()
-        return copies
-
-    def store(xh):
-        here = pl.ds(xh * 8, 8)
-        return pltpu.make_async_copy(r.stress.at[:, here], stress_h.at[:, here], r.store_sem.at[xh])
-
-    def stress(first, count):
+
+    for copy in backs:
+        copy.wait_recv()
+    for first, count in ((0, 1), (1, 14), (15, 1)):
         stress_part(
             first, count, r.disp, r.grad, r.hx, r.hy, r.polar, r.moduli, r.stress, r.rows
         )
-
-    backs = back_half(0)
-    for copy in backs[1:]:
-        copy.wait_recv()
-    stress(1, 6)
-    backs += back_half(1)
-    stress(7, 1)
-    backs[3].wait_recv()
-    stress(0, 1)
-    store(0).start()
-    reply_part(0, r.asked, weights, r.rows, r.reply)
-    backs[0].wait_recv()
-    for copy in backs[4:]:
-        copy.wait_recv()
-    stress(8, 7)
-    stress(15, 1)
-    store(1).start()
-    reply_part(1, r.asked, weights, r.rows, r.reply)
+    store = pltpu.make_async_copy(r.stress, stress_h, r.store_sem.at[0])
+    store.start()
+    reply_part(r.asked, weights, r.rows, r.reply)
     for p in range(NPX):
         r.exc.wire[0, p] = r.reply[p * NPY : p * NPY + NPY, :]
     r.exc.start(0)
     for copy in halo + backs:
         copy.wait_send()
-    for part in range(6):
-        for ex in (r.ex1, r.ex2, r.ex3, r.ex4):
-            ex.finish(part)
+    for c in range(3):
+        r.there.finish(c)
+        r.back.finish(c)
     r.exa.finish(0)
     r.exb.finish(0)
     r.exc.arrive(0)
@@ -721,8 +698,7 @@
     for p in range(NPY):
         r.exd.wire[0, p] = r.reply[pl.ds(p, NPX, stride=NPY), :]
     r.exd.start(0)
-    store(0).wait()
-    store(1).wait()
+    store.wait()
     r.exd.arrive(0)
     force_part(r.exd.got[0].reshape(128, 128), source, r.slot, burgers, line, seg_force)
     r.exc.finish(0)
@@ -732,8 +708,9 @@
 def shards(dist, ids, moduli, seg_source, seg_tile, seg_center, burgers, line_vector):
     fwd_z, inv_z = z_tables()
     fwd_h, inv_h = half_tables()
+    order = x_order()
     tz, tzi = two_parts(fwd_z), two_parts(inv_z)
-    tx, txi = two_parts(fwd_h), two_parts(inv_h)
+    tx, txi = two_parts(fwd_h[:, :, order]), two_parts(inv_h[:, order, :])
     ty = two_parts(fwd_h.transpose(0, 2, 1))
     tyi = two_parts(inv_h.transpose(0, 2, 1))
     sx, sy, sz = wave_lines()
@@ -742,6 +719,7 @@
     scratch = list(plan.values())
     for axis, parts, block, dtype in exchanges.values():
         scratch += exchange_scratch(axis, parts, block, dtype)
+    scratch += turn_scratch() + turn_scratch()
     hbm = pl.BlockSpec(memory_space=pl.ANY)
     return tuple(
         pl.pallas_call(

time: 97.9 us -> 90.5 us (0.924)
  Pallas kernels: 92.6 us -> 85.1 us
    pallas_call x1, Pallas kernels: 92.6 us -> 85.1 us  [shards(): pl.pallas_call(whole_body, out_shape=(sds((6, NX, NY, GRID)), sds((3, 512...]
where the time goes in v4:
time: 90.5 us; the launch traced here: 90.3 us
  Pallas kernels  85.1 us (94%)
  local copies, waits for them, and re-layouts  4.58 us (5%)
    pallas_call x1, Pallas kernels, shards(): pl.pallas_call(whole_body, out_shape=(sds((6, NX, NY, GRID)), sds((3, 512...  85.1 us
    unnamed x4, local copies, waits for them, and re-layouts  4.58 us

profile of v4, /device:TPU:1, one launch (start us, length us, event | category | flops | bytes accessed | tf_op | source)
XLA Modules:
  0.0 90.3 jit_solution(14996766809425162354)
XLA Ops:
  0.6 85.1 %shard_map.185 = (f32[6,16,32,256]{3,2,1,0:T(8,128)}, f32[3,512]{1,0:T(4,128)}) custom-call(f32[2,64]{1,0:T(2,128)} %refs_0_.1, s32[1,512]{1,0:T(1,128)} %bitcast.3, s32[1,512]{1,0:T(1,128)} %bitcast.4, s32[1,512]{1,0:T(1,128)} %bitcast.5, f32[3,512]{1,0:T(4,128)} %refs_4_.1, f32[3,512]{1,0:T(4,128)} %refs_5_.1, f32[2,128,128]{2,1,0:T(8,128)} %constant.20.clone.refs_6_, ...), custom_call_target="tpu_custom_call" | custom-call | tf_op jit(solution)/shard_map/pallas_call | solution.py:725
  85.7 0.0 copy-start
  85.7 4.0 %copy.22 = f32[6,16,32,256]{3,2,1,0:T(8,128)} copy(f32[6,16,32,256]{3,2,1,0:T(8,128)} %get-tuple-element.4) | data formatting | bytes 6291456
  89.7 0.0 copy-done
  89.7 0.6 copy.23
Async XLA Ops:
  85.7 4.0 %copy-start = (f32[3,512]{1,0:T(4,128)S(1)}, f32[3,512]{1,0:T(4,128)}, u32[]{:S(2)}) copy-start(f32[3,512]{1,0:T(4,128)} %get-tuple-element.5) | copy-start | bytes 18436

commit v5 on v4

--- a/solution.py
+++ b/solution.py
@@ -145,10 +145,18 @@
 
 def greet(px, py):
     barrier = pltpu.get_barrier_semaphore()
-    for peer in peers(px, py):
-        pl.semaphore_signal(
-            barrier, inc=1, device_id=place(peer), device_id_type=pl.DeviceIdType.MESH
-        )
+    for d in range(1, NPY):
+        where = (px, lax.rem(py + d, NPY))
+        pl.semaphore_signal(barrier, inc=1, device_id=where, device_id_type=pl.DeviceIdType.MESH)
+    for d in range(1, NPX):
+        where = (lax.rem(px + d, NPX), py)
+        pl.semaphore_signal(barrier, inc=1, device_id=where, device_id_type=pl.DeviceIdType.MESH)
+
+
+def greet_on(inside, px, py):
+    for d in range(1, NPX):
+        where = (lax.rem(px + d, NPX), py)
+        pl.semaphore_signal(inside, inc=1, device_id=where, device_id_type=pl.DeviceIdType.MESH)
 
 
 class Turn:
@@ -404,19 +412,21 @@
                 wire[c, row : row + 8, :] = tile
 
 
-def inverse_z(c, got, tzi, disp, grad, yface, lines):
+def inverse_z(c, got, tzi, disp, yface, lines):
     for xg in range(4):
         turned = jnp.transpose(got[c, pl.ds(xg, 256, stride=4), :])
         hi, lo = split(turned)
         lines[0, xg * 128 : xg * 128 + 128, :] = hi
         lines[1, xg * 128 : xg * 128 + 128, :] = lo
-    pair = (lines[0], lines[1])
-    out = dot3(pair, (tzi[0, :, :256], tzi[1, :, :256]))
+    out = dot3((lines[0], lines[1]), (tzi[0, :, :256], tzi[1, :, :256]))
     for x in range(NX):
         disp[c, x] = out[x * NY : (x + 1) * NY, :]
         yface[0, c, x : x + 1] = out[x * NY : x * NY + 1, :]
         yface[1, c, x : x + 1] = out[x * NY + NY - 1 : x * NY + NY, :]
-    out = dot3(pair, (tzi[0, :, 256:], tzi[1, :, 256:]))
+
+
+def inverse_z_grad(c, tzi, grad, lines):
+    out = dot3((lines[0], lines[1]), (tzi[0, :, 256:], tzi[1, :, 256:]))
     for x in range(NX):
         grad[c, x] = out[x * NY : (x + 1) * NY, :]
 
@@ -453,35 +463,41 @@
     lax.fori_loop(first, first + count, at_x, 0)
 
 
-def reply_part(asked, weights, rows, reply):
+def pick_part(asked, weights, pick, gain):
     column = lax.broadcasted_iota(jnp.int32, (128, 512), 1)
     lane = lax.broadcasted_iota(jnp.int32, (128, 128), 1)
     lane256 = lax.broadcasted_iota(jnp.int32, (128, 256), 1)
-    out = jnp.zeros((128, 128), F32)
-    wh, wl = weights[0], weights[1]
     for k in range(8):
+        here = slice(k * 128, k * 128 + 128)
         tile = asked[:, k : k + 1]
         centre = asked[:, 8 + k : 9 + k]
-        pick = (column == tile // 2).astype(F32).astype(BF16)
-        picked = dot(pick, rows[0]) + dot(pick, rows[1])
+        pick[here, :] = (column == tile // 2).astype(F32).astype(BF16)
         at = (lane == centre).astype(F32).astype(BF16)
-        row = dot(at, wh) + dot(at, wl)
-        weight = jnp.where(lane256 // 128 == tile % 2, jnp.concatenate([row, row], axis=1), 0.0)
-        for c in range(6):
-            value = jnp.sum(picked[:, c * 256 : c * 256 + 256] * weight, axis=1, keepdims=True)
-            out = jnp.where(lane == c * 8 + k, value, out)
+        row = dot(at, weights[0]) + dot(at, weights[1])
+        row = jnp.concatenate([row, row], axis=1)
+        gain[here, :] = jnp.where(lane256 // 128 == tile % 2, row, 0.0)
+
+
+def reply_part(pick, gain, rows, reply):
+    lane = lax.broadcasted_iota(jnp.int32, (128, 128), 1)
+    out = jnp.zeros((128, 128), F32)
+    for c in range(6):
+        here = slice(c * 256, c * 256 + 256)
+        picked = dot(pick[...], rows[0, :, here]) + dot(pick[...], rows[1, :, here])
+        picked = picked * gain[...]
+        total = jnp.sum(picked[:, :128] + picked[:, 128:], axis=1, keepdims=True)
+        for k in range(8):
+            out = jnp.where(lane == c * 8 + k, total[k * 128 : k * 128 + 128], out)
     reply[...] = out
 
 
-def force_part(reply, source, slot, burgers, line, out):
-    match = lax.broadcasted_iota(jnp.int32, (128, 512), 0) == row_of(source[...])
-    match = match.astype(F32).astype(BF16)
+def force_part(reply, match, mine, burgers, line, out):
     hi, lo = split(reply)
     low = (reply - hi.astype(F32) - lo.astype(F32)).astype(BF16)
     first = ((0,), (0,))
+    match = match[...]
     got = dot(hi, match, first) + (dot(lo, match, first) + dot(low, match, first))
-    lane = lax.broadcasted_iota(jnp.int32, (128, 512), 0)
-    mine = jnp.where((lane % 8).astype(F32) == slot[...], got, 0.0)
+    mine = got * mine[...]
     t = [jnp.sum(mine[c * 8 : c * 8 + 8, :], axis=0, keepdims=True) for c in range(6)]
     b = [burgers[i : i + 1, :] for i in range(3)]
     v = [line[i : i + 1, :] for i in range(3)]
@@ -497,6 +513,7 @@
     half = pltpu.VMEM((2, 2, 256, 256), BF16)
     sem = pltpu.SemaphoreType.DMA
     plan = {
+        "inside": pltpu.SemaphoreType.REGULAR,
         "dist": pltpu.VMEM((9, NX, NY, GRID), F32),
         "ids": pltpu.VMEM((NX, NY, GRID), jnp.int32),
         "load_sem": sem((2, 4)),
@@ -531,8 +548,12 @@
         "store_sem": sem((1,)),
         "rows": pltpu.VMEM((2, 512, 1536), BF16),
         "asked": pltpu.VMEM((128, 128), jnp.int32),
+        "pick": pltpu.VMEM((1024, 512), BF16),
+        "gain": pltpu.VMEM((1024, 256), F32),
         "slot": pltpu.VMEM((1, 512), F32),
         "reply": pltpu.VMEM((128, 128), F32),
+        "match": pltpu.VMEM((128, 512), BF16),
+        "mine": pltpu.VMEM((128, 512), F32),
     }
     exchanges = {
         "exa": ("py", 1, (NPX, 128), jnp.int32),
@@ -566,7 +587,6 @@
     r.back = Turn(rest.pop(0), rest.pop(0), rest.pop(0), rest.pop(0))
 
     px, py = lax.axis_index("px"), lax.axis_index("py")
-    greet(px, py)
     loads = []
     for g in range(4):
         here = pl.ds(g * 4, 4)
@@ -582,6 +602,7 @@
     tables = [pltpu.make_async_copy(a, b, r.table_sem.at[i]) for i, (a, b) in enumerate(pairs)]
     for table in tables:
         table.start()
+    greet(px, py)
 
     slot = request_part(source, tile, centre, r.asked)
     r.slot[...] = slot
@@ -611,9 +632,10 @@
         face(r.oy.at[0], r.fy.at[1], r.face_sem, 2, 3),
         face(r.oy.at[1], r.fy.at[0], r.face_sem, 3, 2),
     ]
-    pl.semaphore_wait(pltpu.get_barrier_semaphore(), DEVICES - 1)
+    pl.semaphore_wait(pltpu.get_barrier_semaphore(), NPX + NPY - 2)
     for copy in halo:
         copy.start()
+    greet_on(r.inside, px, py)
     r.exa.start(0)
     tables[0].wait()
 
@@ -627,11 +649,17 @@
 
     for c in range(3):
         forward_z(c, r.polar, (r.fx, r.fy), r.tz, r.base, r.there.wire, r.force)
+        if c == 0:
+            pl.semaphore_wait(r.inside, NPX - 1)
         r.there.start(c)
     r.exa.arrive(0)
     r.asked[...] = r.exa.got[0].reshape(128, 128)
     for p in range(NPX):
         r.exb.wire[0, p] = r.asked[pl.ds(p, NPY, stride=NPX), :]
+    r.exb.start(0)
+    owners = lax.broadcasted_iota(jnp.int32, (128, 512), 0)
+    r.match[...] = (owners == row_of(source[...])).astype(F32).astype(BF16)
+    r.mine[...] = jnp.where((owners % 8).astype(F32) == r.slot[...], 1.0, 0.0)
     tables[1].wait()
     tables[2].wait()
 
@@ -651,11 +679,11 @@
         return carry
 
     lax.fori_loop(0, 3, step_back, 0)
-    r.exb.start(0)
     tables[5].wait()
     r.exb.arrive(0)
     for p in range(NPX):
         r.asked[p * NPY : p * NPY + NPY, :] = r.exb.got[0, p]
+    pick_part(r.asked, weights, r.pick, r.gain)
 
     def faces_back(c):
         sems = r.back_sem.at[c]
@@ -669,10 +697,11 @@
     backs = []
     for c in range(3):
         r.back.arrive(c)
-        inverse_z(c, r.back.got, r.tzi, r.disp, r.grad, r.yface, r.lines)
+        inverse_z(c, r.back.got, r.tzi, r.disp, r.yface, r.lines)
         backs += faces_back(c)
         for copy in backs[4 * c :]:
             copy.start()
+        inverse_z_grad(c, r.tzi, r.grad, r.lines)
 
     for copy in backs:
         copy.wait_recv()
@@ -682,7 +711,7 @@
         )
     store = pltpu.make_async_copy(r.stress, stress_h, r.store_sem.at[0])
     store.start()
-    reply_part(r.asked, weights, r.rows, r.reply)
+    reply_part(r.pick, r.gain, r.rows, r.reply)
     for p in range(NPX):
         r.exc.wire[0, p] = r.reply[p * NPY : p * NPY + NPY, :]
     r.exc.start(0)
@@ -700,7 +729,7 @@
     r.exd.start(0)
     store.wait()
     r.exd.arrive(0)
-    force_part(r.exd.got[0].reshape(128, 128), source, r.slot, burgers, line, seg_force)
+    force_part(r.exd.got[0].reshape(128, 128), r.match, r.mine, burgers, line, seg_force)
     r.exc.finish(0)
     r.exd.finish(0)
 

time: 90.5 us -> 87.2 us (0.964)
  Pallas kernels: 85.1 us -> 81.8 us
    pallas_call x1, Pallas kernels: 85.1 us -> 81.8 us  [shards(): pl.pallas_call(whole_body, out_shape=(sds((6, NX, NY, GRID)), sds((3, 512...]
where the time goes in v5:
time: 87.2 us; the launch traced here: 87.1 us
  Pallas kernels  81.8 us (94%)
  local copies, waits for them, and re-layouts  4.58 us (5%)
    pallas_call x1, Pallas kernels, shards(): pl.pallas_call(whole_body, out_shape=(sds((6, NX, NY, GRID)), sds((3, 512...  81.8 us
    unnamed x4, local copies, waits for them, and re-layouts  4.58 us

profile of v5, /device:TPU:1, one launch (start us, length us, event | category | flops | bytes accessed | tf_op | source)
XLA Modules:
  0.0 87.1 jit_solution(9712990092643052908)
XLA Ops:
  0.6 81.8 %shard_map.185 = (f32[6,16,32,256]{3,2,1,0:T(8,128)}, f32[3,512]{1,0:T(4,128)}) custom-call(f32[2,64]{1,0:T(2,128)} %refs_0_.1, s32[1,512]{1,0:T(1,128)} %bitcast.3, s32[1,512]{1,0:T(1,128)} %bitcast.4, s32[1,512]{1,0:T(1,128)} %bitcast.5, f32[3,512]{1,0:T(4,128)} %refs_4_.1, f32[3,512]{1,0:T(4,128)} %refs_5_.1, f32[2,128,128]{2,1,0:T(8,128)} %constant.20.clone.refs_6_, ...), custom_call_target="tpu_custom_call" | custom-call | tf_op jit(solution)/shard_map/pallas_call | solution.py:754
  82.5 0.0 copy-start
  82.5 4.0 %copy.22 = f32[6,16,32,256]{3,2,1,0:T(8,128)} copy(f32[6,16,32,256]{3,2,1,0:T(8,128)} %get-tuple-element.4) | data formatting | bytes 6291456
  86.5 0.0 copy-done
  86.5 0.6 copy.23
Async XLA Ops:
  82.5 4.0 %copy-start = (f32[3,512]{1,0:T(4,128)S(1)}, f32[3,512]{1,0:T(4,128)}, u32[]{:S(2)}) copy-start(f32[3,512]{1,0:T(4,128)} %get-tuple-element.5) | copy-start | bytes 18436

commit v6 on v5

--- a/solution.py
+++ b/solution.py
@@ -431,28 +431,32 @@
         grad[c, x] = out[x * NY : (x + 1) * NY, :]
 
 
-def stress_part(first, count, disp, grad, hx, hy, polar, moduli, stress, rows):
+def stress_part(first, count, late, disp, grad, hx, hy, polar, moduli, stress, rows):
     def at_x(x, carry):
-        lame, shear = moduli[0, x], moduli[1, x]
-        gx, gy, gz = [], [], []
-        for c in range(3):
+        shear = moduli[1, x]
+        row = pl.ds(pl.multiple_of(x * NY, NY), NY)
+
+        def grad_x(c):
             after = hx[1, c] if first == NX - 1 else disp[c, x + 1]
             before = hx[0, c] if first == 0 else disp[c, x - 1]
-            gx.append(after - before)
-            gy.append(shift_y(disp[c, x], hy[0, c, pl.ds(x, 1), :], hy[1, c, pl.ds(x, 1), :]))
-            gz.append(grad[c, x])
-        trace = (0.5 * lame) * (gx[0] + gy[1] + gz[2])
+            return after - before
+
+        def grad_y(c):
+            return shift_y(disp[c, x], hy[0, c, pl.ds(x, 1), :], hy[1, c, pl.ds(x, 1), :])
+
         half = 0.5 * shear
-        parts = (
-            shear * gx[0] + trace,
-            shear * gy[1] + trace,
-            shear * gz[2] + trace,
-            half * (gz[1] + gy[2]),
-            half * (gz[0] + gx[2]),
-            half * (gy[0] + gx[1]),
-        )
-        row = pl.ds(pl.multiple_of(x * NY, NY), NY)
-        for c, part in enumerate(parts):
+        if late:
+            parts = {3: half * (grad[1, x] + grad_y(2)), 4: half * (grad[0, x] + grad_x(2))}
+        else:
+            exx, eyy, ezz = grad_x(0), grad_y(1), grad[2, x]
+            trace = (0.5 * moduli[0, x]) * (exx + eyy + ezz)
+            parts = {
+                0: shear * exx + trace,
+                1: shear * eyy + trace,
+                2: shear * ezz + trace,
+                5: half * (grad_y(0) + grad_x(1)),
+            }
+        for c, part in parts.items():
             total = part + polar[c, x]
             stress[c, x] = total
             hi, lo = split(total)
@@ -478,17 +482,16 @@
         gain[here, :] = jnp.where(lane256 // 128 == tile % 2, row, 0.0)
 
 
-def reply_part(pick, gain, rows, reply):
+def reply_part(comps, pick, gain, rows, out):
     lane = lax.broadcasted_iota(jnp.int32, (128, 128), 1)
-    out = jnp.zeros((128, 128), F32)
-    for c in range(6):
+    for c in comps:
         here = slice(c * 256, c * 256 + 256)
         picked = dot(pick[...], rows[0, :, here]) + dot(pick[...], rows[1, :, here])
         picked = picked * gain[...]
         total = jnp.sum(picked[:, :128] + picked[:, 128:], axis=1, keepdims=True)
         for k in range(8):
             out = jnp.where(lane == c * 8 + k, total[k * 128 : k * 128 + 128], out)
-    reply[...] = out
+    return out
 
 
 def force_part(reply, match, mine, burgers, line, out):
@@ -530,7 +533,7 @@
         "oy": pltpu.VMEM((2, 3, NX, GRID), F32),
         "fx": pltpu.VMEM((2, 3, NY, GRID), F32),
         "fy": pltpu.VMEM((2, 3, NX, GRID), F32),
-        "face_sem": sem((2, 4)),
+        "face_sem": sem((3, 2, 4)),
         "hx": pltpu.VMEM((2, 3, NY, GRID), F32),
         "hy": pltpu.VMEM((2, 3, NX, GRID), F32),
         "yface": pltpu.VMEM((2, 3, NX, GRID), F32),
@@ -626,12 +629,15 @@
     def face(src, dst, sems, to, k):
         return send(src, dst, (sems.at[0, k], sems.at[1, k]), sides[to])
 
-    halo = [
-        face(r.ox.at[0], r.fx.at[1], r.face_sem, 0, 1),
-        face(r.ox.at[1], r.fx.at[0], r.face_sem, 1, 0),
-        face(r.oy.at[0], r.fy.at[1], r.face_sem, 2, 3),
-        face(r.oy.at[1], r.fy.at[0], r.face_sem, 3, 2),
-    ]
+    halo = []
+    for c in range(3):
+        sems = r.face_sem.at[c]
+        halo += [
+            face(r.ox.at[0, c], r.fx.at[1, c], sems, 0, 1),
+            face(r.ox.at[1, c], r.fx.at[0, c], sems, 1, 0),
+            face(r.oy.at[0, c], r.fy.at[1, c], sems, 2, 3),
+            face(r.oy.at[1, c], r.fy.at[0, c], sems, 3, 2),
+        ]
     pl.semaphore_wait(pltpu.get_barrier_semaphore(), NPX + NPY - 2)
     for copy in halo:
         copy.start()
@@ -644,10 +650,9 @@
         return carry
 
     lax.fori_loop(0, 3, local, 0)
-    for copy in halo:
-        copy.wait_recv()
-
     for c in range(3):
+        for copy in halo[4 * c : 4 * c + 4]:
+            copy.wait_recv()
         forward_z(c, r.polar, (r.fx, r.fy), r.tz, r.base, r.there.wire, r.force)
         if c == 0:
             pl.semaphore_wait(r.inside, NPX - 1)
@@ -703,15 +708,22 @@
             copy.start()
         inverse_z_grad(c, r.tzi, r.grad, r.lines)
 
-    for copy in backs:
+    def stress(late):
+        for first, count in ((0, 1), (1, NX - 2), (NX - 1, 1)):
+            stress_part(
+                first, count, late, r.disp, r.grad, r.hx, r.hy, r.polar, r.moduli, r.stress, r.rows
+            )
+
+    for copy in backs[:8]:
         copy.wait_recv()
-    for first, count in ((0, 1), (1, 14), (15, 1)):
-        stress_part(
-            first, count, r.disp, r.grad, r.hx, r.hy, r.polar, r.moduli, r.stress, r.rows
-        )
+    stress(False)
+    reply = reply_part((0, 1, 2, 5), r.pick, r.gain, r.rows, jnp.zeros((128, 128), F32))
+    for copy in backs[8:]:
+        copy.wait_recv()
+    stress(True)
     store = pltpu.make_async_copy(r.stress, stress_h, r.store_sem.at[0])
     store.start()
-    reply_part(r.pick, r.gain, r.rows, r.reply)
+    r.reply[...] = reply_part((3, 4), r.pick, r.gain, r.rows, reply)
     for p in range(NPX):
         r.exc.wire[0, p] = r.reply[p * NPY : p * NPY + NPY, :]
     r.exc.start(0)
@@ -734,6 +746,26 @@
     r.exd.finish(0)
 
 
+def finish_body(stress_in, force_in, stress_out, force_out, buffer, sems):
+    count = 8
+    width = NX // count
+    spans = [pl.ds(i * width, width) for i in range(count)]
+    loads = [
+        pltpu.make_async_copy(stress_in.at[:, s], buffer.at[:, s], sems.at[0, i]) for i, s in enumerate(spans)
+    ]
+    stores = [
+        pltpu.make_async_copy(buffer.at[:, s], stress_out.at[:, s], sems.at[1, i]) for i, s in enumerate(spans)
+    ]
+    for load in loads:
+        load.start()
+    force_out[...] = force_in[...]
+    for load, store in zip(loads, stores):
+        load.wait()
+        store.start()
+    for store in stores:
+        store.wait()
+
+
 def shards(dist, ids, moduli, seg_source, seg_tile, seg_center, burgers, line_vector):
     fwd_z, inv_z = z_tables()
     fwd_h, inv_h = half_tables()
@@ -750,7 +782,7 @@
         scratch += exchange_scratch(axis, parts, block, dtype)
     scratch += turn_scratch() + turn_scratch()
     hbm = pl.BlockSpec(memory_space=pl.ANY)
-    return tuple(
+    stress, seg_force = (
         pl.pallas_call(
             whole_body,
             out_shape=(sds((6, NX, NY, GRID)), sds((3, 512))),
@@ -781,6 +813,19 @@
             tzi,
         )
     )
+    return tuple(
+        pl.pallas_call(
+            finish_body,
+            out_shape=(sds((6, NX, NY, GRID)), sds((3, 512))),
+            in_specs=[hbm, VM],
+            out_specs=(hbm, VM),
+            scratch_shapes=[
+                pltpu.VMEM((6, NX, NY, GRID), F32),
+                pltpu.SemaphoreType.DMA((2, 8)),
+            ],
+            compiler_params=pltpu.CompilerParams(vmem_limit_bytes=VMEM_LIMIT),
+        )(stress, seg_force)
+    )
 
 
 def solution(mesh):

time: 87.2 us -> 82.8 us (0.950)
  local copies, waits for them, and re-layouts: 4.58 us -> 0 us
    unnamed x4 -> x0, local copies, waits for them, and re-layouts: 4.58 us -> none
    pallas_call x1, Pallas kernels: 81.8 us -> 77.7 us  [shards(): pl.pallas_call(whole_body, out_shape=(sds((6, NX, NY, GRID)), sds((3, 512...]
    pallas_call x0 -> x1, Pallas kernels: none -> 4.08 us  [shards(): pl.pallas_call(finish_body, out_shape=(sds((6, NX, NY, GRID)), sds((3, 51...]
where the time goes in v6:
time: 82.8 us; the launch traced here: 82.6 us
  Pallas kernels  81.8 us (99%)
    pallas_call x1, Pallas kernels, shards(): pl.pallas_call(whole_body, out_shape=(sds((6, NX, NY, GRID)), sds((3, 512...  77.7 us
    pallas_call x1, Pallas kernels, shards(): pl.pallas_call(finish_body, out_shape=(sds((6, NX, NY, GRID)), sds((3, 51...  4.08 us

profile of v6, /device:TPU:1, one launch (start us, length us, event | category | flops | bytes accessed | tf_op | source)
XLA Modules:
  0.0 82.6 jit_solution(9026317236854752872)
XLA Ops:
  0.6 77.7 %shard_map.185 = (f32[6,16,32,256]{3,2,1,0:T(8,128)}, f32[3,512]{1,0:T(4,128)}) custom-call(f32[2,64]{1,0:T(2,128)} %refs_0_.1, s32[1,512]{1,0:T(1,128)} %bitcast.3, s32[1,512]{1,0:T(1,128)} %bitcast.4, s32[1,512]{1,0:T(1,128)} %bitcast.5, f32[3,512]{1,0:T(4,128)} %refs_4_.1, f32[3,512]{1,0:T(4,128)} %refs_5_.1, f32[2,128,128]{2,1,0:T(8,128)} %constant.20.clone.refs_6_, ...), custom_call_target="tpu_custom_call" | custom-call | tf_op jit(solution)/shard_map/pallas_call | solution.py:786
  78.4 4.1 %shard_map.186 = (f32[6,16,32,256]{3,2,1,0:T(8,128)}, f32[3,512]{1,0:T(4,128)}) custom-call(f32[6,16,32,256]{3,2,1,0:T(8,128)} %get-tuple-element.4.stress_in, f32[3,512]{1,0:T(4,128)} %get-tuple-element.5.force_in), custom_call_target="tpu_custom_call" | custom-call | tf_op jit(solution)/shard_map/pallas_call | solution.py:817

commit v7 on v6

--- a/solution.py
+++ b/solution.py
@@ -134,9 +134,14 @@
     )
 
 
+def hops(mask):
+    return sum((0, 1, 2, 1)[(mask >> shift) % 4] for shift in (1, 3, 5))
+
+
 def peers(px, py):
     me = px * NPY + py
-    return [lax.rem(me + (53 * k) % DEVICES, DEVICES) for k in range(1, DEVICES)]
+    masks = sorted([(53 * k) % DEVICES for k in range(1, DEVICES)], key=lambda mask: -hops(mask))
+    return [jnp.bitwise_xor(me, mask) for mask in masks]
 
 
 def place(device):
@@ -528,7 +533,10 @@
         "txi": half,
         "tyi": half,
         "tzi": pltpu.VMEM((2, 256, 512), BF16),
-        "table_sem": sem((6,)),
+        "table_sem": sem((9,)),
+        "sx": pltpu.VMEM((2, 128, 128), F32),
+        "sz": pltpu.VMEM((128, 128), F32),
+        "weights": pltpu.VMEM((2, 128, 128), BF16),
         "ox": pltpu.VMEM((2, 3, NY, GRID), F32),
         "oy": pltpu.VMEM((2, 3, NX, GRID), F32),
         "fx": pltpu.VMEM((2, 3, NY, GRID), F32),
@@ -575,8 +583,8 @@
     plan, exchanges = scratch_plan()
     n_in, n_out = 18, 2
     (
-        moduli_in, source, tile, centre, burgers, line, sx, sy, sz, weights,
-        dist_h, ids_h, tz_h, ty_h, tx_h, txi_h, tyi_h, tzi_h,
+        moduli_in, source, tile, centre, burgers, line, sy,
+        sx_h, sz_h, weights_h, dist_h, ids_h, tz_h, ty_h, tx_h, txi_h, tyi_h, tzi_h,
     ) = refs[:n_in]
     stress_h, seg_force = refs[n_in : n_in + n_out]
     rest = list(refs[n_in + n_out :])
@@ -601,10 +609,12 @@
         )
         for load in loads[-1]:
             load.start()
-    pairs = ((tz_h, r.tz), (ty_h, r.ty), (tx_h, r.tx), (txi_h, r.txi), (tyi_h, r.tyi), (tzi_h, r.tzi))
+    pairs = (
+        (tz_h, r.tz), (ty_h, r.ty), (tx_h, r.tx), (txi_h, r.txi), (tyi_h, r.tyi), (tzi_h, r.tzi),
+        (sx_h, r.sx), (sz_h, r.sz), (weights_h, r.weights),
+    )
     tables = [pltpu.make_async_copy(a, b, r.table_sem.at[i]) for i, (a, b) in enumerate(pairs)]
-    for table in tables:
-        table.start()
+    tables[0].start()
     greet(px, py)
 
     slot = request_part(source, tile, centre, r.asked)
@@ -642,6 +652,8 @@
     for copy in halo:
         copy.start()
     greet_on(r.inside, px, py)
+    for table in tables[1:]:
+        table.start()
     r.exa.start(0)
     tables[0].wait()
 
@@ -674,7 +686,9 @@
         return carry
 
     lax.fori_loop(0, 3, step_plane, 0)
-    solve(r.waves, r.solved, sx, sy, sz, px * NPY + py)
+    for table in tables[6:]:
+        table.wait()
+    solve(r.waves, r.solved, r.sx, sy, r.sz, px * NPY + py)
     tables[3].wait()
     tables[4].wait()
 
@@ -688,7 +702,7 @@
     r.exb.arrive(0)
     for p in range(NPX):
         r.asked[p * NPY : p * NPY + NPY, :] = r.exb.got[0, p]
-    pick_part(r.asked, weights, r.pick, r.gain)
+    pick_part(r.asked, r.weights, r.pick, r.gain)
 
     def faces_back(c):
         sems = r.back_sem.at[c]
@@ -786,7 +800,7 @@
         pl.pallas_call(
             whole_body,
             out_shape=(sds((6, NX, NY, GRID)), sds((3, 512))),
-            in_specs=[VM] * 10 + [hbm] * 8,
+            in_specs=[VM] * 7 + [hbm] * 11,
             out_specs=(hbm, VM),
             scratch_shapes=scratch,
             compiler_params=pltpu.CompilerParams(
@@ -799,8 +813,8 @@
             seg_center.reshape(1, 512),
             burgers,
             line_vector,
+            sy,
             sx,
-            sy,
             sz,
             weights,
             dist,

time: 82.8 us -> 81.4 us (0.983)
  Pallas kernels: 81.8 us -> 80.5 us
    pallas_call x1, Pallas kernels: 77.7 us -> 76.5 us  [shards(): pl.pallas_call(whole_body, out_shape=(sds((6, NX, NY, GRID)), sds((3, 512...]
where the time goes in v7:
time: 81.4 us; the launch traced here: 81.2 us
  Pallas kernels  80.5 us (99%)
    pallas_call x1, Pallas kernels, shards(): pl.pallas_call(whole_body, out_shape=(sds((6, NX, NY, GRID)), sds((3, 512...  76.5 us
    pallas_call x1, Pallas kernels, shards(): pl.pallas_call(finish_body, out_shape=(sds((6, NX, NY, GRID)), sds((3, 51...  4.08 us

profile of v7, /device:TPU:1, one launch (start us, length us, event | category | flops | bytes accessed | tf_op | source)
XLA Modules:
  0.0 81.2 jit_solution(10812583222853202045)
XLA Ops:
  0.6 76.5 %shard_map.185 = (f32[6,16,32,256]{3,2,1,0:T(8,128)}, f32[3,512]{1,0:T(4,128)}) custom-call(f32[2,64]{1,0:T(2,128)} %refs_0_.1, s32[1,512]{1,0:T(1,128)} %bitcast.3, s32[1,512]{1,0:T(1,128)} %bitcast.4, s32[1,512]{1,0:T(1,128)} %bitcast.5, f32[3,512]{1,0:T(4,128)} %refs_4_.1, f32[3,512]{1,0:T(4,128)} %refs_5_.1, f32[1,256]{1,0:T(1,128)} %constant.20.clone.refs_6_, ...), custom_call_target="tpu_custom_call" | custom-call | tf_op jit(solution)/shard_map/pallas_call | solution.py:800
  77.1 4.1 %shard_map.186 = (f32[6,16,32,256]{3,2,1,0:T(8,128)}, f32[3,512]{1,0:T(4,128)}) custom-call(f32[6,16,32,256]{3,2,1,0:T(8,128)} %get-tuple-element.4.stress_in, f32[3,512]{1,0:T(4,128)} %get-tuple-element.5.force_in), custom_call_target="tpu_custom_call" | custom-call | tf_op jit(solution)/shard_map/pallas_call | solution.py:831

commit v8 on v7

--- a/solution.py
+++ b/solution.py
@@ -220,8 +220,9 @@
         )
 
     def start(self, part):
-        for d in range(1, self.count):
-            peer = lax.rem(self.me + d, self.count)
+        shift = NPY if self.axis == "px" else 1
+        for mask in sorted(range(1, self.count), key=lambda mask: -hops(mask * shift)):
+            peer = jnp.bitwise_xor(self.me, mask)
             where = (peer, self.py) if self.axis == "px" else (self.px, peer)
             sems = (self.sems.at[0, part], self.sems.at[1, part])
             send(self.wire.at[part, peer], self.got.at[part, self.me], sems, where).start()

time: 81.4 us -> 80.6 us (level)
  no operation moved by 1% of the time
where the time goes in v8:
time: 80.6 us; the launch traced here: 80.4 us
  Pallas kernels  79.8 us (99%)
    pallas_call x1, Pallas kernels, shards(): pl.pallas_call(whole_body, out_shape=(sds((6, NX, NY, GRID)), sds((3, 512...  75.7 us
    pallas_call x1, Pallas kernels, shards(): pl.pallas_call(finish_body, out_shape=(sds((6, NX, NY, GRID)), sds((3, 51...  4.08 us

profile of v8, /device:TPU:1, one launch (start us, length us, event | category | flops | bytes accessed | tf_op | source)
XLA Modules:
  0.0 80.4 jit_solution(15101278202867352702)
XLA Ops:
  0.6 75.7 %shard_map.185 = (f32[6,16,32,256]{3,2,1,0:T(8,128)}, f32[3,512]{1,0:T(4,128)}) custom-call(f32[2,64]{1,0:T(2,128)} %refs_0_.1, s32[1,512]{1,0:T(1,128)} %bitcast.3, s32[1,512]{1,0:T(1,128)} %bitcast.4, s32[1,512]{1,0:T(1,128)} %bitcast.5, f32[3,512]{1,0:T(4,128)} %refs_4_.1, f32[3,512]{1,0:T(4,128)} %refs_5_.1, f32[1,256]{1,0:T(1,128)} %constant.20.clone.refs_6_, ...), custom_call_target="tpu_custom_call" | custom-call | tf_op jit(solution)/shard_map/pallas_call | solution.py:801
  76.3 4.1 %shard_map.186 = (f32[6,16,32,256]{3,2,1,0:T(8,128)}, f32[3,512]{1,0:T(4,128)}) custom-call(f32[6,16,32,256]{3,2,1,0:T(8,128)} %get-tuple-element.4.stress_in, f32[3,512]{1,0:T(4,128)} %get-tuple-element.5.force_in), custom_call_target="tpu_custom_call" | custom-call | tf_op jit(solution)/shard_map/pallas_call | solution.py:832
